TPU v7x, 32 devices: a whole 2x2x4 slice. The times are simulated.
32 devices in a mesh: dp: 4 (over z), expert: 8 (over y, x, core).
Axes of the slice: x: 2, y: 2, z: 4, core: 2. Of those that a mesh axis runs over, the one named last changes fastest.
Arguments:
- cotangent: bfloat16 [4096, 1440], P(('dp', 'expert')), may hold values from -0.0625 to 0.0625
- gates: bfloat16 [4096, 4], P(('dp', 'expert')), may hold values from 0.049804688 to 0.59765625
- routes: int32 [4096, 4], P(('dp', 'expert')), may hold values from 0 to 7, as said below
- slots: int32 [4096, 4], P(('dp', 'expert')), may hold values from 0 to 127, as said below
- saved_hidden: bfloat16 [4, 8, 8, 128, 1440], P('dp', 'expert'), may hold values from -6 to 6
- left_wide: bfloat16 [8, 960, 960], P('expert', None, 'dp')
- left_narrow: bfloat16 [8, 480, 480], P('expert', None, 'dp')
- right_wide: bfloat16 [8, 960, 960], P('expert', None, 'dp')
- right_narrow: bfloat16 [8, 480, 480], P('expert', None, 'dp')
Outputs:
- precond_wide: float32 [8, 1440, 960], P('expert', None, 'dp')
- precond_narrow: float32 [8, 1440, 480], P('expert', None, 'dp')
Inputs may be any that keep to these rules, and one draw needn't show every extreme that they name: Each row names 4 different experts. On each device the experts fall into groups of four and a token's routes name one whole group; no expert is named more than 128 times by the tokens of one device, and one expert is named exactly 128 times by the tokens of every device. slots[t, k] is the row of route k of token t in the buffer of 128 rows that its device fills for that expert; the routes of one device to one expert have different slots.
All inputs are finite; a program needn't handle non-finite values.
Results may differ from a plain program's by a relative error of at most 0.024.
Values may be sent and summed in bfloat16 or wider, within the bound.
No kernel may reach another device: no remote copies, remote signals or barrier semaphores. Data moves between devices by JAX's collectives and lax.ppermute only.
A program may use at most 64 MiB of HBM per device.

v0:
```python
import jax
import jax.numpy as jnp
from jax import lax
from jax.sharding import PartitionSpec as P


def matmul_half(left_side, right_side):
    return jnp.dot(left_side, right_side, preferred_element_type=jnp.float32)


def body(
    cotangent, gates, routes, slots, saved_hidden, left_wide, left_narrow, right_wide, right_narrow
):
    model_width = cotangent.shape[1]
    expert_count = lax.axis_size("expert")
    capacity = saved_hidden.shape[3]
    ff_width = saved_hidden.shape[4]
    block_size = left_wide.shape[1]
    scaled_rows = (
        gates.astype(jnp.float32)[:, :, None] * cotangent.astype(jnp.float32)[:, None, :]
    ).astype(jnp.bfloat16)
    target = (routes * capacity + slots).reshape(-1)
    outbound = (
        jnp.zeros((expert_count * capacity, model_width), jnp.bfloat16)
        .at[target]
        .set(scaled_rows.reshape(-1, model_width))
    )
    inbound = lax.all_to_all(
        outbound.reshape(expert_count, capacity, model_width),
        "expert",
        split_axis=0,
        concat_axis=0,
        tiled=True,
    )
    arrived = inbound.reshape(-1, model_width)
    activations = saved_hidden.reshape(-1, ff_width)
    contract = (((0,), (0,)), ((), ()))
    partial_value = lax.dot_general(
        activations, arrived, contract, preferred_element_type=jnp.float32
    )
    gradient = lax.psum(partial_value.astype(jnp.bfloat16), "dp")
    column_wide = matmul_half(gradient[:, :block_size], right_wide[0]).astype(jnp.bfloat16)
    column_narrow = matmul_half(gradient[:, block_size:], right_narrow[0]).astype(jnp.bfloat16)
    columns = jnp.concatenate([column_wide, column_narrow], axis=1)
    offset = jnp.int32(0)
    piece_wide = lax.all_gather(left_wide, "dp", axis=2, tiled=True)
    piece_narrow = lax.all_gather(left_narrow, "dp", axis=2, tiled=True)
    rows_upper = lax.dynamic_slice_in_dim(columns, offset, piece_wide.shape[2], 0)
    rows_lower = lax.dynamic_slice_in_dim(columns, block_size, piece_narrow.shape[2], 0)
    upper_rows = matmul_half(piece_wide[0], rows_upper)
    lower_rows = matmul_half(piece_narrow[0], rows_lower)
    upper_rows, lower_rows = (upper_rows, lower_rows)
    stacked = jnp.concatenate([upper_rows, lower_rows], axis=0)
    split_at = right_wide.shape[2]
    return (stacked[None, :, :split_at], stacked[None, :, split_at:])


def solution(mesh):
    return jax.shard_map(
        body,
        mesh=mesh,
        in_specs=(
            P(("dp", "expert"), None),
            P(("dp", "expert"), None),
            P(("dp", "expert"), None),
            P(("dp", "expert"), None),
            P("dp", "expert", None, None, None),
            P("expert", None, "dp"),
            P("expert", None, "dp"),
            P("expert", None, "dp"),
            P("expert", None, "dp"),
        ),
        out_specs=(P("expert", None, "dp"), P("expert", None, "dp")),
        check_vma=False,
    )
```

profile of v0, /device:TPU:0, one launch (start us, length us, event | category | flops | bytes accessed | tf_op | source)
XLA Modules:
  0.0 310.1 jit_solution(4158915168748914753)
XLA Ops:
  7.2 0.0 copy-start
  7.2 1.2 copy.42
  8.4 2.2 mul.31
  10.6 0.0 copy-start.3
  10.6 0.0 copy-start.4
  10.6 0.0 copy-start.5
  10.6 4.9 %mul.32 = f32[512,1440]{1,0:T(8,128)} reshape(f32[128,4,1440]{2,1,0:T(4,128)} %mul.31) | data formatting | bytes 5898240 | tf_op jit(solution)/shard_map/mul | solution.py:20
  15.5 0.0 copy-done.3
  15.5 0.0 copy-done.4
  15.6 0.1 copy.40
  15.7 0.1 reshape.51
  15.8 0.0 copy-done.5
  15.8 0.1 copy.41
  15.9 0.1 reshape.55
  16.0 6.5 %scatter_custom_fusion = bf16[1024,1440]{1,0:T(8,128)(2,1)} fusion(s32[512]{0:T(512)S(1)} %bitcast.42, f32[512,1440]{1,0:T(8,128)} %mul.32, f32[512]{0:T(512)S(1)} %reshape.55, bf16[]{:T(256)} %constant.0.clone.1), kind=kCustom, calls=%fused_computation.16 | custom fusion | flops 1474560 | bytes 5900290 | tf_op jit(solution)/shard_map/scatter | solution.py:26
  22.6 4.6 %copy.44 = bf16[8,128,1440]{1,2,0:T(8,128)(2,1)} copy(bf16[8,128,1440]{2,1,0:T(8,128)(2,1)} %bitcast.40) | data formatting | bytes 5898240 | tf_op jit(solution)/shard_map/reshape | solution.py:29
  27.2 0.0 copy-start.1
  27.2 5.4 %all-to-all-start = ((bf16[8,128,1440]{1,2,0:T(8,128)(2,1)}), bf16[8,128,1440]{1,2,0:T(8,128)(2,1)}, u32[]{:S(2)}, u32[]{:S(2)}) async-start(bf16[8,128,1440]{1,2,0:T(8,128)(2,1)} %copy.44), calls=%async_computation | async-start | bytes 5898240 | tf_op jit(solution)/shard_map/all_to_all | solution.py:28
  32.6 0.0 all-gather.2.cloned.1.call-start
  32.7 3.5 %copy.47 = bf16[1,960,240]{1,0,2:T(2,128)(2,1)} copy(bf16[1,960,240]{2,1,0:T(8,128)(2,1)} %param.14) | data formatting | bytes 921600 | tf_op args[5]
  36.2 0.0 all-gather.2.cloned.1.call-update
  36.2 0.2 all-reduce.2.cloned.1.call-start
  36.4 0.0 copy-done.1
  36.5 8.0 %copy.46 = bf16[1,1,8,128,1440]{3,2,4,1,0:T(8,128)(2,1)} copy(bf16[1,1,8,128,1440]{3,4,2,1,0:T(8,128)(2,1)S(1)} %copy-done.1) | data formatting | bytes 5898240 | tf_op args[4]
  44.5 24.0 %all-to-all-done = bf16[8,128,1440]{1,2,0:T(8,128)(2,1)} async-done(((bf16[8,128,1440]{1,2,0:T(8,128)(2,1)}), bf16[8,128,1440]{1,2,0:T(8,128)(2,1)}, u32[]{:S(2)}, u32[]{:S(2)}) %all-to-all-start) | async-done | bytes 2949152 | tf_op jit(solution)/shard_map/all_to_all | solution.py:28
  68.5 9.6 %fusion = bf16[1440,1440]{0,1:T(8,128)(2,1)} fusion(bf16[180,8,8,128]{3,2,1,0:T(8,128)(2,1)} %bitcast.41, bf16[8,128,1440]{1,2,0:T(8,128)(2,1)} %all-to-all-done), kind=kOutput, calls=%fused_computation.2 | convolution fusion | flops 4248806400 | bytes 10045440 | tf_op jit(solution)/shard_map/dot_general | solution.py:38
  78.1 0.0 copy-start.2
  78.1 0.0 all-reduce.2.cloned.1.call-update
  78.1 0.9 copy-done.2
  79.0 0.2 copy.49
  79.2 36.4 %all_gather.7 = bf16[1,480,480]{1,0,2:T(2,128)(2,1)S(1)} all-gather(bf16[1,480,120]{1,0,2:T(2,128)(2,1)S(1)} %copy.49), channel_id=1, replica_groups=mesh['dp'=4,'expert'=8] {'dp'}, dimensions={2}, use_global_device_ids=true | all-gather | bytes 576000 | tf_op jit(solution)/shard_map/all_gather | solution.py:47
  115.6 1.4 copy.50
  117.0 13.8 %all-gather.2.cloned.1.call-done = bf16[1,960,960]{1,0,2:T(2,128)(2,1)} async-done(((bf16[1,960,240]{1,0,2:T(2,128)(2,1)}), bf16[1,960,960]{1,0,2:T(2,128)(2,1)}) %all-gather.2.cloned.1.call-update) | async-done | bytes 1843216 | tf_op jit(solution)/shard_map/all_gather | solution.py:46
  130.8 9.3 %copy.48 = bf16[1,960,960]{2,1,0:T(8,128)(2,1)S(1)} copy(bf16[1,960,960]{1,0,2:T(2,128)(2,1)} %all-gather.2.cloned.1.call-done) | data formatting | bytes 3686400 | tf_op jit(solution)/shard_map/all_gather | solution.py:46
  140.1 0.0 copy-start.6
  140.1 154.0 %all-reduce.2.cloned.1.call-done = bf16[1440,1440]{0,1:T(8,128)(2,1)} async-done(((bf16[1440,1440]{0,1:T(8,128)(2,1)}), bf16[1440,1440]{0,1:T(8,128)(2,1)}) %all-reduce.2.cloned.1.call-update) | async-done | bytes 4147216 | tf_op jit(solution)/shard_map/psum | solution.py:41
  294.1 0.0 copy-done
  294.1 2.8 fusion.7
  296.9 0.0 copy-done.6
  297.0 1.8 convolution_convert_fusion.1
  298.7 0.4 convolution_bitcast_fusion
  299.1 1.0 fusion.18
  300.1 0.2 fusion.23
  300.3 0.2 fusion.16
  300.5 1.1 copy.52
  301.7 1.6 copy.51
  (2 shorter events, 0.0 us)
Async XLA Ops:
  7.2 287.0 %copy-start = (bf16[1,960,240]{2,1,0:T(8,128)(2,1)S(1)}, bf16[1,960,240]{2,1,0:T(8,128)(2,1)}, u32[]{:S(2)}) copy-start(bf16[1,960,240]{2,1,0:T(8,128)(2,1)} %param.16) | copy-start | bytes 1382404
  10.6 4.9 %copy-start.3 = (s32[128,4]{0,1:T(4,128)S(1)}, s32[128,4]{0,1:T(4,128)}, u32[]{:S(2)}) copy-start(s32[128,4]{0,1:T(4,128)} %param.12) | copy-start | bytes 6148
  10.6 4.9 %copy-start.4 = (s32[128,4]{0,1:T(4,128)S(1)}, s32[128,4]{0,1:T(4,128)}, u32[]{:S(2)}) copy-start(s32[128,4]{0,1:T(4,128)} %param.11) | copy-start | bytes 6148
  10.6 5.2 %copy-start.5 = (bf16[128,4]{0,1:T(4,128)(2,1)S(1)}, bf16[128,4]{0,1:T(4,128)(2,1)}, u32[]{:S(2)}) copy-start(bf16[128,4]{0,1:T(4,128)(2,1)} %param.10) | copy-start | bytes 3076
  27.2 9.3 %copy-start.1 = (bf16[1,1,8,128,1440]{3,4,2,1,0:T(8,128)(2,1)S(1)}, bf16[1,1,8,128,1440]{3,4,2,1,0:T(8,128)(2,1)}, u32[]{:S(2)}) copy-start(bf16[1,1,8,128,1440]{3,4,2,1,0:T(8,128)(2,1)} %param.13) | copy-start | bytes 8847364
  27.2 41.3 %all-to-all-start = ((bf16[8,128,1440]{1,2,0:T(8,128)(2,1)}), bf16[8,128,1440]{1,2,0:T(8,128)(2,1)}, u32[]{:S(2)}, u32[]{:S(2)}) async-start(bf16[8,128,1440]{1,2,0:T(8,128)(2,1)} %copy.44), calls=%async_computation | async-start | bytes 5898240 | tf_op jit(solution)/shard_map/all_to_all | solution.py:28
  32.6 98.2 %all-gather.2.cloned.1.call-start = ((), (), s32[]{:S(2)}) async-start(), calls=%async_computation.2 | async-start | bytes 4915200 | tf_op jit(solution)/shard_map/all_gather | solution.py:46
  36.2 257.9 %all-reduce.2.cloned.1.call-start = ((), (), s32[]{:S(2)}) async-start(), calls=%async_computation.1 | async-start | bytes 8847360 | tf_op jit(solution)/shard_map/psum | solution.py:41
  78.1 0.9 copy-start.2
  140.1 156.9 %copy-start.6 = (bf16[1,480,120]{2,1,0:T(8,128)(2,1)S(1)}, bf16[1,480,120]{2,1,0:T(8,128)(2,1)}, u32[]{:S(2)}) copy-start(bf16[1,480,120]{2,1,0:T(8,128)(2,1)} %param.17) | copy-start | bytes 345604
Sparse Core Ops, SparseCore 0:
  36.3 94.4 all-gather.1
  133.2 160.8 all-reduce.1
where the time goes:
time: 311 us; the launch traced here: 310 us
  waiting for transfers between devices  192 us (62%)
  local copies, waits for them, and re-layouts  39.4 us (13%)
  blocking collectives  36.4 us (12%)
  matrix products  15.6 us (5%)
  between operations  14.2 us (5%)
  other arithmetic  6.96 us (2%)
  starting transfers between devices  5.69 us (2%)
    psum x1, waiting for transfers between devices, body(): gradient = lax.psum(partial_value.astype(jnp.bfloat16), 'dp')  154 us
    all_gather x1, blocking collectives, body(): piece_narrow = lax.all_gather(left_narrow, 'dp', axis=2, tiled=True)  36.4 us
    all_to_all x1, waiting for transfers between devices, body(): lax.all_to_all(outbound.reshape(expert_count, capacity, model_width), 'ex...  24 us
    unnamed x19, local copies, waits for them, and re-layouts  15.3 us
    all_gather x1, waiting for transfers between devices, body(): piece_wide = lax.all_gather(left_wide, 'dp', axis=2, tiled=True)  13.8 us
    dot_general x1, matrix products, body(): lax.dot_general(activations, arrived, contract, preferred_element_type=jn...  9.61 us
    all_gather x1, local copies, waits for them, and re-layouts, body(): piece_wide = lax.all_gather(left_wide, 'dp', axis=2, tiled=True)  9.25 us
    mul x4, local copies, waits for them, and re-layouts, body(): gates.astype(jnp.float32)[:, :, None]  7.37 us
  transfers between devices with their start and end apart: 3, of which 3 were waited for; matrix products, arithmetic and copies ran while one was open for 10% of the time, Pallas kernels for 0%

commit v1 on v0

v1 whole, which is shorter than its diff:
```python
import functools

import jax
import jax.numpy as jnp
from jax import lax
from jax.experimental import pallas as pl
from jax.experimental.pallas import tpu as pltpu
from jax.sharding import PartitionSpec as P

BF16 = jnp.bfloat16
F32 = jnp.float32
LANES = 128
META_ROWS = 16
ROW_CHUNKS = 3
MIB = 1024 * 1024


def round_up(value, unit):
    return (value + unit - 1) // unit * unit


def params(mib):
    return pltpu.CompilerParams(vmem_limit_bytes=mib * MIB)


def cost():
    return pl.CostEstimate(flops=0, bytes_accessed=0, transcendentals=0)


class Order:
    def __init__(self, tick):
        self.tick = tick

    def gate(self, ready, values):
        self.tick, _, values = lax.optimization_barrier((self.tick, ready, values))
        return values


def dot_nn(left, right):
    return lax.dot_general(left, right, (((1,), (0,)), ((), ())), preferred_element_type=F32)


def dot_nt(left, right):
    return lax.dot_general(left, right, (((1,), (1,)), ((), ())), preferred_element_type=F32)


ANY = pl.BlockSpec(memory_space=pl.ANY)
VMEM = pl.BlockSpec(memory_space=pltpu.VMEM)


class Fold:
    def __init__(self, rows_w, rows_n, wide, narrow):
        self.rows_w, self.rows_n, self.wide, self.narrow = rows_w, rows_n, wide, narrow
        self.lanes = round_up(wide, LANES)
        self.step = round_up(narrow, LANES)
        self.ways = max(1, self.lanes // self.step)
        while rows_n % (self.ways * 16):
            self.ways -= 1
        self.part = rows_n // self.ways
        self.rows = rows_w + self.part
        self.shape = (self.rows, self.lanes)

    def write(self, ref, wide_value, narrow_value):
        ref[...] = jnp.zeros(self.shape, ref.dtype)
        ref[0 : self.rows_w, 0 : self.wide] = wide_value
        for way in range(self.ways):
            start = way * self.step
            ref[self.rows_w : self.rows, start : start + self.narrow] = narrow_value[
                way * self.part : (way + 1) * self.part
            ]

    def wide_of(self, value):
        return value[0 : self.rows_w, 0 : self.wide]

    def narrow_of(self, value):
        low = value[self.rows_w : self.rows]
        parts = [low[:, way * self.step : way * self.step + self.narrow] for way in range(self.ways)]
        return parts[0] if self.ways == 1 else jnp.concatenate(parts, axis=0)


def token_kernel(cot_ref, gate_ref, route_ref, slot_ref, tok_ref, gate, route, slot, meta, sem):
    width = cot_ref.shape[0]
    ways = gate_ref.shape[0]
    targets = (tok_ref.at[pl.ds(0, width)], gate, route, slot)
    copies = [
        pltpu.make_async_copy(source, target, sem.at[i])
        for i, (source, target) in enumerate(zip((cot_ref, gate_ref, route_ref, slot_ref), targets))
    ]
    for copy in copies:
        copy.start()
    for copy in copies[1:]:
        copy.wait()
    meta[...] = jnp.zeros(meta.shape, F32)
    meta[0:ways, :] = gate[...].astype(F32)
    meta[ways : 2 * ways, :] = route[...].astype(F32)
    meta[2 * ways : 3 * ways, :] = slot[...].astype(F32)
    tok_ref[width : width + META_ROWS, :] = meta[...].astype(BF16)
    copies[0].wait()


def pack_left_kernel(root, lw_ref, ln_ref, out_ref, wide, narrow, sem):
    copies = [
        pltpu.make_async_copy(lw_ref, wide, sem.at[0]),
        pltpu.make_async_copy(ln_ref, narrow, sem.at[1]),
    ]
    for copy in copies:
        copy.start()
    for copy in copies:
        copy.wait()
    root.write(out_ref, wide[...], narrow[...])


def partial_kernel(topk, width, low, high, hidden_ref, mine_ref, theirs_ref, out_ref, rows_ref):
    sources, _, capacity = hidden_ref.shape
    expert = lax.axis_index("expert")

    @pl.when(pl.program_id(0) == 0)
    def _():
        for offset in range(sources):
            token_ref = (mine_ref, theirs_ref)[offset % 2].at[offset // 2]
            source = jnp.bitwise_xor(expert, offset)
            meta = token_ref[width : width + META_ROWS, :].astype(F32)
            tokens = meta.shape[1]
            place = lax.broadcasted_iota(jnp.int32, (capacity, tokens), 0).astype(F32)
            here = expert.astype(F32)
            weights = jnp.zeros((capacity, tokens), F32)
            for k in range(topk):
                gate = meta[k : k + 1, :]
                route = meta[topk + k : topk + k + 1, :]
                slot = meta[2 * topk + k : 2 * topk + k + 1, :]
                wanted = jnp.where(route == here, slot, -1.0)
                weights = jnp.where(place == wanted, gate, weights)
            rows = pl.ds(pl.multiple_of(source * capacity, capacity), capacity)
            rows_ref[rows, :] = dot_nt(weights.astype(BF16), token_ref[low:high, :]).astype(BF16)

    if capacity % LANES == 0:
        hidden = jnp.concatenate([hidden_ref[s] for s in range(sources)], axis=1)
        out_ref[...] = dot_nn(hidden, rows_ref[...]).astype(BF16)
    else:
        total = dot_nn(hidden_ref[0], rows_ref[0:capacity, :])
        for s in range(1, sources):
            total += dot_nn(hidden_ref[s], rows_ref[s * capacity : (s + 1) * capacity, :])
        out_ref[...] = total.astype(BF16)


def sends(n, t, s):
    z = lax.axis_index("dp")
    up = z % 2 == s
    return jnp.where(up, (z <= t - 1) & (z < n - 1), z >= max(1, n - t))


def product_kernel(n, t, sets, partial_ref, *refs):
    count = len(refs) // 2
    rows = partial_ref.shape[0] // ROW_CHUNKS

    def product(root_ref, out_ref):
        for i in range(ROW_CHUNKS):
            part = slice(i * rows, (i + 1) * rows)
            out_ref[part, :] = dot_nn(partial_ref[part, :], root_ref[...]).astype(BF16)

    for i in range(count):
        make = functools.partial(product, refs[i], refs[count + i])
        if i < len(sets):
            pl.when(sends(n, t, sets[i]))(make)
        else:
            make()


def add_kernel(n, t, s, term_ref, got_ref, out_ref):
    @pl.when(sends(n, t, s))
    def _():
        out_ref[...] = (term_ref[...].astype(F32) + got_ref[...].astype(F32)).astype(BF16)


def left_kernel(root, n, own_ref, ends_ref, rest_ref, odd_ref, *refs):
    got = refs[: 2 * (n - 2)]
    wide_ref, narrow_ref, held, sem = refs[2 * (n - 2) :]
    z = lax.axis_index("dp")
    for here in range(n):
        even_ref = ends_ref if here in (1, n - 2) else rest_ref
        near = (even_ref, odd_ref) + got

        @pl.when(z == here)
        def _():
            copies = [pltpu.make_async_copy(own_ref, held.at[here], sem.at[here])]
            for q in range(n):
                if q != here:
                    s = here % 2 if q > here else 1 - here % 2
                    copies.append(
                        pltpu.make_async_copy(near[2 * (abs(q - here) - 1) + s], held.at[q], sem.at[q])
                    )
            for copy in copies:
                copy.start()
            for copy in copies:
                copy.wait()

    for q in range(n):
        piece = held[q]
        wide_ref[:, q * root.wide : (q + 1) * root.wide] = root.wide_of(piece)
        narrow_ref[:, q * root.narrow : (q + 1) * root.narrow] = root.narrow_of(piece)


def final_kernel(block, count, own_ref, *refs):
    wide_ref, narrow_ref, out_ref = refs[count:]
    rows = own_ref[...].astype(F32)
    for got_ref in refs[:count]:
        rows += got_ref[...].astype(F32)
    rows = rows.astype(BF16)
    out_ref[0:block, :] = dot_nn(wide_ref[...], rows[0:block])
    out_ref[block:, :] = dot_nn(narrow_ref[...], rows[block:])


def collect_kernel(count, *refs):
    sem = refs[-1]
    out_ref = refs[count]
    copies = [pltpu.make_async_copy(refs[i], out_ref.at[i], sem.at[i]) for i in range(count)]
    for copy in copies:
        copy.start()
    for copy in copies:
        copy.wait()


def body(
    cotangent, gates, routes, slots, saved_hidden, left_wide, left_narrow, right_wide, right_narrow
):
    tokens, width = cotangent.shape
    topk = gates.shape[1]
    n = lax.axis_size("dp")
    experts = lax.axis_size("expert")
    _, _, sources, capacity, ffn = saved_hidden.shape
    block, wide = right_wide.shape[1:]
    rest, narrow = right_narrow.shape[1:]
    root = Fold(block, rest, wide, narrow)

    def gather_pairs(k, s):
        up = [(i, i + 1) for i in range(s, n - 1, 2) if i >= k - 1]
        return up + [(i + 1, i) for i in range(s, n - 1, 2) if i <= n - 1 - k]

    def sum_pairs(t, s):
        up = [(i, i + 1) for i in range(s, n - 1, 2) if i <= t - 1]
        return up + [(i + 1, i) for i in range(s, n - 1, 2) if i + 1 >= n - t]

    def hop(k, pieces):
        return [
            lax.ppermute(pieces[1 - s], "dp", gather_pairs(k, s)) if gather_pairs(k, s) else pieces[1 - s]
            for s in (0, 1)
        ]

    tok = pl.pallas_call(
        token_kernel,
        in_specs=[ANY] * 4,
        out_specs=VMEM,
        out_shape=jax.ShapeDtypeStruct((width + META_ROWS, tokens), BF16),
        scratch_shapes=[
            pltpu.VMEM((topk, tokens), BF16),
            pltpu.VMEM((topk, tokens), jnp.int32),
            pltpu.VMEM((topk, tokens), jnp.int32),
            pltpu.VMEM((META_ROWS, tokens), F32),
            pltpu.SemaphoreType.DMA((4,)),
        ],
        compiler_params=params(56),
        cost_estimate=cost(),
        name="tokens",
    )(cotangent.T, gates.T, routes.T, slots.T)
    chips = experts // 2

    def collect(values):
        return pl.pallas_call(
            functools.partial(collect_kernel, chips),
            in_specs=[ANY] * chips,
            out_specs=ANY,
            out_shape=jax.ShapeDtypeStruct((chips,) + tok.shape, BF16),
            scratch_shapes=[pltpu.SemaphoreType.DMA((chips,))],
            compiler_params=params(16),
            cost_estimate=cost(),
            name="collect",
        )(*values)

    def pack_left(wide_piece, narrow_piece):
        return pl.pallas_call(
            functools.partial(pack_left_kernel, root),
            in_specs=[ANY] * 2,
            out_shape=jax.ShapeDtypeStruct(root.shape, BF16),
            scratch_shapes=[
                pltpu.VMEM((block, wide), BF16),
                pltpu.VMEM((rest, narrow), BF16),
                pltpu.SemaphoreType.DMA((2,)),
            ],
            compiler_params=params(16),
            cost_estimate=cost(),
            name="pack_left",
        )(wide_piece, narrow_piece)

    chunk_rows = ffn // ROW_CHUNKS
    hidden = jnp.swapaxes(saved_hidden[0, 0], 1, 2)

    def partial(low, high, mine, theirs):
        return pl.pallas_call(
            functools.partial(partial_kernel, topk, width, low, high),
            grid=(ROW_CHUNKS,),
            in_specs=[pl.BlockSpec((sources, chunk_rows, capacity), lambda i: (0, i, 0)), VMEM, VMEM],
            out_specs=pl.BlockSpec((chunk_rows, high - low), lambda i: (i, 0)),
            out_shape=jax.ShapeDtypeStruct((ffn, high - low), BF16),
            scratch_shapes=[pltpu.VMEM((sources * capacity, high - low), BF16)],
            compiler_params=params(24),
            cost_estimate=cost(),
            name="partial",
        )(hidden, mine, theirs)

    def product(value, t, got):
        sets = [s for s in (0, 1) if sum_pairs(t, s)]
        pieces = [got[n - t][s] for s in sets] + ([got[0][0]] if t == n - 1 else [])
        columns = pieces[0].shape[1]
        made = pl.pallas_call(
            functools.partial(product_kernel, n, t, sets),
            in_specs=[VMEM] * (1 + len(pieces)),
            out_specs=[VMEM] * len(pieces),
            out_shape=[jax.ShapeDtypeStruct((ffn, columns), BF16)] * len(pieces),
            compiler_params=params(16),
            cost_estimate=cost(),
            name="product",
        )(value, *pieces)
        return dict(zip(sets + [2], made))

    def add(t, s, term, got):
        return pl.pallas_call(
            functools.partial(add_kernel, n, t, s),
            in_specs=[VMEM] * 2,
            out_specs=VMEM,
            out_shape=jax.ShapeDtypeStruct(term.shape, BF16),
            compiler_params=params(16),
            cost_estimate=cost(),
            name="add",
        )(term, got)

    def send_sums(t, terms, last):
        sent = {}
        for s in (0, 1):
            if sum_pairs(t, s):
                term = terms[s]
                if 1 - s in last:
                    term = add(t, s, term, last[1 - s])
                sent[s] = lax.ppermute(term, "dp", sum_pairs(t, s))
        return sent

    order = Order(slots)
    mine = [tok] + [None] * (chips - 1)

    def exchange(value, steps):
        for m in steps:
            mine[m] = lax.ppermute(value, "expert", [(i, i ^ (2 * m)) for i in range(experts)])

    straight = [m for m in range(1, chips) if m & (m - 1) == 0]
    exchange(tok, straight)
    near = [[right_narrow[0]] * 2]
    for k in range(1, 3):
        near.append(hop(k, near[-1]))
    near[2], right_far, tok, left_wide, left_narrow = order.gate(
        [mine[m] for m in straight], (near[2], right_wide[0], tok, left_wide, left_narrow)
    )

    exchange(tok, [m for m in range(1, chips) if m not in straight])
    for k in range(3, n):
        near.append(hop(k, near[-1]))
    far = [[right_far] * 2]
    far.append(hop(1, far[0]))
    left = pack_left(left_wide[0], left_narrow[0])
    mine, near, far[1], left = order.gate((), (mine, near, far[1], left))

    mine = collect(mine)
    theirs = lax.ppermute(mine, "expert", [(i, i ^ 1) for i in range(experts)])
    far.append(hop(2, far[1]))
    ends = [pair for pair in gather_pairs(1, 0) if pair in ((0, 1), (n - 1, n - 2))]
    others = [pair for pair in gather_pairs(1, 0) if pair not in ends]
    left_ends = lax.ppermute(left, "dp", ends)
    part_near = partial(block, width, mine, theirs)
    terms_near = {1: product(part_near, 1, near)}
    far, left, left_ends, terms_near, part_near, mine, theirs = order.gate(
        (), (far, left, left_ends, terms_near, part_near, mine, theirs)
    )

    sent_near = send_sums(1, terms_near[1], {})
    for k in range(3, n):
        far.append(hop(k, far[-1]))
    left_odd = lax.ppermute(left, "dp", gather_pairs(1, 1))
    part_far = partial(0, block, mine, theirs)
    for t in range(2, n):
        terms_near[t] = product(part_near, t, near)
    terms_far = {1: product(part_far, 1, far)}
    far, part_far, terms_near, terms_far, sent_near, left, left_odd = order.gate(
        (), (far, part_far, terms_near, terms_far, sent_near, left, left_odd)
    )

    sent_far = send_sums(1, terms_far[1], {})
    sent_near = send_sums(2, terms_near[2], sent_near)
    left_rest = lax.ppermute(left, "dp", others) if others else left
    inner = {target for _, target in ends}
    z = lax.axis_index("dp")
    if all(pair[0] in inner for pair in gather_pairs(2, 1)):
        left_even = left_ends
    else:
        left_even = jnp.where((z == 1) | (z == n - 2), left_ends, left_rest)
    lefts = [[left, left], [left_even, left_odd]]
    lefts.append(hop(2, [left_even, lax.optimization_barrier((left_odd, left_rest))[0]]))
    for t in range(2, n):
        terms_far[t] = product(part_far, t, far)
    sent_far, sent_near, terms_far, left_rest, lefts[2] = order.gate(
        (), (sent_far, sent_near, terms_far, left_rest, lefts[2])
    )

    for t in range(2, n):
        sent_far = send_sums(t, terms_far[t], sent_far)
        if t + 1 < n:
            sent_near = send_sums(t + 1, terms_near[t + 1], sent_near)
            lefts.append(hop(t + 1, lefts[-1]))
            sent_far, sent_near, lefts[-1] = order.gate((), (sent_far, sent_near, lefts[-1]))

    left_inputs = [left, left_ends, left_rest, left_odd] + [value for pair in lefts[2:] for value in pair]
    left_w, left_n = pl.pallas_call(
        functools.partial(left_kernel, root, n),
        in_specs=[ANY] * len(left_inputs),
        out_shape=(
            jax.ShapeDtypeStruct((block, block), BF16),
            jax.ShapeDtypeStruct((rest, rest), BF16),
        ),
        scratch_shapes=[pltpu.VMEM((n,) + root.shape, BF16), pltpu.SemaphoreType.DMA((n,))],
        compiler_params=params(32),
        cost_estimate=cost(),
        name="left",
    )(*left_inputs)

    outs = []
    for terms, last in ((terms_near, sent_near), (terms_far, sent_far)):
        own = terms[n - 1][2]
        got = [last[s] for s in sorted(last)]
        outs.append(
            pl.pallas_call(
                functools.partial(final_kernel, block, len(got)),
                in_specs=[VMEM] * (3 + len(got)),
                out_specs=VMEM,
                out_shape=jax.ShapeDtypeStruct(own.shape, F32),
                compiler_params=params(32),
                cost_estimate=cost(),
                name="final",
            )(own, *got, left_w, left_n)[None]
        )
    return outs[1], outs[0]


def solution(mesh):
    return jax.shard_map(
        body,
        mesh=mesh,
        in_specs=(
            P(("dp", "expert"), None),
            P(("dp", "expert"), None),
            P(("dp", "expert"), None),
            P(("dp", "expert"), None),
            P("dp", "expert", None, None, None),
            P("expert", None, "dp"),
            P("expert", None, "dp"),
            P("expert", None, "dp"),
            P("expert", None, "dp"),
        ),
        out_specs=(P("expert", None, "dp"), P("expert", None, "dp")),
        check_vma=False,
    )
```

time: 311 us -> 147 us (0.47)
  waiting for transfers between devices: 192 us -> 65.8 us
  starting transfers between devices: 5.69 us -> 55.2 us
  local copies, waits for them, and re-layouts: 39.4 us -> 2.27 us
  blocking collectives: 36.4 us -> 0 us
  Pallas kernels: 0 us -> 22.1 us
  matrix products: 15.6 us -> 0 us
  between operations: 14.2 us -> 1.08 us
  other arithmetic: 6.96 us -> 0 us
    psum x1 -> x0, waiting for transfers between devices: 154 us -> none  [body(): gradient = lax.psum(partial_value.astype(jnp.bfloat16), 'dp')]
    ppermute x0 -> x30, waiting for transfers between devices: none -> 65.8 us  [the longest x10 30.5 us: send_sums(): sent[s] = lax.ppermute(term, 'dp', sum_pairs(t, s))]
    ppermute x0 -> x30, starting transfers between devices: none -> 55.2 us  [the longest x10 25.3 us: send_sums(): sent[s] = lax.ppermute(term, 'dp', sum_pairs(t, s))]
    all_gather x1 -> x0, blocking collectives: 36.4 us -> none  [body(): piece_narrow = lax.all_gather(left_narrow, 'dp', axis=2, tiled=True)]
    all_to_all x1 -> x0, waiting for transfers between devices: 24 us -> none  [body(): lax.all_to_all(outbound.reshape(expert_count, capacity, model_width), 'ex...]
    pallas_call x0 -> x20, Pallas kernels: none -> 22.1 us  [the longest x2 7.56 us: partial(): pl.pallas_call(functools.partial(partial_kernel, topk, width, low, high),...]
    dot_general x5 -> x0, matrix products: 15.6 us -> none  [the longest x1 9.61 us: body(): lax.dot_general(activations, arrived, contract, preferred_element_type=jn...]
    all_gather x1 -> x0, waiting for transfers between devices: 13.8 us -> none  [body(): piece_wide = lax.all_gather(left_wide, 'dp', axis=2, tiled=True)]
  transfers between devices with their start and end apart: 3 -> 30, of which waited for: 3 -> 10; matrix products, arithmetic and copies ran while one was open for 10% -> 0% of each run, Pallas kernels for 0% -> 12%
where the time goes in v1:
time: 147 us
  waiting for transfers between devices  65.8 us (45%)
  starting transfers between devices  55.2 us (38%)
  Pallas kernels  22.1 us (15%)
  local copies, waits for them, and re-layouts  2.27 us (2%)
    ppermute x10, waiting for transfers between devices, send_sums(): sent[s] = lax.ppermute(term, 'dp', sum_pairs(t, s))  30.5 us
    ppermute x13, waiting for transfers between devices, hop(): lax.ppermute(pieces[1 - s], 'dp', gather_pairs(k, s))  26.1 us
    ppermute x10, starting transfers between devices, send_sums(): sent[s] = lax.ppermute(term, 'dp', sum_pairs(t, s))  25.3 us
    ppermute x13, starting transfers between devices, hop(): lax.ppermute(pieces[1 - s], 'dp', gather_pairs(k, s))  19.9 us
    ppermute x1, waiting for transfers between devices, body(): left_rest = lax.ppermute(left, 'dp', others) if others else left  9.15 us
    pallas_call x2, Pallas kernels, partial(): pl.pallas_call(functools.partial(partial_kernel, topk, width, low, high),...  7.56 us
    pallas_call x6, Pallas kernels, product(): pl.pallas_call(functools.partial(product_kernel, n, t, sets), in_specs=[V...  5.98 us
    ppermute x3, starting transfers between devices, exchange(): lax.ppermute(value, 'expert', [(i, i ^ 2 * m) for i in range(experts)])  5.07 us
  transfers between devices with their start and end apart: 30, of which 10 were waited for; matrix products, arithmetic and copies ran while one was open for 0% of the time, Pallas kernels for 12%

profile of v1, /device:TPU:0, one launch (start us, length us, event | category | flops | bytes accessed | tf_op | source)
XLA Modules:
  0.0 146.6 jit_solution(11106479865887672115)
XLA Ops:
  0.6 1.8 %tokens.1.refs_0_ = bf16[1456,128]{1,0:T(8,128)(2,1)} custom-call(bf16[1440,128]{1,0:T(8,128)(2,1)} %bitcast.25, bf16[4,128]{1,0:T(4,128)(2,1)} %bitcast.28, s32[4,128]{1,0:T(4,128)} %bitcast.26, s32[4,128]{1,0:T(4,128)} %bitcast.27), custom_call_target="tpu_custom_call" | custom-call | tf_op jit(solution)/shard_map/tokens/pallas_call | solution.py:249
  2.4 3.0 %collective-permute-start = (bf16[1456,128]{1,0:T(8,128)(2,1)}, bf16[1456,128]{1,0:T(8,128)(2,1)S(1)}, u32[]{:S(2)}, u32[]{:S(2)}) collective-permute-start(bf16[1456,128]{1,0:T(8,128)(2,1)} %tokens.1.refs_0_), channel_id=1, source_target_pairs={{0,2},{1,3},{2,0},{3,1},{4,6},{5,7},{6,4},{7,5},{8,10},{9,11},{10,... | collective-permute-start | bytes 1118216 | tf_op jit(solution)/shard_map/ppermute | solution.py:351
  5.4 1.5 %collective-permute-start.1 = (bf16[1456,128]{1,0:T(8,128)(2,1)}, bf16[1456,128]{1,0:T(8,128)(2,1)S(1)}, u32[]{:S(2)}, u32[]{:S(2)}) collective-permute-start(bf16[1456,128]{1,0:T(8,128)(2,1)} %tokens.1.refs_0_), channel_id=1, source_target_pairs={{0,4},{1,5},{2,6},{3,7},{4,0},{5,1},{6,2},{7,3},{8,12},{9,13},{10,... | collective-permute-start | bytes 1118216 | tf_op jit(solution)/shard_map/ppermute | solution.py:351
  7.6 4.5 %collective-permute-start.4 = (bf16[480,120]{1,0:T(8,128)(2,1)}, bf16[480,120]{1,0:T(8,128)(2,1)S(1)}, u32[]{:S(2)}, u32[]{:S(2)}) collective-permute-start(bf16[480,120]{1,0:T(8,128)(2,1)} %bitcast.20), channel_id=1, source_target_pairs={{0,8},{16,24},{8,0},{24,16},{1,9},{17,25},{9,1},{25,17},{2,10},{18... | collective-permute-start | bytes 345608 | tf_op jit(solution)/shard_map/ppermute | solution.py:245
  12.1 1.3 collective-permute-start.3
  13.4 1.8 %collective-permute-done.4.refs_0_ = bf16[480,120]{1,0:T(8,128)(2,1)S(1)} collective-permute-done((bf16[480,120]{1,0:T(8,128)(2,1)}, bf16[480,120]{1,0:T(8,128)(2,1)S(1)}, u32[]{:S(2)}, u32[]{:S(2)}) %collective-permute-start.4) | collective-permute-done | bytes 115232 | tf_op jit(solution)/shard_map/ppermute | solution.py:245
  15.8 3.8 %collective-permute-done.3.refs_0_ = bf16[480,120]{1,0:T(8,128)(2,1)S(1)} collective-permute-done((bf16[480,120]{1,0:T(8,128)(2,1)S(1)}, bf16[480,120]{1,0:T(8,128)(2,1)S(1)}, u32[]{:S(2)}, u32[]{:S(2)}) %collective-permute-start.3) | collective-permute-done | bytes 115232 | tf_op jit(solution)/shard_map/ppermute | solution.py:245
  19.6 4.3 %collective-permute-start.8 = (bf16[960,240]{1,0:T(8,128)(2,1)}, bf16[960,240]{1,0:T(8,128)(2,1)S(1)}, u32[]{:S(2)}, u32[]{:S(2)}) collective-permute-start(bf16[960,240]{1,0:T(8,128)(2,1)} %bitcast.16), channel_id=1, source_target_pairs={{0,8},{16,24},{8,0},{24,16},{1,9},{17,25},{9,1},{25,17},{2,10},{18... | collective-permute-start | bytes 1382408 | tf_op jit(solution)/shard_map/ppermute | solution.py:245
  23.9 0.7 collective-permute-start.9
  25.2 1.3 collective-permute-start.7
  26.5 1.0 copy-done.2
  27.5 0.9 copy-done.5
  29.0 6.2 %collective-permute-done.7.refs_0_ = bf16[480,120]{1,0:T(8,128)(2,1)S(1)} collective-permute-done((bf16[480,120]{1,0:T(8,128)(2,1)S(1)}, bf16[480,120]{1,0:T(8,128)(2,1)S(1)}, u32[]{:S(2)}, u32[]{:S(2)}) %collective-permute-start.7) | collective-permute-done | bytes 115232 | tf_op jit(solution)/shard_map/ppermute | solution.py:245
  35.2 0.7 collect.1.mine_ref
  35.9 2.9 %collective-permute-start.12 = (bf16[1200,256]{1,0:T(8,128)(2,1)S(1)}, bf16[1200,256]{1,0:T(8,128)(2,1)S(1)}, u32[]{:S(2)}, u32[]{:S(2)}) collective-permute-start(bf16[1200,256]{1,0:T(8,128)(2,1)S(1)} %pack_left.1.own_ref), channel_id=1, source_target_pairs={{0,8},{24,16},{1,9},{25,17},{2,10},{26,18},{3,11},{27,19},{4,12},{... | collective-permute-start | bytes 1843208 | tf_op jit(solution)/shard_map/ppermute | solution.py:375
  38.9 1.3 collective-permute-start.10
  40.2 0.7 collective-permute-start.11
  40.9 2.9 %partial.2.partial_ref = bf16[1440,480]{1,0:T(8,128)(2,1)S(1)} custom-call(bf16[8,1440,128]{2,1,0:T(8,128)(2,1)S(1)} %bitcast.13, bf16[4,1456,128]{2,1,0:T(8,128)(2,1)S(1)} %collect.1.mine_ref, bf16[4,1456,128]{2,1,0:T(8,128)(2,1)S(1)} %collective-permute-done.13.theirs_ref), custom_call_target="tpu_custom_call" | custom-call | tf_op jit(solution)/shard_map/partial/pallas_call | solution.py:298
  44.4 9.7 %collective-permute-done.10.refs_0_ = bf16[960,240]{1,0:T(8,128)(2,1)S(1)} collective-permute-done((bf16[960,240]{1,0:T(8,128)(2,1)S(1)}, bf16[960,240]{1,0:T(8,128)(2,1)S(1)}, u32[]{:S(2)}, u32[]{:S(2)}) %collective-permute-start.10) | collective-permute-done | bytes 460832 | tf_op jit(solution)/shard_map/ppermute | solution.py:245
  54.1 0.7 collective-permute-start.16
  54.8 1.3 collective-permute-start.14
  56.1 8.4 %collective-permute-start.15 = (bf16[1440,120]{1,0:T(8,128)(2,1)S(1)}, bf16[1440,120]{1,0:T(8,128)(2,1)S(1)}, u32[]{:S(2)}, u32[]{:S(2)}) collective-permute-start(bf16[1440,120]{1,0:T(8,128)(2,1)S(1)} %product.6), channel_id=1, source_target_pairs={{0,8},{24,16},{1,9},{25,17},{2,10},{26,18},{3,11},{27,19},{4,12},{... | collective-permute-start | bytes 1036808 | tf_op jit(solution)/shard_map/ppermute | solution.py:343
  64.5 4.7 %partial.3.partial_ref = bf16[1440,960]{1,0:T(8,128)(2,1)S(1)} custom-call(bf16[8,1440,128]{2,1,0:T(8,128)(2,1)S(1)} %bitcast.14, bf16[4,1456,128]{2,1,0:T(8,128)(2,1)S(1)} %collect.1.mine_ref, bf16[4,1456,128]{2,1,0:T(8,128)(2,1)S(1)} %collective-permute-done.13.theirs_ref), custom_call_target="tpu_custom_call" | custom-call | tf_op jit(solution)/shard_map/partial/pallas_call | solution.py:298
  70.0 1.1 product.8
  71.1 1.5 %collective-permute-done.14.refs_0_ = bf16[960,240]{1,0:T(8,128)(2,1)S(1)} collective-permute-done((bf16[960,240]{1,0:T(8,128)(2,1)S(1)}, bf16[960,240]{1,0:T(8,128)(2,1)S(1)}, u32[]{:S(2)}, u32[]{:S(2)}) %collective-permute-start.14) | collective-permute-done | bytes 460832 | tf_op jit(solution)/shard_map/ppermute | solution.py:245
  72.6 0.9 product.9
  73.6 1.3 collective-permute-start.20
  74.9 4.6 %collective-permute-start.17 = (bf16[1440,240]{1,0:T(8,128)(2,1)S(1)}, bf16[1440,240]{1,0:T(8,128)(2,1)S(1)}, u32[]{:S(2)}, u32[]{:S(2)}) collective-permute-start(bf16[1440,240]{1,0:T(8,128)(2,1)S(1)} %product.9), channel_id=1, source_target_pairs={{0,8},{24,16},{1,9},{25,17},{2,10},{26,18},{3,11},{27,19},{4,12},{... | collective-permute-start | bytes 2073608 | tf_op jit(solution)/shard_map/ppermute | solution.py:343
  79.5 0.7 collective-permute-start.22
  80.2 9.2 %collective-permute-done.20.rest_ref = bf16[1200,256]{1,0:T(8,128)(2,1)S(1)} collective-permute-done((bf16[1200,256]{1,0:T(8,128)(2,1)S(1)}, bf16[1200,256]{1,0:T(8,128)(2,1)S(1)}, u32[]{:S(2)}, u32[]{:S(2)}) %collective-permute-start.20) | collective-permute-done | bytes 614432 | tf_op jit(solution)/shard_map/ppermute | solution.py:396
  89.4 1.3 collective-permute-start.21
  90.7 4.6 %collective-permute-start.18 = (bf16[1440,120]{1,0:T(8,128)(2,1)S(1)}, bf16[1440,120]{1,0:T(8,128)(2,1)S(1)}, u32[]{:S(2)}, u32[]{:S(2)}) collective-permute-start(bf16[1440,120]{1,0:T(8,128)(2,1)S(1)} %get-tuple-element.112), channel_id=1, source_target_pairs={{0,8},{24,16},{1,9},{25,17},{2,10},{26,18},{3,11},{27,19},{4,12},{... | collective-permute-start | bytes 1036808 | tf_op jit(solution)/shard_map/ppermute | solution.py:343
  95.3 0.8 collective-permute-start.19
  96.2 1.0 product.10
  97.1 1.9 %product.11 = (bf16[1440,240]{1,0:T(8,128)(2,1)S(1)}, bf16[1440,240]{1,0:T(8,128)(2,1)S(1)}, bf16[1440,240]{1,0:T(8,128)(2,1)S(1)}) custom-call(bf16[1440,960]{1,0:T(8,128)(2,1)S(1)} %partial.3.partial_ref, bf16[960,240]{1,0:T(8,128)(2,1)S(1)} %collective-permute-done.8.refs_0_, bf16[960,240]{1,0:T(8,128)(2,1)S(1)} %collective-permute-done.9.refs_1_, ...), custom_call_target="tpu_custom_call" | custom-call | tf_op jit(solution)/shard_map/product/pallas_call | solution.py:314
  99.0 2.1 %collective-permute-done.18.got_ref = bf16[1440,120]{1,0:T(8,128)(2,1)S(1)} collective-permute-done((bf16[1440,120]{1,0:T(8,128)(2,1)S(1)}, bf16[1440,120]{1,0:T(8,128)(2,1)S(1)}, u32[]{:S(2)}, u32[]{:S(2)}) %collective-permute-start.18) | collective-permute-done | bytes 345632 | tf_op jit(solution)/shard_map/ppermute | solution.py:343
  101.2 3.1 %collective-permute-done.21.refs_0_.refs_3_ = bf16[1200,256]{1,0:T(8,128)(2,1)S(1)} collective-permute-done((bf16[1200,256]{1,0:T(8,128)(2,1)S(1)}, bf16[1200,256]{1,0:T(8,128)(2,1)S(1)}, u32[]{:S(2)}, u32[]{:S(2)}) %collective-permute-start.21) | collective-permute-done | bytes 614432 | tf_op jit(solution)/shard_map/ppermute | solution.py:245
  104.3 2.0 %collective-permute-start.23 = (bf16[1440,240]{1,0:T(8,128)(2,1)S(1)}, bf16[1440,240]{1,0:T(8,128)(2,1)S(1)}, u32[]{:S(2)}, u32[]{:S(2)}) collective-permute-start(bf16[1440,240]{1,0:T(8,128)(2,1)S(1)} %get-tuple-element.132), channel_id=1, source_target_pairs={{0,8},{24,16},{1,9},{25,17},{2,10},{26,18},{3,11},{27,19},{4,12},{... | collective-permute-start | bytes 2073608 | tf_op jit(solution)/shard_map/ppermute | solution.py:343
  106.5 0.7 collective-permute-start.24
  107.2 1.3 collective-permute-start.27
  108.6 2.7 %collective-permute-start.25 = (bf16[1440,120]{1,0:T(8,128)(2,1)S(1)}, bf16[1440,120]{1,0:T(8,128)(2,1)S(1)}, u32[]{:S(2)}, u32[]{:S(2)}) collective-permute-start(bf16[1440,120]{1,0:T(8,128)(2,1)S(1)} %add.8), channel_id=1, source_target_pairs={{0,8},{16,24},{8,0},{24,16},{1,9},{17,25},{9,1},{25,17},{2,10},{18... | collective-permute-start | bytes 1036808 | tf_op jit(solution)/shard_map/ppermute | solution.py:343
  111.4 0.7 collective-permute-start.26
  112.1 18.5 %collective-permute-done.25.refs_0_ = bf16[1440,120]{1,0:T(8,128)(2,1)S(1)} collective-permute-done((bf16[1440,120]{1,0:T(8,128)(2,1)S(1)}, bf16[1440,120]{1,0:T(8,128)(2,1)S(1)}, u32[]{:S(2)}, u32[]{:S(2)}) %collective-permute-start.25) | collective-permute-done | bytes 345632 | tf_op jit(solution)/shard_map/ppermute | solution.py:343
  130.8 0.7 collective-permute-start.29
  131.6 1.3 left.1
  132.9 1.7 %final.3 = f32[1440,120]{1,0:T(8,128)} custom-call(bf16[1440,120]{1,0:T(8,128)(2,1)S(1)} %get-tuple-element.149.own_ref, bf16[1440,120]{1,0:T(8,128)(2,1)S(1)} %collective-permute-done.25.refs_0_, bf16[1440,120]{1,0:T(8,128)(2,1)S(1)} %collective-permute-done.26.refs_1_, bf16[960,960]{1,0:T(8,128)(2,1)S(1)} %get-tuple-element.147.refs_2_, ...), custom_call_target="tpu_custom_call" | custom-call | tf_op jit(solution)/shard_map/final/pallas_call | solution.py:437
  134.6 9.9 %collective-permute-done.28.refs_0_ = bf16[1440,240]{1,0:T(8,128)(2,1)S(1)} collective-permute-done((bf16[1440,240]{1,0:T(8,128)(2,1)S(1)}, bf16[1440,240]{1,0:T(8,128)(2,1)S(1)}, u32[]{:S(2)}, u32[]{:S(2)}) %collective-permute-start.28) | collective-permute-done | bytes 691232 | tf_op jit(solution)/shard_map/ppermute | solution.py:343
  144.6 2.0 %final.2 = f32[1440,240]{1,0:T(8,128)} custom-call(bf16[1440,240]{1,0:T(8,128)(2,1)S(1)} %get-tuple-element.130.own_ref, bf16[1440,240]{1,0:T(8,128)(2,1)S(1)} %collective-permute-done.28.refs_0_, bf16[1440,240]{1,0:T(8,128)(2,1)S(1)} %collective-permute-done.29.refs_1_, bf16[960,960]{1,0:T(8,128)(2,1)S(1)} %get-tuple-element.147.refs_2_, ...), custom_call_target="tpu_custom_call" | custom-call | tf_op jit(solution)/shard_map/final/pallas_call | solution.py:437
  (44 shorter events, 4.6 us)
Async XLA Ops:
  2.4 32.8 %copy-start.1 = (bf16[1456,128]{1,0:T(8,128)(2,1)S(1)}, bf16[1456,128]{1,0:T(8,128)(2,1)}, u32[]{:S(2)}) copy-start(bf16[1456,128]{1,0:T(8,128)(2,1)} %tokens.1.refs_0_) | copy-start | bytes 1118212
  2.4 17.2 %collective-permute-start = (bf16[1456,128]{1,0:T(8,128)(2,1)}, bf16[1456,128]{1,0:T(8,128)(2,1)S(1)}, u32[]{:S(2)}, u32[]{:S(2)}) collective-permute-start(bf16[1456,128]{1,0:T(8,128)(2,1)} %tokens.1.refs_0_), channel_id=1, source_target_pairs={{0,2},{1,3},{2,0},{3,1},{4,6},{5,7},{6,4},{7,5},{8,10},{9,11},{10,... | collective-permute-start | bytes 1118216 | tf_op jit(solution)/shard_map/ppermute | solution.py:351
  5.4 14.2 %collective-permute-start.1 = (bf16[1456,128]{1,0:T(8,128)(2,1)}, bf16[1456,128]{1,0:T(8,128)(2,1)S(1)}, u32[]{:S(2)}, u32[]{:S(2)}) collective-permute-start(bf16[1456,128]{1,0:T(8,128)(2,1)} %tokens.1.refs_0_), channel_id=1, source_target_pairs={{0,4},{1,5},{2,6},{3,7},{4,0},{5,1},{6,2},{7,3},{8,12},{9,13},{10,... | collective-permute-start | bytes 1118216 | tf_op jit(solution)/shard_map/ppermute | solution.py:351
  6.9 5.1 %collective-permute-start.2 = (bf16[480,120]{1,0:T(8,128)(2,1)}, bf16[480,120]{1,0:T(8,128)(2,1)S(1)}, u32[]{:S(2)}, u32[]{:S(2)}) collective-permute-start(bf16[480,120]{1,0:T(8,128)(2,1)} %bitcast.19), channel_id=1, source_target_pairs={{8,16},{16,8},{9,17},{17,9},{10,18},{18,10},{11,19},{19,11},{12,20... | collective-permute-start | bytes 345608 | tf_op jit(solution)/shard_map/ppermute | solution.py:245
  7.6 7.5 %collective-permute-start.4 = (bf16[480,120]{1,0:T(8,128)(2,1)}, bf16[480,120]{1,0:T(8,128)(2,1)S(1)}, u32[]{:S(2)}, u32[]{:S(2)}) collective-permute-start(bf16[480,120]{1,0:T(8,128)(2,1)} %bitcast.20), channel_id=1, source_target_pairs={{0,8},{16,24},{8,0},{24,16},{1,9},{17,25},{9,1},{25,17},{2,10},{18... | collective-permute-start | bytes 345608 | tf_op jit(solution)/shard_map/ppermute | solution.py:245
  12.1 7.5 %collective-permute-start.3 = (bf16[480,120]{1,0:T(8,128)(2,1)S(1)}, bf16[480,120]{1,0:T(8,128)(2,1)S(1)}, u32[]{:S(2)}, u32[]{:S(2)}) collective-permute-start(bf16[480,120]{1,0:T(8,128)(2,1)S(1)} %collective-permute-done.2.refs_1_), channel_id=1, source_target_pairs={{16,24},{8,0},{17,25},{9,1},{18,26},{10,2},{19,27},{11,3},{20,28},... | collective-permute-start | bytes 345608 | tf_op jit(solution)/shard_map/ppermute | solution.py:245
  15.1 4.5 %collective-permute-start.5 = (bf16[480,120]{1,0:T(8,128)(2,1)S(1)}, bf16[480,120]{1,0:T(8,128)(2,1)S(1)}, u32[]{:S(2)}, u32[]{:S(2)}) collective-permute-start(bf16[480,120]{1,0:T(8,128)(2,1)S(1)} %collective-permute-done.4.refs_0_), channel_id=1, source_target_pairs={{8,16},{16,8},{9,17},{17,9},{10,18},{18,10},{11,19},{19,11},{12,20... | collective-permute-start | bytes 345608 | tf_op jit(solution)/shard_map/ppermute | solution.py:245
  19.6 15.5 %collective-permute-start.8 = (bf16[960,240]{1,0:T(8,128)(2,1)}, bf16[960,240]{1,0:T(8,128)(2,1)S(1)}, u32[]{:S(2)}, u32[]{:S(2)}) collective-permute-start(bf16[960,240]{1,0:T(8,128)(2,1)} %bitcast.16), channel_id=1, source_target_pairs={{0,8},{16,24},{8,0},{24,16},{1,9},{17,25},{9,1},{25,17},{2,10},{18... | collective-permute-start | bytes 1382408 | tf_op jit(solution)/shard_map/ppermute | solution.py:245
  23.9 11.2 %collective-permute-start.9 = (bf16[960,240]{1,0:T(8,128)(2,1)}, bf16[960,240]{1,0:T(8,128)(2,1)S(1)}, u32[]{:S(2)}, u32[]{:S(2)}) collective-permute-start(bf16[960,240]{1,0:T(8,128)(2,1)} %bitcast.17), channel_id=1, source_target_pairs={{8,16},{16,8},{9,17},{17,9},{10,18},{18,10},{11,19},{19,11},{12,20... | collective-permute-start | bytes 1382408 | tf_op jit(solution)/shard_map/ppermute | solution.py:245
  24.6 10.5 %collective-permute-start.6 = (bf16[1456,128]{1,0:T(8,128)(2,1)}, bf16[1456,128]{1,0:T(8,128)(2,1)S(1)}, u32[]{:S(2)}, u32[]{:S(2)}) collective-permute-start(bf16[1456,128]{1,0:T(8,128)(2,1)} %tokens.1.refs_0_), channel_id=1, source_target_pairs={{0,6},{1,7},{2,4},{3,5},{4,2},{5,3},{6,0},{7,1},{8,14},{9,15},{10,... | collective-permute-start | bytes 1118216 | tf_op jit(solution)/shard_map/ppermute | solution.py:351
  25.2 10.0 %collective-permute-start.7 = (bf16[480,120]{1,0:T(8,128)(2,1)S(1)}, bf16[480,120]{1,0:T(8,128)(2,1)S(1)}, u32[]{:S(2)}, u32[]{:S(2)}) collective-permute-start(bf16[480,120]{1,0:T(8,128)(2,1)S(1)} %collective-permute-done.5.refs_1_), channel_id=1, source_target_pairs={{16,24},{8,0},{17,25},{9,1},{18,26},{10,2},{19,27},{11,3},{20,28},... | collective-permute-start | bytes 345608 | tf_op jit(solution)/shard_map/ppermute | solution.py:245
  26.4 1.0 copy-start.2
  27.5 0.9 copy-start.5
  29.0 11.9 %copy-start = (bf16[1,1,8,128,1440]{3,4,2,1,0:T(8,128)(2,1)S(1)}, bf16[1,1,8,128,1440]{3,4,2,1,0:T(8,128)(2,1)}, u32[]{:S(2)}) copy-start(bf16[1,1,8,128,1440]{3,4,2,1,0:T(8,128)(2,1)} %param.13) | copy-start | bytes 8847364
  35.9 5.0 %collective-permute-start.13 = (bf16[4,1456,128]{2,1,0:T(8,128)(2,1)S(1)}, bf16[4,1456,128]{2,1,0:T(8,128)(2,1)S(1)}, u32[]{:S(2)}, u32[]{:S(2)}) collective-permute-start(bf16[4,1456,128]{2,1,0:T(8,128)(2,1)S(1)} %collect.1.mine_ref), channel_id=1, source_target_pairs={{0,1},{1,0},{2,3},{3,2},{4,5},{5,4},{6,7},{7,6},{8,9},{9,8},{10,11... | collective-permute-start | bytes 4472840 | tf_op jit(solution)/shard_map/ppermute | solution.py:371
  35.9 18.2 %collective-permute-start.12 = (bf16[1200,256]{1,0:T(8,128)(2,1)S(1)}, bf16[1200,256]{1,0:T(8,128)(2,1)S(1)}, u32[]{:S(2)}, u32[]{:S(2)}) collective-permute-start(bf16[1200,256]{1,0:T(8,128)(2,1)S(1)} %pack_left.1.own_ref), channel_id=1, source_target_pairs={{0,8},{24,16},{1,9},{25,17},{2,10},{26,18},{3,11},{27,19},{4,12},{... | collective-permute-start | bytes 1843208 | tf_op jit(solution)/shard_map/ppermute | solution.py:375
  38.9 15.2 %collective-permute-start.10 = (bf16[960,240]{1,0:T(8,128)(2,1)S(1)}, bf16[960,240]{1,0:T(8,128)(2,1)S(1)}, u32[]{:S(2)}, u32[]{:S(2)}) collective-permute-start(bf16[960,240]{1,0:T(8,128)(2,1)S(1)} %collective-permute-done.9.refs_1_), channel_id=1, source_target_pairs={{16,24},{8,0},{17,25},{9,1},{18,26},{10,2},{19,27},{11,3},{20,28},... | collective-permute-start | bytes 1382408 | tf_op jit(solution)/shard_map/ppermute | solution.py:245
  40.2 13.9 %collective-permute-start.11 = (bf16[960,240]{1,0:T(8,128)(2,1)S(1)}, bf16[960,240]{1,0:T(8,128)(2,1)S(1)}, u32[]{:S(2)}, u32[]{:S(2)}) collective-permute-start(bf16[960,240]{1,0:T(8,128)(2,1)S(1)} %collective-permute-done.8.refs_0_), channel_id=1, source_target_pairs={{8,16},{16,8},{9,17},{17,9},{10,18},{18,10},{11,19},{19,11},{12,20... | collective-permute-start | bytes 1382408 | tf_op jit(solution)/shard_map/ppermute | solution.py:245
  54.1 19.5 %collective-permute-start.16 = (bf16[1200,256]{1,0:T(8,128)(2,1)S(1)}, bf16[1200,256]{1,0:T(8,128)(2,1)S(1)}, u32[]{:S(2)}, u32[]{:S(2)}) collective-permute-start(bf16[1200,256]{1,0:T(8,128)(2,1)S(1)} %pack_left.1.own_ref), channel_id=1, source_target_pairs={{8,16},{16,8},{9,17},{17,9},{10,18},{18,10},{11,19},{19,11},{12,20... | collective-permute-start | bytes 1843208 | tf_op jit(solution)/shard_map/ppermute | solution.py:385
  54.8 17.8 %collective-permute-start.14 = (bf16[960,240]{1,0:T(8,128)(2,1)S(1)}, bf16[960,240]{1,0:T(8,128)(2,1)S(1)}, u32[]{:S(2)}, u32[]{:S(2)}) collective-permute-start(bf16[960,240]{1,0:T(8,128)(2,1)S(1)} %collective-permute-done.11.refs_1_), channel_id=1, source_target_pairs={{16,24},{8,0},{17,25},{9,1},{18,26},{10,2},{19,27},{11,3},{20,28},... | collective-permute-start | bytes 1382408 | tf_op jit(solution)/shard_map/ppermute | solution.py:245
  56.1 17.5 %collective-permute-start.15 = (bf16[1440,120]{1,0:T(8,128)(2,1)S(1)}, bf16[1440,120]{1,0:T(8,128)(2,1)S(1)}, u32[]{:S(2)}, u32[]{:S(2)}) collective-permute-start(bf16[1440,120]{1,0:T(8,128)(2,1)S(1)} %product.6), channel_id=1, source_target_pairs={{0,8},{24,16},{1,9},{25,17},{2,10},{26,18},{3,11},{27,19},{4,12},{... | collective-permute-start | bytes 1036808 | tf_op jit(solution)/shard_map/ppermute | solution.py:343
  69.1 0.9 copy-start.4
  73.6 15.8 %collective-permute-start.20 = (bf16[1200,256]{1,0:T(8,128)(2,1)S(1)}, bf16[1200,256]{1,0:T(8,128)(2,1)S(1)}, u32[]{:S(2)}, u32[]{:S(2)}) collective-permute-start(bf16[1200,256]{1,0:T(8,128)(2,1)S(1)} %pack_left.1.own_ref), channel_id=1, source_target_pairs={{16,24},{8,0},{17,25},{9,1},{18,26},{10,2},{19,27},{11,3},{20,28},... | collective-permute-start | bytes 1843208 | tf_op jit(solution)/shard_map/ppermute | solution.py:396
  74.9 26.2 %collective-permute-start.17 = (bf16[1440,240]{1,0:T(8,128)(2,1)S(1)}, bf16[1440,240]{1,0:T(8,128)(2,1)S(1)}, u32[]{:S(2)}, u32[]{:S(2)}) collective-permute-start(bf16[1440,240]{1,0:T(8,128)(2,1)S(1)} %product.9), channel_id=1, source_target_pairs={{0,8},{24,16},{1,9},{25,17},{2,10},{26,18},{3,11},{27,19},{4,12},{... | collective-permute-start | bytes 2073608 | tf_op jit(solution)/shard_map/ppermute | solution.py:343
  79.5 19.5 %collective-permute-start.22 = (bf16[1200,256]{1,0:T(8,128)(2,1)S(1)}, bf16[1200,256]{1,0:T(8,128)(2,1)S(1)}, u32[]{:S(2)}, u32[]{:S(2)}) collective-permute-start(bf16[1200,256]{1,0:T(8,128)(2,1)S(1)} %collective-permute-done.12.ends_ref), channel_id=1, source_target_pairs={{8,16},{16,8},{9,17},{17,9},{10,18},{18,10},{11,19},{19,11},{12,20... | collective-permute-start | bytes 1843208 | tf_op jit(solution)/shard_map/ppermute | solution.py:245
  89.4 14.9 %collective-permute-start.21 = (bf16[1200,256]{1,0:T(8,128)(2,1)S(1)}, bf16[1200,256]{1,0:T(8,128)(2,1)S(1)}, u32[]{:S(2)}, u32[]{:S(2)}) collective-permute-start(bf16[1200,256]{1,0:T(8,128)(2,1)S(1)} %collective-permute-done.16.odd_ref), channel_id=1, source_target_pairs={{16,24},{8,0},{17,25},{9,1},{18,26},{10,2},{19,27},{11,3},{20,28},... | collective-permute-start | bytes 1843208 | tf_op jit(solution)/shard_map/ppermute | solution.py:245
  90.7 10.5 %collective-permute-start.18 = (bf16[1440,120]{1,0:T(8,128)(2,1)S(1)}, bf16[1440,120]{1,0:T(8,128)(2,1)S(1)}, u32[]{:S(2)}, u32[]{:S(2)}) collective-permute-start(bf16[1440,120]{1,0:T(8,128)(2,1)S(1)} %get-tuple-element.112), channel_id=1, source_target_pairs={{0,8},{24,16},{1,9},{25,17},{2,10},{26,18},{3,11},{27,19},{4,12},{... | collective-permute-start | bytes 1036808 | tf_op jit(solution)/shard_map/ppermute | solution.py:343
  95.3 1.8 %copy-start.3 = (bf16[1,960,240]{2,1,0:T(8,128)(2,1)S(1)}, bf16[1,960,240]{2,1,0:T(8,128)(2,1)}, u32[]{:S(2)}) copy-start(bf16[1,960,240]{2,1,0:T(8,128)(2,1)} %param.16) | copy-start | bytes 1382404
  95.3 5.8 %collective-permute-start.19 = (bf16[1440,120]{1,0:T(8,128)(2,1)S(1)}, bf16[1440,120]{1,0:T(8,128)(2,1)S(1)}, u32[]{:S(2)}, u32[]{:S(2)}) collective-permute-start(bf16[1440,120]{1,0:T(8,128)(2,1)S(1)} %add.6), channel_id=1, source_target_pairs={{8,16},{16,8},{9,17},{17,9},{10,18},{18,10},{11,19},{19,11},{12,20... | collective-permute-start | bytes 1036808 | tf_op jit(solution)/shard_map/ppermute | solution.py:343
  104.3 26.3 %collective-permute-start.23 = (bf16[1440,240]{1,0:T(8,128)(2,1)S(1)}, bf16[1440,240]{1,0:T(8,128)(2,1)S(1)}, u32[]{:S(2)}, u32[]{:S(2)}) collective-permute-start(bf16[1440,240]{1,0:T(8,128)(2,1)S(1)} %get-tuple-element.132), channel_id=1, source_target_pairs={{0,8},{24,16},{1,9},{25,17},{2,10},{26,18},{3,11},{27,19},{4,12},{... | collective-permute-start | bytes 2073608 | tf_op jit(solution)/shard_map/ppermute | solution.py:343
  106.5 24.0 %collective-permute-start.24 = (bf16[1440,240]{1,0:T(8,128)(2,1)S(1)}, bf16[1440,240]{1,0:T(8,128)(2,1)S(1)}, u32[]{:S(2)}, u32[]{:S(2)}) collective-permute-start(bf16[1440,240]{1,0:T(8,128)(2,1)S(1)} %add.7), channel_id=1, source_target_pairs={{8,16},{16,8},{9,17},{17,9},{10,18},{18,10},{11,19},{19,11},{12,20... | collective-permute-start | bytes 2073608 | tf_op jit(solution)/shard_map/ppermute | solution.py:343
  107.2 23.3 %collective-permute-start.27 = (bf16[1200,256]{1,0:T(8,128)(2,1)S(1)}, bf16[1200,256]{1,0:T(8,128)(2,1)S(1)}, u32[]{:S(2)}, u32[]{:S(2)}) collective-permute-start(bf16[1200,256]{1,0:T(8,128)(2,1)S(1)} %collective-permute-done.22.refs_1_), channel_id=1, source_target_pairs={{16,24},{8,0},{17,25},{9,1},{18,26},{10,2},{19,27},{11,3},{20,28},... | collective-permute-start | bytes 1843208 | tf_op jit(solution)/shard_map/ppermute | solution.py:245
  108.6 21.9 %collective-permute-start.25 = (bf16[1440,120]{1,0:T(8,128)(2,1)S(1)}, bf16[1440,120]{1,0:T(8,128)(2,1)S(1)}, u32[]{:S(2)}, u32[]{:S(2)}) collective-permute-start(bf16[1440,120]{1,0:T(8,128)(2,1)S(1)} %add.8), channel_id=1, source_target_pairs={{0,8},{16,24},{8,0},{24,16},{1,9},{17,25},{9,1},{25,17},{2,10},{18... | collective-permute-start | bytes 1036808 | tf_op jit(solution)/shard_map/ppermute | solution.py:343
  111.4 19.1 %collective-permute-start.26 = (bf16[1440,120]{1,0:T(8,128)(2,1)S(1)}, bf16[1440,120]{1,0:T(8,128)(2,1)S(1)}, u32[]{:S(2)}, u32[]{:S(2)}) collective-permute-start(bf16[1440,120]{1,0:T(8,128)(2,1)S(1)} %add.9), channel_id=1, source_target_pairs={{8,16},{16,8},{9,17},{17,9},{10,18},{18,10},{11,19},{19,11},{12,20... | collective-permute-start | bytes 1036808 | tf_op jit(solution)/shard_map/ppermute | solution.py:343
  130.7 13.8 %collective-permute-start.28 = (bf16[1440,240]{1,0:T(8,128)(2,1)S(1)}, bf16[1440,240]{1,0:T(8,128)(2,1)S(1)}, u32[]{:S(2)}, u32[]{:S(2)}) collective-permute-start(bf16[1440,240]{1,0:T(8,128)(2,1)S(1)} %add.10), channel_id=1, source_target_pairs={{0,8},{16,24},{8,0},{24,16},{1,9},{17,25},{9,1},{25,17},{2,10},{18... | collective-permute-start | bytes 2073608 | tf_op jit(solution)/shard_map/ppermute | solution.py:343
  130.8 13.7 %collective-permute-start.29 = (bf16[1440,240]{1,0:T(8,128)(2,1)S(1)}, bf16[1440,240]{1,0:T(8,128)(2,1)S(1)}, u32[]{:S(2)}, u32[]{:S(2)}) collective-permute-start(bf16[1440,240]{1,0:T(8,128)(2,1)S(1)} %add.11), channel_id=1, source_target_pairs={{8,16},{16,8},{9,17},{17,9},{10,18},{18,10},{11,19},{19,11},{12,20... | collective-permute-start | bytes 2073608 | tf_op jit(solution)/shard_map/ppermute | solution.py:343

commit v2 on v1

v2 whole, which is shorter than its diff:
```python
import functools

import jax
import jax.numpy as jnp
from jax import lax
from jax.experimental import pallas as pl
from jax.experimental.pallas import tpu as pltpu
from jax.sharding import PartitionSpec as P

BF16 = jnp.bfloat16
F32 = jnp.float32
LANES = 128
META_ROWS = 16
ROW_CHUNKS = 3
MIB = 1024 * 1024


def round_up(value, unit):
    return (value + unit - 1) // unit * unit


def params(mib):
    return pltpu.CompilerParams(vmem_limit_bytes=mib * MIB)


def cost(micros=0):
    return pl.CostEstimate(flops=int(micros * 1.15e9), bytes_accessed=0, transcendentals=0)


class Order:
    def __init__(self, tick):
        self.tick = tick

    def gate(self, ready, values):
        self.tick, _, values = lax.optimization_barrier((self.tick, ready, values))
        return values


def dot_nn(left, right):
    return lax.dot_general(left, right, (((1,), (0,)), ((), ())), preferred_element_type=F32)


def dot_nt(left, right):
    return lax.dot_general(left, right, (((1,), (1,)), ((), ())), preferred_element_type=F32)


ANY = pl.BlockSpec(memory_space=pl.ANY)
VMEM = pl.BlockSpec(memory_space=pltpu.VMEM)


class Fold:
    def __init__(self, rows_w, rows_n, wide, narrow):
        self.rows_w, self.rows_n, self.wide, self.narrow = rows_w, rows_n, wide, narrow
        self.lanes = round_up(wide, LANES)
        self.step = round_up(narrow, LANES)
        self.ways = max(1, self.lanes // self.step)
        while rows_n % (self.ways * 16):
            self.ways -= 1
        self.part = rows_n // self.ways
        self.rows = rows_w + self.part
        self.shape = (self.rows, self.lanes)

    def write(self, ref, wide_value, narrow_value):
        ref[...] = jnp.zeros(self.shape, ref.dtype)
        ref[0 : self.rows_w, 0 : self.wide] = wide_value
        for way in range(self.ways):
            start = way * self.step
            ref[self.rows_w : self.rows, start : start + self.narrow] = narrow_value[
                way * self.part : (way + 1) * self.part
            ]

    def wide_of(self, value):
        return value[0 : self.rows_w, 0 : self.wide]

    def narrow_of(self, value):
        low = value[self.rows_w : self.rows]
        parts = [low[:, way * self.step : way * self.step + self.narrow] for way in range(self.ways)]
        return parts[0] if self.ways == 1 else jnp.concatenate(parts, axis=0)


def token_kernel(root, cot_ref, gate_ref, route_ref, slot_ref, rw_ref, rn_ref, tok_ref, right_ref,
                 gate, route, slot, wide, narrow, meta, sem):
    width = cot_ref.shape[0]
    ways = gate_ref.shape[0]
    sources = (rw_ref, rn_ref, gate_ref, route_ref, slot_ref, cot_ref)
    targets = (wide, narrow, gate, route, slot, tok_ref.at[pl.ds(0, width)])
    copies = [
        pltpu.make_async_copy(source, target, sem.at[i])
        for i, (source, target) in enumerate(zip(sources, targets))
    ]
    for copy in copies:
        copy.start()
    for copy in copies[:5]:
        copy.wait()
    root.write(right_ref, wide[...], narrow[...])
    meta[...] = jnp.zeros(meta.shape, F32)
    meta[0:ways, :] = gate[...].astype(F32)
    meta[ways : 2 * ways, :] = route[...].astype(F32)
    meta[2 * ways : 3 * ways, :] = slot[...].astype(F32)
    tok_ref[width : width + META_ROWS, :] = meta[...].astype(BF16)
    copies[5].wait()


def pack_left_kernel(root, lw_ref, ln_ref, out_ref, wide, narrow, sem):
    copies = [
        pltpu.make_async_copy(lw_ref, wide, sem.at[0]),
        pltpu.make_async_copy(ln_ref, narrow, sem.at[1]),
    ]
    for copy in copies:
        copy.start()
    for copy in copies:
        copy.wait()
    root.write(out_ref, wide[...], narrow[...])


def partial_kernel(topk, width, block, gap, first, later, hidden_ref, *refs):
    sources, _, capacity = hidden_ref.shape
    out_ref, rows_ref = refs[-2:]
    token_refs = {}
    for i, m in enumerate(first + later):
        token_refs[2 * m] = refs[i]
        if i < len(first):
            token_refs[2 * m + 1] = refs[len(first + later)].at[i]
        else:
            token_refs[2 * m + 1] = refs[len(first + later) + 1 + i - len(first)]
    expert = lax.axis_index("expert")
    parts = ((0, block, 0), (block, width, gap))

    @pl.when(pl.program_id(0) == 0)
    def _():
        for offset in range(sources):
            token_ref = token_refs[offset]
            source = jnp.bitwise_xor(expert, offset)
            meta = token_ref[width : width + META_ROWS, :].astype(F32)
            tokens = meta.shape[1]
            place = lax.broadcasted_iota(jnp.int32, (capacity, tokens), 0).astype(F32)
            here = expert.astype(F32)
            weights = jnp.zeros((capacity, tokens), F32)
            for k in range(topk):
                gate = meta[k : k + 1, :]
                route = meta[topk + k : topk + k + 1, :]
                slot = meta[2 * topk + k : 2 * topk + k + 1, :]
                wanted = jnp.where(route == here, slot, -1.0)
                weights = jnp.where(place == wanted, gate, weights)
            weights = weights.astype(BF16)
            rows = pl.ds(pl.multiple_of(source * capacity, capacity), capacity)
            for low, high, at in parts:
                value = dot_nt(weights, token_ref[low:high, :]).astype(BF16)
                rows_ref[rows, at : at + high - low] = value

    if capacity % LANES == 0:
        hidden = jnp.concatenate([hidden_ref[s] for s in range(sources)], axis=1)
    for low, high, at in parts:
        columns = slice(at, at + high - low)
        if capacity % LANES == 0:
            total = dot_nn(hidden, rows_ref[:, columns])
        else:
            total = dot_nn(hidden_ref[0], rows_ref[0:capacity, columns])
            for s in range(1, sources):
                total += dot_nn(hidden_ref[s], rows_ref[s * capacity : (s + 1) * capacity, columns])
        out_ref[:, columns] = total.astype(BF16)


class Chain:
    def __init__(self, n, half, order, low, fold):
        self.n, self.half, self.order, self.low, self.fold = n, half, order, low, fold
        self.steps = max(t for t in range(1, 2 * n) if self.pairs(t, 0) or self.pairs(t, 1))

    def distance(self, t, z, s):
        i = z if z % 2 == s else self.n - 1 - z
        if (z % 2 == s and z == self.n - 1) or (z % 2 != s and z == 0):
            return 0
        k = t - 1 - i
        if 0 <= k < len(self.order) and self.order[k] > i:
            return self.order[k] - i
        return 0

    def pairs(self, t, s):
        return [
            (z, z + 1 if z % 2 == s else z - 1) for z in range(self.n) if self.distance(t, z, s)
        ]

    def sets(self, t):
        return [s for s in (0, 1) if self.pairs(t, s)]

    def adds(self, t, s):
        targets = {target for _, target in self.pairs(t - 1, 1 - s)} if t > 1 else set()
        return any(z in targets for z, _ in self.pairs(t, s))

    def arrivals(self, z):
        found = []
        for t in range(1, self.steps + 1):
            for s in (0, 1):
                for sender, target in self.pairs(t, s):
                    if target == z and self.distance(t, sender, s) == 1:
                        found.append((t, s))
        return found


def product_kernel(chain, t, keys, root, block, gap, partial_ref, *refs):
    root_refs = dict(zip(keys, refs))
    out_refs, piece_ref = refs[len(keys) : -1], refs[-1]
    z = lax.axis_index("dp")
    fold = chain.fold

    def product(root_ref, out_ref):
        piece = root_ref[...]
        rows = slice(chain.low, chain.low + fold.rows_w)
        wide = dot_nn(partial_ref[rows, 0:block], root.wide_of(piece))
        narrow = dot_nn(partial_ref[rows, gap : gap + root.rows_n], root.narrow_of(piece))
        fold.write(out_ref, wide.astype(BF16), narrow.astype(BF16))

    def take(root_ref):
        piece_ref[...] = root_ref[...]

    if t == 0:
        product(root_refs[0, 0], out_refs[0])
        return
    for s, out_ref in zip(chain.sets(t), out_refs):
        by_far = {}
        for here in range(chain.n):
            far = chain.distance(t, here, s)
            if far:
                by_far[far] = by_far.get(far, False) | (z == here)
        if len(by_far) <= 2:
            for far, here in by_far.items():
                pl.when(here)(functools.partial(product, root_refs[far, s], out_ref))
        else:
            for far, here in by_far.items():
                pl.when(here)(functools.partial(take, root_refs[far, s]))
            here = functools.reduce(jnp.logical_or, by_far.values())
            pl.when(here)(functools.partial(product, piece_ref, out_ref))


def add_kernel(chain, t, s, term_ref, got_ref, out_ref):
    z = lax.axis_index("dp")
    sends = functools.reduce(jnp.logical_or, [z == here for here, _ in chain.pairs(t, s)])

    @pl.when(sends)
    def _():
        out_ref[...] = (term_ref[...].astype(F32) + got_ref[...].astype(F32)).astype(BF16)


def left_kernel(root, n, own_ref, ends_ref, rest_ref, odd_ref, *refs):
    got = refs[: 2 * (n - 2)]
    wide_ref, narrow_ref, held, sem = refs[2 * (n - 2) :]
    z = lax.axis_index("dp")
    for here in range(n):
        even_ref = ends_ref if here in (1, n - 2) else rest_ref
        near = (even_ref, odd_ref) + got

        @pl.when(z == here)
        def _():
            copies = [pltpu.make_async_copy(own_ref, held.at[here], sem.at[here])]
            for q in range(n):
                if q != here:
                    s = here % 2 if q > here else 1 - here % 2
                    copies.append(
                        pltpu.make_async_copy(near[2 * (abs(q - here) - 1) + s], held.at[q], sem.at[q])
                    )
            for copy in copies:
                copy.start()
            for copy in copies:
                copy.wait()

    for q in range(n):
        piece = held[q]
        wide_ref[:, q * root.wide : (q + 1) * root.wide] = root.wide_of(piece)
        narrow_ref[:, q * root.narrow : (q + 1) * root.narrow] = root.narrow_of(piece)


def add_arrivals(chains, got_refs, own_refs, out_refs, dtype):
    z = lax.axis_index("dp")
    for here in range(chains[0].n):

        @pl.when(z == here)
        def _():
            for chain, own_ref, out_ref in zip(chains, own_refs, out_refs):
                value = own_ref[...].astype(F32)
                for t, s in chain.arrivals(here):
                    if (chain.half, t, s) in got_refs:
                        value += got_refs[chain.half, t, s][...].astype(F32)
                out_ref[...] = value.astype(dtype)


def total_kernel(chains, keys, *refs):
    got_refs = dict(zip(keys, refs[len(chains) :]))
    add_arrivals(chains, got_refs, refs[: len(chains)], refs[len(chains) + len(keys) :], F32)


def final_kernel(chains, block, keys, *refs):
    got_refs = dict(zip(keys, refs[len(chains) :]))
    wide_ref, narrow_ref, out_w_ref, out_n_ref = refs[len(chains) + len(keys) :][:4]
    totals = refs[len(refs) - len(chains) :]
    add_arrivals(chains, got_refs, refs[: len(chains)], totals, BF16)
    wides = [chain.fold.wide_of(total[...]) for chain, total in zip(chains, totals)]
    narrows = [chain.fold.narrow_of(total[...]) for chain, total in zip(chains, totals)]
    for parts, out_ref in ((wides, out_w_ref), (narrows, out_n_ref)):
        rows = jnp.concatenate(parts, axis=0)
        out_ref[0:block, :] = dot_nn(wide_ref[...], rows[0:block])
        out_ref[block:, :] = dot_nn(narrow_ref[...], rows[block:])


def collect_kernel(count, *refs):
    sem = refs[-1]
    out_ref = refs[count]
    copies = [pltpu.make_async_copy(refs[i], out_ref.at[i], sem.at[i]) for i in range(count)]
    for copy in copies:
        copy.start()
    for copy in copies:
        copy.wait()


def body(
    cotangent, gates, routes, slots, saved_hidden, left_wide, left_narrow, right_wide, right_narrow
):
    tokens, width = cotangent.shape
    topk = gates.shape[1]
    n = lax.axis_size("dp")
    experts = lax.axis_size("expert")
    chips = experts // 2
    _, _, sources, capacity, ffn = saved_hidden.shape
    block, wide = right_wide.shape[1:]
    rest, narrow = right_narrow.shape[1:]
    gap = round_up(block, LANES)
    span = gap + round_up(rest, LANES)
    root = Fold(block, rest, wide, narrow)
    cut = ffn // 64 * 32
    folds = [Fold(rows, rows, wide, narrow) for rows in (cut, ffn - cut)]
    sooner = [n - 2, n - 1] if n > 2 else [1]
    chains = [
        Chain(n, 0, sooner + list(range(n - 3, 0, -1)), 0, folds[0]),
        Chain(n, 1, list(range(n - 1, 0, -1)), cut, folds[1]),
    ]

    def gather_pairs(k, s):
        up = [(i, i + 1) for i in range(s, n - 1, 2) if i >= k - 1]
        return up + [(i + 1, i) for i in range(s, n - 1, 2) if i <= n - 1 - k]

    def hop(k, pieces):
        return [
            lax.ppermute(pieces[1 - s], "dp", gather_pairs(k, s)) if gather_pairs(k, s) else pieces[1 - s]
            for s in (0, 1)
        ]

    tok, right = pl.pallas_call(
        functools.partial(token_kernel, root),
        in_specs=[ANY] * 6,
        out_specs=[VMEM] * 2,
        out_shape=[
            jax.ShapeDtypeStruct((width + META_ROWS, tokens), BF16),
            jax.ShapeDtypeStruct(root.shape, BF16),
        ],
        scratch_shapes=[
            pltpu.VMEM((topk, tokens), BF16),
            pltpu.VMEM((topk, tokens), jnp.int32),
            pltpu.VMEM((topk, tokens), jnp.int32),
            pltpu.VMEM((block, wide), BF16),
            pltpu.VMEM((rest, narrow), BF16),
            pltpu.VMEM((META_ROWS, tokens), F32),
            pltpu.SemaphoreType.DMA((6,)),
        ],
        compiler_params=params(56),
        cost_estimate=cost(),
        name="tokens",
    )(cotangent.T, gates.T, routes.T, slots.T, right_wide[0], right_narrow[0])

    def collect(values):
        count = len(values)
        return pl.pallas_call(
            functools.partial(collect_kernel, count),
            in_specs=[ANY] * count,
            out_specs=ANY,
            out_shape=jax.ShapeDtypeStruct((count,) + tok.shape, BF16),
            scratch_shapes=[pltpu.SemaphoreType.DMA((count,))],
            compiler_params=params(16),
            cost_estimate=cost(),
            name="collect",
        )(*values)

    def pack_left(wide_piece, narrow_piece):
        return pl.pallas_call(
            functools.partial(pack_left_kernel, root),
            in_specs=[ANY] * 2,
            out_shape=jax.ShapeDtypeStruct(root.shape, BF16),
            scratch_shapes=[
                pltpu.VMEM((block, wide), BF16),
                pltpu.VMEM((rest, narrow), BF16),
                pltpu.SemaphoreType.DMA((2,)),
            ],
            compiler_params=params(16),
            cost_estimate=cost(),
            name="pack_left",
        )(wide_piece, narrow_piece)

    chunk_rows = ffn // ROW_CHUNKS
    hidden = jnp.swapaxes(saved_hidden[0, 0], 1, 2)

    def partial(first, later, mine, theirs_first, theirs_later):
        return pl.pallas_call(
            functools.partial(partial_kernel, topk, width, block, gap, first, later),
            grid=(ROW_CHUNKS,),
            in_specs=[pl.BlockSpec((sources, chunk_rows, capacity), lambda i: (0, i, 0))]
            + [VMEM] * (1 + len(mine) + len(later)),
            out_specs=pl.BlockSpec((chunk_rows, span), lambda i: (i, 0)),
            out_shape=jax.ShapeDtypeStruct((ffn, span), BF16),
            scratch_shapes=[pltpu.VMEM((sources * capacity, span), BF16)],
            compiler_params=params(32),
            cost_estimate=cost(),
            name="partial",
        )(hidden, *mine, theirs_first, *theirs_later)

    def product(chain, t, value, got):
        keys = [(0, 0)]
        if t:
            keys = sorted({(chain.distance(t, z, s), s) for z in range(n) for s in (0, 1)})
            keys = [key for key in keys if key[0]]
        sets = chain.sets(t) if t else [0]
        made = pl.pallas_call(
            functools.partial(product_kernel, chain, t, keys, root, block, gap),
            in_specs=[VMEM] * (1 + len(keys)),
            out_specs=[VMEM] * len(sets),
            out_shape=[jax.ShapeDtypeStruct(chain.fold.shape, BF16)] * len(sets),
            scratch_shapes=[pltpu.VMEM(root.shape, BF16)],
            compiler_params=params(16),
            cost_estimate=cost(),
            name="product",
        )(value, *[got[far][s] for far, s in keys])
        return dict(zip(sets, made))

    def add(chain, t, s, term, got):
        return pl.pallas_call(
            functools.partial(add_kernel, chain, t, s),
            in_specs=[VMEM] * 2,
            out_specs=VMEM,
            out_shape=jax.ShapeDtypeStruct(term.shape, BF16),
            compiler_params=params(16),
            cost_estimate=cost(),
            name="add",
        )(term, got)

    order = Order(slots)
    straight = [m for m in range(1, chips) if m & (m - 1) == 0]
    mine = {0: tok}
    for m in straight:
        mine[m] = lax.ppermute(tok, "expert", [(i, i ^ (2 * m)) for i in range(experts)])
    got = [[right, right]]
    got.append(hop(1, got[0]))
    left = pack_left(left_wide[0], left_narrow[0])
    mine, got, left = order.gate((), (mine, got, left))

    first = [0] + straight
    later = [m for m in range(1, chips) if m not in straight]
    for m in later:
        mine[m] = lax.ppermute(mine[0], "expert", [(i, i ^ (2 * m)) for i in range(experts)])
    for k in range(2, n - 1):
        got.append(hop(k, got[-1]))

    def sibling(piece):
        return lax.ppermute(piece, "expert", [(i, i ^ 1) for i in range(experts)])

    theirs_first = sibling(collect([mine[m] for m in first]))
    ends = [pair for pair in gather_pairs(1, 0) if pair in ((0, 1), (n - 1, n - 2))]
    others = [pair for pair in gather_pairs(1, 0) if pair not in ends]
    left_ends = lax.ppermute(left, "dp", ends)
    theirs_later = [sibling(mine[m]) for m in later]
    value = partial(first, later, [mine[m] for m in first + later], theirs_first, theirs_later)
    got, left, left_ends, value = order.gate((), (got, left, left_ends, value))

    one, two = chains
    sent, terms = {}, {}

    def hop_one(pairs, piece):
        return lax.ppermute(piece, "dp", pairs) if pairs else piece

    def make(chain, t):
        terms[chain.half, t] = product(chain, t, value, got)

    def wait(keys, more=(), values=()):
        ready, _, values = order.gate((), ([sent[key] for key in keys], more, values))
        sent.update(zip(keys, ready))
        return values

    def go(chain, t, s):
        term = terms[chain.half, t][s]
        if chain.adds(t, s):
            term = add(chain, t, s, term, sent[chain.half, t - 1, 1 - s])
        sent[chain.half, t, s] = lax.ppermute(term, "dp", chain.pairs(t, s))

    make(one, 1)
    for s in one.sets(1):
        go(one, 1, s)
    for k in range(max(2, n - 1), n):
        got.append(hop(k, got[-1]))
    left_odd = hop_one(gather_pairs(1, 1), left)
    left_rest = hop_one(others, left)
    inner = {target for _, target in ends}
    if all(pair[0] in inner for pair in gather_pairs(2, 1)):
        left_even = left_ends
    else:
        z = lax.axis_index("dp")
        left_even = jnp.where((z == 1) | (z == n - 2), left_ends, left_rest)
    second = [None, hop_one(gather_pairs(2, 1), left_even)]
    own = [product(chain, 0, value, got)[0] for chain in chains]

    got, value, left_odd = wait([(0, 1, s) for s in one.sets(1)], (), (got, value, left_odd))
    make(two, 1)
    make(one, 2)
    for s in two.sets(1):
        go(two, 1, s)
    if n == 4:
        go(one, 2, 1)
        second[0] = hop_one(gather_pairs(2, 0), left_odd)
        left_rest, second[1], terms[0, 2] = wait([], (), (left_rest, second[1], terms[0, 2]))
        go(one, 2, 0)
        third = hop_one(gather_pairs(3, 0), second[1])
        make(two, 2)
        second[0], terms[1, 2] = wait([(1, 1, 0)], (), (second[0], terms[1, 2]))
        go(two, 2, 1)
        go(two, 2, 0)
        make(one, 3)
        terms[0, 3] = wait([(0, 2, 0), (0, 2, 1)], (), terms[0, 3])
        go(one, 3, 1)
        go(one, 3, 0)
        make(two, 3)
        third, terms[1, 3] = wait([(1, 2, 1)], (), (third, terms[1, 3]))
        go(two, 3, 0)
        make(one, 4)
        terms[0, 4], terms[1, 3] = wait([(0, 3, 1), (1, 2, 0)], (), (terms[0, 4], terms[1, 3]))
        go(one, 4, 0)
        go(two, 3, 1)
        lefts = [[left, left], [left_even, left_odd], second, [third, third]]
    else:
        for s in one.sets(2):
            go(one, 2, s)
        second[0] = hop_one(gather_pairs(2, 0), left_odd)
        lefts = [[left, left], [left_even, left_odd], second]
        for t in range(2, max(chain.steps for chain in chains) + 1):
            for chain in chains:
                if t <= chain.steps and (chain.half, t) != (0, 2):
                    make(chain, t)
                    before = [(chain.half, t - 1, s) for s in chain.sets(t - 1)]
                    terms[chain.half, t] = wait(before, (), terms[chain.half, t])
                    for s in chain.sets(t):
                        go(chain, t, s)
            if 2 < t < n:
                lefts.append(hop(t, wait([], (), lefts[-1])))

    left_inputs = [left, left_ends, left_rest, left_odd] + [item for pair in lefts[2:] for item in pair]
    left_w, left_n = pl.pallas_call(
        functools.partial(left_kernel, root, n),
        in_specs=[ANY] * len(left_inputs),
        out_shape=(
            jax.ShapeDtypeStruct((block, block), BF16),
            jax.ShapeDtypeStruct((rest, rest), BF16),
        ),
        scratch_shapes=[pltpu.VMEM((n,) + root.shape, BF16), pltpu.SemaphoreType.DMA((n,))],
        compiler_params=params(32),
        cost_estimate=cost(),
        name="left",
    )(*left_inputs)

    keys = sorted({(chain.half, t, s) for chain in chains for here in range(n) for t, s in chain.arrivals(here)})
    last = [(0, one.steps, s) for s in one.sets(one.steps)] + [(1, two.steps, 1)]
    early = [key for key in keys if key not in last]
    last = [key for key in keys if key in last]
    own = wait(early, (left_w, left_n), own)
    totals = pl.pallas_call(
        functools.partial(total_kernel, chains, early),
        in_specs=[VMEM] * (len(chains) + len(early)),
        out_specs=[VMEM] * len(chains),
        out_shape=[jax.ShapeDtypeStruct(chain.fold.shape, F32) for chain in chains],
        compiler_params=params(32),
        cost_estimate=cost(3),
        name="total",
    )(*own, *[sent[key] for key in early])
    out_w, out_n = pl.pallas_call(
        functools.partial(final_kernel, chains, block, last),
        in_specs=[VMEM] * (len(chains) + len(last) + 2),
        out_specs=[VMEM] * 2,
        out_shape=[jax.ShapeDtypeStruct((ffn, wide), F32), jax.ShapeDtypeStruct((ffn, narrow), F32)],
        scratch_shapes=[pltpu.VMEM(chain.fold.shape, BF16) for chain in chains],
        compiler_params=params(32),
        cost_estimate=cost(),
        name="final",
    )(*totals, *[sent[key] for key in last], left_w, left_n)
    return out_w[None], out_n[None]


def solution(mesh):
    return jax.shard_map(
        body,
        mesh=mesh,
        in_specs=(
            P(("dp", "expert"), None),
            P(("dp", "expert"), None),
            P(("dp", "expert"), None),
            P(("dp", "expert"), None),
            P("dp", "expert", None, None, None),
            P("expert", None, "dp"),
            P("expert", None, "dp"),
            P("expert", None, "dp"),
            P("expert", None, "dp"),
        ),
        out_specs=(P("expert", None, "dp"), P("expert", None, "dp")),
        check_vma=False,
    )
```

time: 147 us -> 133 us (0.905)
  waiting for transfers between devices: 65.8 us -> 49.2 us
  starting transfers between devices: 55.2 us -> 59.6 us
  Pallas kernels: 22.1 us -> 20.6 us
    ppermute x13 -> x5, waiting for transfers between devices: 26.1 us -> 2.18 us  [hop(): lax.ppermute(pieces[1 - s], 'dp', gather_pairs(k, s))]
    ppermute x13 -> x5, starting transfers between devices: 19.9 us -> 7.04 us  [hop(): lax.ppermute(pieces[1 - s], 'dp', gather_pairs(k, s))]
    ppermute x16 -> x21, starting transfers between devices: 32.4 us -> 43 us  [the longest x11 31.9 us: go(): sent[chain.half, t, s] = lax.ppermute(term, 'dp', chain.pairs(t, s))]
    ppermute x1, starting transfers between devices: 2.93 us -> 9.51 us  [body(): left_ends = lax.ppermute(left, 'dp', ends)]
    ppermute x1, waiting for transfers between devices: 0.01 us -> 4.58 us  [body(): left_ends = lax.ppermute(left, 'dp', ends)]
    ppermute x16 -> x21, waiting for transfers between devices: 39.7 us -> 42.5 us  [the longest x11 20 us: go(): sent[chain.half, t, s] = lax.ppermute(term, 'dp', chain.pairs(t, s))]
    pallas_call x18 -> x20, Pallas kernels: 20.2 us -> 18.7 us  [the longest x1 6.61 us: partial(): pl.pallas_call(functools.partial(partial_kernel, topk, width, block, gap,...]
  transfers between devices with their start and end apart: 30 -> 27, of which waited for: 10 -> 13; matrix products, arithmetic and copies ran while one was open for 0% -> 0% of each run, Pallas kernels for 12% -> 11%
where the time goes in v2:
time: 133 us; the launch traced here: 132 us
  starting transfers between devices  59.6 us (45%)
  waiting for transfers between devices  49.2 us (37%)
  Pallas kernels  20.6 us (15%)
  local copies, waits for them, and re-layouts  1.95 us (1%)
    ppermute x11, starting transfers between devices, go(): sent[chain.half, t, s] = lax.ppermute(term, 'dp', chain.pairs(t, s))  31.9 us
    ppermute x11, waiting for transfers between devices, go(): sent[chain.half, t, s] = lax.ppermute(term, 'dp', chain.pairs(t, s))  20 us
    ppermute x5, waiting for transfers between devices, hop_one(): return lax.ppermute(piece, 'dp', pairs) if pairs else piece  14.8 us
    ppermute x1, starting transfers between devices, body(): left_ends = lax.ppermute(left, 'dp', ends)  9.51 us
    ppermute x5, starting transfers between devices, hop(): lax.ppermute(pieces[1 - s], 'dp', gather_pairs(k, s))  7.04 us
    pallas_call x1, Pallas kernels, partial(): pl.pallas_call(functools.partial(partial_kernel, topk, width, block, gap,...  6.61 us
    pallas_call x9, Pallas kernels, product(): pl.pallas_call(functools.partial(product_kernel, chain, t, keys, root, bl...  6.18 us
    ppermute x2, waiting for transfers between devices, body(): lax.ppermute(tok, 'expert', [(i, i ^ 2 * m) for i in range(experts)])  6.03 us
  transfers between devices with their start and end apart: 27, of which 13 were waited for; matrix products, arithmetic and copies ran while one was open for 0% of the time, Pallas kernels for 11%

profile of v2, /device:TPU:0, one launch (start us, length us, event | category | flops | bytes accessed | tf_op | source)
XLA Modules:
  0.0 132.5 jit_solution(17434476862421441466)
XLA Ops:
  0.6 2.2 %tokens.1 = (bf16[1456,128]{1,0:T(8,128)(2,1)}, bf16[1200,256]{1,0:T(8,128)(2,1)}) custom-call(bf16[1440,128]{1,0:T(8,128)(2,1)} %bitcast.17, bf16[4,128]{1,0:T(4,128)(2,1)} %bitcast.21, s32[4,128]{1,0:T(4,128)} %bitcast.19, s32[4,128]{1,0:T(4,128)} %bitcast.20, bf16[960,240]{1,0:T(8,128)(2,1)} %bitcast.16, bf16[480,120]{1,0:T(8,128)(2,1)} %bitcast.18), custom_call_target="tpu_custom_call" | custom-call | tf_op jit(solution)/shard_map/tokens/pallas_call | solution.py:346
  2.9 3.1 %collective-permute-start.2 = (bf16[1200,256]{1,0:T(8,128)(2,1)}, bf16[1200,256]{1,0:T(8,128)(2,1)S(1)}, u32[]{:S(2)}, u32[]{:S(2)}) collective-permute-start(bf16[1200,256]{1,0:T(8,128)(2,1)} %get-tuple-element.78.refs_0_), channel_id=1, source_target_pairs={{0,8},{16,24},{8,0},{24,16},{1,9},{17,25},{9,1},{25,17},{2,10},{18... | collective-permute-start | bytes 1843208 | tf_op jit(solution)/shard_map/ppermute | solution.py:342
  6.0 0.7 collective-permute-start.3
  6.7 1.6 %collective-permute-start = (bf16[1456,128]{1,0:T(8,128)(2,1)}, bf16[1456,128]{1,0:T(8,128)(2,1)S(1)}, u32[]{:S(2)}, u32[]{:S(2)}) collective-permute-start(bf16[1456,128]{1,0:T(8,128)(2,1)} %get-tuple-element.71.refs_0_), channel_id=1, source_target_pairs={{0,2},{1,3},{2,0},{3,1},{4,6},{5,7},{6,4},{7,5},{8,10},{9,11},{10,... | collective-permute-start | bytes 1118216 | tf_op jit(solution)/shard_map/ppermute | solution.py:446
  8.2 1.5 %collective-permute-start.1 = (bf16[1456,128]{1,0:T(8,128)(2,1)}, bf16[1456,128]{1,0:T(8,128)(2,1)S(1)}, u32[]{:S(2)}, u32[]{:S(2)}) collective-permute-start(bf16[1456,128]{1,0:T(8,128)(2,1)} %get-tuple-element.71.refs_0_), channel_id=1, source_target_pairs={{0,4},{1,5},{2,6},{3,7},{4,0},{5,1},{6,2},{7,3},{8,12},{9,13},{10,... | collective-permute-start | bytes 1118216 | tf_op jit(solution)/shard_map/ppermute | solution.py:446
  9.8 1.0 copy-done.3
  10.8 0.9 copy-done.4
  12.3 4.8 %collective-permute-done.refs_1_ = bf16[1456,128]{1,0:T(8,128)(2,1)S(1)} collective-permute-done((bf16[1456,128]{1,0:T(8,128)(2,1)}, bf16[1456,128]{1,0:T(8,128)(2,1)S(1)}, u32[]{:S(2)}, u32[]{:S(2)}) %collective-permute-start) | collective-permute-done | bytes 372768 | tf_op jit(solution)/shard_map/ppermute | solution.py:446
  17.1 1.2 collective-permute-done.1.refs_2_
  18.3 1.7 %collective-permute-done.2.refs_0_ = bf16[1200,256]{1,0:T(8,128)(2,1)S(1)} collective-permute-done((bf16[1200,256]{1,0:T(8,128)(2,1)}, bf16[1200,256]{1,0:T(8,128)(2,1)S(1)}, u32[]{:S(2)}, u32[]{:S(2)}) %collective-permute-start.2) | collective-permute-done | bytes 614432 | tf_op jit(solution)/shard_map/ppermute | solution.py:342
  20.6 2.7 %collective-permute-start.7 = (bf16[1456,128]{1,0:T(8,128)(2,1)S(1)}, bf16[1456,128]{1,0:T(8,128)(2,1)S(1)}, u32[]{:S(2)}, u32[]{:S(2)}) collective-permute-start(bf16[1456,128]{1,0:T(8,128)(2,1)S(1)} %copy-done.2), channel_id=1, source_target_pairs={{0,6},{1,7},{2,4},{3,5},{4,2},{5,3},{6,0},{7,1},{8,14},{9,15},{10,... | collective-permute-start | bytes 1118216 | tf_op jit(solution)/shard_map/ppermute | solution.py:455
  23.3 1.3 collective-permute-start.4
  24.6 0.7 collective-permute-start.5
  25.3 9.5 %collective-permute-start.6 = (bf16[1200,256]{1,0:T(8,128)(2,1)S(1)}, bf16[1200,256]{1,0:T(8,128)(2,1)S(1)}, u32[]{:S(2)}, u32[]{:S(2)}) collective-permute-start(bf16[1200,256]{1,0:T(8,128)(2,1)S(1)} %pack_left.1.own_ref), channel_id=1, source_target_pairs={{0,8},{24,16},{1,9},{25,17},{2,10},{26,18},{3,11},{27,19},{4,12},{... | collective-permute-start | bytes 1843208 | tf_op jit(solution)/shard_map/ppermute | solution.py:465
  34.9 1.7 %collective-permute-done.9.refs_5_ = bf16[1456,128]{1,0:T(8,128)(2,1)S(1)} collective-permute-done((bf16[1456,128]{1,0:T(8,128)(2,1)S(1)}, bf16[1456,128]{1,0:T(8,128)(2,1)S(1)}, u32[]{:S(2)}, u32[]{:S(2)}) %collective-permute-start.9) | collective-permute-done | bytes 372768 | tf_op jit(solution)/shard_map/ppermute | solution.py:460
  36.6 6.6 %partial.1.partial_ref = bf16[1440,1536]{1,0:T(8,128)(2,1)S(1)} custom-call(bf16[8,1440,128]{2,1,0:T(8,128)(2,1)S(1)} %bitcast.13, bf16[1456,128]{1,0:T(8,128)(2,1)S(1)} %copy-done.2, bf16[1456,128]{1,0:T(8,128)(2,1)S(1)} %collective-permute-done.refs_1_, bf16[1456,128]{1,0:T(8,128)(2,1)S(1)} %collective-permute-done.1.refs_2_, ...), custom_call_target="tpu_custom_call" | custom-call | tf_op jit(solution)/shard_map/partial/pallas_call | solution.py:400
  43.4 4.6 %collective-permute-done.6.ends_ref = bf16[1200,256]{1,0:T(8,128)(2,1)S(1)} collective-permute-done((bf16[1200,256]{1,0:T(8,128)(2,1)S(1)}, bf16[1200,256]{1,0:T(8,128)(2,1)S(1)}, u32[]{:S(2)}, u32[]{:S(2)}) %collective-permute-start.6) | collective-permute-done | bytes 614432 | tf_op jit(solution)/shard_map/ppermute | solution.py:465
  47.9 1.3 collective-permute-start.13
  49.2 0.7 collective-permute-start.14
  49.9 0.7 product.9
  50.7 5.4 %collective-permute-start.12 = (bf16[1056,256]{1,0:T(8,128)(2,1)S(1)}, bf16[1056,256]{1,0:T(8,128)(2,1)S(1)}, u32[]{:S(2)}, u32[]{:S(2)}) collective-permute-start(bf16[1056,256]{1,0:T(8,128)(2,1)S(1)} %product.9), channel_id=1, source_target_pairs={{0,8},{24,16},{1,9},{25,17},{2,10},{26,18},{3,11},{27,19},{4,12},{... | collective-permute-start | bytes 1622024 | tf_op jit(solution)/shard_map/ppermute | solution.py:488
  56.1 1.3 collective-permute-start.10
  57.4 0.7 collective-permute-start.11
  58.1 8.2 %collective-permute-done.12.got_ref = bf16[1056,256]{1,0:T(8,128)(2,1)S(1)} collective-permute-done((bf16[1056,256]{1,0:T(8,128)(2,1)S(1)}, bf16[1056,256]{1,0:T(8,128)(2,1)S(1)}, u32[]{:S(2)}, u32[]{:S(2)}) %collective-permute-start.12) | collective-permute-done | bytes 540704 | tf_op jit(solution)/shard_map/ppermute | solution.py:488
  66.6 1.3 collective-permute-start.19
  67.9 0.8 product.12
  68.7 5.2 %collective-permute-start.18 = (bf16[1104,256]{1,0:T(8,128)(2,1)S(1)}, bf16[1104,256]{1,0:T(8,128)(2,1)S(1)}, u32[]{:S(2)}, u32[]{:S(2)}) collective-permute-start(bf16[1104,256]{1,0:T(8,128)(2,1)S(1)} %product.12), channel_id=1, source_target_pairs={{0,8},{24,16},{1,9},{25,17},{2,10},{26,18},{3,11},{27,19},{4,12},{... | collective-permute-start | bytes 1695752 | tf_op jit(solution)/shard_map/ppermute | solution.py:488
  73.9 0.7 product.10
  74.7 0.7 collective-permute-start.16
  75.4 4.4 %collective-permute-done.10.rest_ref = bf16[1200,256]{1,0:T(8,128)(2,1)S(1)} collective-permute-done((bf16[1200,256]{1,0:T(8,128)(2,1)S(1)}, bf16[1200,256]{1,0:T(8,128)(2,1)S(1)}, u32[]{:S(2)}, u32[]{:S(2)}) %collective-permute-start.10) | collective-permute-done | bytes 614432 | tf_op jit(solution)/shard_map/ppermute | solution.py:474
  79.8 5.9 %collective-permute-start.15 = (bf16[1056,256]{1,0:T(8,128)(2,1)S(1)}, bf16[1056,256]{1,0:T(8,128)(2,1)S(1)}, u32[]{:S(2)}, u32[]{:S(2)}) collective-permute-start(bf16[1056,256]{1,0:T(8,128)(2,1)S(1)} %get-tuple-element.87), channel_id=1, source_target_pairs={{0,8},{24,16},{1,9},{25,17},{2,10},{26,18},{3,11},{27,19},{4,12},{... | collective-permute-start | bytes 1622024 | tf_op jit(solution)/shard_map/ppermute | solution.py:488
  85.7 1.3 collective-permute-start.21
  87.0 0.8 product.13
  87.8 5.2 %collective-permute-done.19.refs_0_ = bf16[1200,256]{1,0:T(8,128)(2,1)S(1)} collective-permute-done((bf16[1200,256]{1,0:T(8,128)(2,1)S(1)}, bf16[1200,256]{1,0:T(8,128)(2,1)S(1)}, u32[]{:S(2)}, u32[]{:S(2)}) %collective-permute-start.19) | collective-permute-done | bytes 614432 | tf_op jit(solution)/shard_map/ppermute | solution.py:474
  93.6 3.1 %collective-permute-start.24 = (bf16[1104,256]{1,0:T(8,128)(2,1)S(1)}, bf16[1104,256]{1,0:T(8,128)(2,1)S(1)}, u32[]{:S(2)}, u32[]{:S(2)}) collective-permute-start(bf16[1104,256]{1,0:T(8,128)(2,1)S(1)} %get-tuple-element.120), channel_id=1, source_target_pairs={{0,8},{24,16},{1,9},{25,17},{2,10},{26,18},{3,11},{27,19},{4,12},{... | collective-permute-start | bytes 1695752 | tf_op jit(solution)/shard_map/ppermute | solution.py:488
  96.8 0.7 product.11
  97.6 0.7 collective-permute-start.23
  98.3 0.8 product.14
  99.1 5.2 %collective-permute-done.21.refs_2_.refs_3_ = bf16[1200,256]{1,0:T(8,128)(2,1)S(1)} collective-permute-done((bf16[1200,256]{1,0:T(8,128)(2,1)S(1)}, bf16[1200,256]{1,0:T(8,128)(2,1)S(1)}, u32[]{:S(2)}, u32[]{:S(2)}) %collective-permute-start.21) | collective-permute-done | bytes 614432 | tf_op jit(solution)/shard_map/ppermute | solution.py:474
  104.4 6.1 %collective-permute-start.22 = (bf16[1104,256]{1,0:T(8,128)(2,1)S(1)}, bf16[1104,256]{1,0:T(8,128)(2,1)S(1)}, u32[]{:S(2)}, u32[]{:S(2)}) collective-permute-start(bf16[1104,256]{1,0:T(8,128)(2,1)S(1)} %add.8), channel_id=1, source_target_pairs={{0,8},{8,0},{16,24},{24,16},{1,9},{9,1},{17,25},{25,17},{2,10},{10... | collective-permute-start | bytes 1695752 | tf_op jit(solution)/shard_map/ppermute | solution.py:488
  110.5 2.0 %collective-permute-start.17 = (bf16[1056,256]{1,0:T(8,128)(2,1)S(1)}, bf16[1056,256]{1,0:T(8,128)(2,1)S(1)}, u32[]{:S(2)}, u32[]{:S(2)}) collective-permute-start(bf16[1056,256]{1,0:T(8,128)(2,1)S(1)} %get-tuple-element.94), channel_id=1, source_target_pairs={{0,8},{24,16},{1,9},{25,17},{2,10},{26,18},{3,11},{27,19},{4,12},{... | collective-permute-start | bytes 1622024 | tf_op jit(solution)/shard_map/ppermute | solution.py:488
  112.7 0.8 collective-permute-start.26
  113.6 1.3 collective-permute-start.25
  114.9 0.7 product.16.refs_1_
  115.6 0.7 product.15.refs_0_
  116.3 1.3 %left.1 = (bf16[960,960]{1,0:T(8,128)(2,1)S(1)}, bf16[480,480]{1,0:T(8,128)(2,1)S(1)}) custom-call(bf16[1200,256]{1,0:T(8,128)(2,1)S(1)} %pack_left.1.own_ref, bf16[1200,256]{1,0:T(8,128)(2,1)S(1)} %collective-permute-done.6.ends_ref, bf16[1200,256]{1,0:T(8,128)(2,1)S(1)} %collective-permute-done.10.rest_ref, ...), custom_call_target="tpu_custom_call" | custom-call | tf_op jit(solution)/shard_map/left/pallas_call | solution.py:550
  117.7 11.6 %collective-permute-done.17.refs_3_ = bf16[1056,256]{1,0:T(8,128)(2,1)S(1)} collective-permute-done((bf16[1056,256]{1,0:T(8,128)(2,1)S(1)}, bf16[1056,256]{1,0:T(8,128)(2,1)S(1)}, u32[]{:S(2)}, u32[]{:S(2)}) %collective-permute-start.17) | collective-permute-done | bytes 540704 | tf_op jit(solution)/shard_map/ppermute | solution.py:488
  129.7 2.8 %final.1 = (f32[1440,240]{1,0:T(8,128)}, f32[1440,120]{1,0:T(8,128)}) custom-call(f32[1056,256]{1,0:T(8,128)S(1)} %get-tuple-element.116.refs_0_, f32[1104,256]{1,0:T(8,128)S(1)} %get-tuple-element.117.refs_1_, bf16[1056,256]{1,0:T(8,128)(2,1)S(1)} %collective-permute-done.25.refs_2_, bf16[1104,256]{1,0:T(8,128)(2,1)S(1)} %collective-permute-done.26.refs_3_, ...), custom_call_target="tpu_custom_call" | custom-call | tf_op jit(solution)/shard_map/final/pallas_call | solution.py:577
  (38 shorter events, 3.1 us)
Async XLA Ops:
  2.9 17.2 %copy-start.2 = (bf16[1456,128]{1,0:T(8,128)(2,1)S(1)}, bf16[1456,128]{1,0:T(8,128)(2,1)}, u32[]{:S(2)}) copy-start(bf16[1456,128]{1,0:T(8,128)(2,1)} %get-tuple-element.71.refs_0_) | copy-start | bytes 1118212
  2.9 17.2 %collective-permute-start.2 = (bf16[1200,256]{1,0:T(8,128)(2,1)}, bf16[1200,256]{1,0:T(8,128)(2,1)S(1)}, u32[]{:S(2)}, u32[]{:S(2)}) collective-permute-start(bf16[1200,256]{1,0:T(8,128)(2,1)} %get-tuple-element.78.refs_0_), channel_id=1, source_target_pairs={{0,8},{16,24},{8,0},{24,16},{1,9},{17,25},{9,1},{25,17},{2,10},{18... | collective-permute-start | bytes 1843208 | tf_op jit(solution)/shard_map/ppermute | solution.py:342
  6.0 14.1 %collective-permute-start.3 = (bf16[1200,256]{1,0:T(8,128)(2,1)}, bf16[1200,256]{1,0:T(8,128)(2,1)S(1)}, u32[]{:S(2)}, u32[]{:S(2)}) collective-permute-start(bf16[1200,256]{1,0:T(8,128)(2,1)} %get-tuple-element.78.refs_0_), channel_id=1, source_target_pairs={{8,16},{16,8},{9,17},{17,9},{10,18},{18,10},{11,19},{19,11},{12,20... | collective-permute-start | bytes 1843208 | tf_op jit(solution)/shard_map/ppermute | solution.py:342
  6.7 10.4 %collective-permute-start = (bf16[1456,128]{1,0:T(8,128)(2,1)}, bf16[1456,128]{1,0:T(8,128)(2,1)S(1)}, u32[]{:S(2)}, u32[]{:S(2)}) collective-permute-start(bf16[1456,128]{1,0:T(8,128)(2,1)} %get-tuple-element.71.refs_0_), channel_id=1, source_target_pairs={{0,2},{1,3},{2,0},{3,1},{4,6},{5,7},{6,4},{7,5},{8,10},{9,11},{10,... | collective-permute-start | bytes 1118216 | tf_op jit(solution)/shard_map/ppermute | solution.py:446
  8.2 10.1 %collective-permute-start.1 = (bf16[1456,128]{1,0:T(8,128)(2,1)}, bf16[1456,128]{1,0:T(8,128)(2,1)S(1)}, u32[]{:S(2)}, u32[]{:S(2)}) collective-permute-start(bf16[1456,128]{1,0:T(8,128)(2,1)} %get-tuple-element.71.refs_0_), channel_id=1, source_target_pairs={{0,4},{1,5},{2,6},{3,7},{4,0},{5,1},{6,2},{7,3},{8,12},{9,13},{10,... | collective-permute-start | bytes 1118216 | tf_op jit(solution)/shard_map/ppermute | solution.py:446
  9.8 1.0 copy-start.3
  10.8 0.9 copy-start.4
  11.7 24.9 %copy-start = (bf16[1,1,8,128,1440]{3,4,2,1,0:T(8,128)(2,1)S(1)}, bf16[1,1,8,128,1440]{3,4,2,1,0:T(8,128)(2,1)}, u32[]{:S(2)}) copy-start(bf16[1,1,8,128,1440]{3,4,2,1,0:T(8,128)(2,1)} %param.13) | copy-start | bytes 8847364
  20.6 16.0 %collective-permute-start.8 = (bf16[3,1456,128]{2,1,0:T(8,128)(2,1)S(1)}, bf16[3,1456,128]{2,1,0:T(8,128)(2,1)S(1)}, u32[]{:S(2)}, u32[]{:S(2)}) collective-permute-start(bf16[3,1456,128]{2,1,0:T(8,128)(2,1)S(1)} %collect.1), channel_id=1, source_target_pairs={{0,1},{1,0},{2,3},{3,2},{4,5},{5,4},{6,7},{7,6},{8,9},{9,8},{10,11... | collective-permute-start | bytes 3354632 | tf_op jit(solution)/shard_map/ppermute | solution.py:460
  20.6 14.2 %collective-permute-start.7 = (bf16[1456,128]{1,0:T(8,128)(2,1)S(1)}, bf16[1456,128]{1,0:T(8,128)(2,1)S(1)}, u32[]{:S(2)}, u32[]{:S(2)}) collective-permute-start(bf16[1456,128]{1,0:T(8,128)(2,1)S(1)} %copy-done.2), channel_id=1, source_target_pairs={{0,6},{1,7},{2,4},{3,5},{4,2},{5,3},{6,0},{7,1},{8,14},{9,15},{10,... | collective-permute-start | bytes 1118216 | tf_op jit(solution)/shard_map/ppermute | solution.py:455
  23.3 20.0 %collective-permute-start.4 = (bf16[1200,256]{1,0:T(8,128)(2,1)S(1)}, bf16[1200,256]{1,0:T(8,128)(2,1)S(1)}, u32[]{:S(2)}, u32[]{:S(2)}) collective-permute-start(bf16[1200,256]{1,0:T(8,128)(2,1)S(1)} %collective-permute-done.3.refs_0_.refs_1_), channel_id=1, source_target_pairs={{16,24},{8,0},{17,25},{9,1},{18,26},{10,2},{19,27},{11,3},{20,28},... | collective-permute-start | bytes 1843208 | tf_op jit(solution)/shard_map/ppermute | solution.py:342
  24.6 18.8 %collective-permute-start.5 = (bf16[1200,256]{1,0:T(8,128)(2,1)S(1)}, bf16[1200,256]{1,0:T(8,128)(2,1)S(1)}, u32[]{:S(2)}, u32[]{:S(2)}) collective-permute-start(bf16[1200,256]{1,0:T(8,128)(2,1)S(1)} %collective-permute-done.2.refs_0_), channel_id=1, source_target_pairs={{8,16},{16,8},{9,17},{17,9},{10,18},{18,10},{11,19},{19,11},{12,20... | collective-permute-start | bytes 1843208 | tf_op jit(solution)/shard_map/ppermute | solution.py:342
  25.3 22.6 %collective-permute-start.6 = (bf16[1200,256]{1,0:T(8,128)(2,1)S(1)}, bf16[1200,256]{1,0:T(8,128)(2,1)S(1)}, u32[]{:S(2)}, u32[]{:S(2)}) collective-permute-start(bf16[1200,256]{1,0:T(8,128)(2,1)S(1)} %pack_left.1.own_ref), channel_id=1, source_target_pairs={{0,8},{24,16},{1,9},{25,17},{2,10},{26,18},{3,11},{27,19},{4,12},{... | collective-permute-start | bytes 1843208 | tf_op jit(solution)/shard_map/ppermute | solution.py:465
  34.9 1.8 %collective-permute-start.9 = (bf16[1456,128]{1,0:T(8,128)(2,1)S(1)}, bf16[1456,128]{1,0:T(8,128)(2,1)S(1)}, u32[]{:S(2)}, u32[]{:S(2)}) collective-permute-start(bf16[1456,128]{1,0:T(8,128)(2,1)S(1)} %collective-permute-done.7.refs_3_), channel_id=1, source_target_pairs={{0,1},{1,0},{2,3},{3,2},{4,5},{5,4},{6,7},{7,6},{8,9},{9,8},{10,11... | collective-permute-start | bytes 1118216 | tf_op jit(solution)/shard_map/ppermute | solution.py:460
  47.9 18.7 %collective-permute-start.13 = (bf16[1200,256]{1,0:T(8,128)(2,1)S(1)}, bf16[1200,256]{1,0:T(8,128)(2,1)S(1)}, u32[]{:S(2)}, u32[]{:S(2)}) collective-permute-start(bf16[1200,256]{1,0:T(8,128)(2,1)S(1)} %collective-permute-done.5.refs_1_), channel_id=1, source_target_pairs={{16,24},{8,0},{17,25},{9,1},{18,26},{10,2},{19,27},{11,3},{20,28},... | collective-permute-start | bytes 1843208 | tf_op jit(solution)/shard_map/ppermute | solution.py:342
  49.2 17.4 %collective-permute-start.14 = (bf16[1200,256]{1,0:T(8,128)(2,1)S(1)}, bf16[1200,256]{1,0:T(8,128)(2,1)S(1)}, u32[]{:S(2)}, u32[]{:S(2)}) collective-permute-start(bf16[1200,256]{1,0:T(8,128)(2,1)S(1)} %pack_left.1.own_ref), channel_id=1, source_target_pairs={{8,16},{16,8},{9,17},{17,9},{10,18},{18,10},{11,19},{19,11},{12,20... | collective-permute-start | bytes 1843208 | tf_op jit(solution)/shard_map/ppermute | solution.py:474
  50.7 15.6 %collective-permute-start.12 = (bf16[1056,256]{1,0:T(8,128)(2,1)S(1)}, bf16[1056,256]{1,0:T(8,128)(2,1)S(1)}, u32[]{:S(2)}, u32[]{:S(2)}) collective-permute-start(bf16[1056,256]{1,0:T(8,128)(2,1)S(1)} %product.9), channel_id=1, source_target_pairs={{0,8},{24,16},{1,9},{25,17},{2,10},{26,18},{3,11},{27,19},{4,12},{... | collective-permute-start | bytes 1622024 | tf_op jit(solution)/shard_map/ppermute | solution.py:488
  56.1 23.7 %collective-permute-start.10 = (bf16[1200,256]{1,0:T(8,128)(2,1)S(1)}, bf16[1200,256]{1,0:T(8,128)(2,1)S(1)}, u32[]{:S(2)}, u32[]{:S(2)}) collective-permute-start(bf16[1200,256]{1,0:T(8,128)(2,1)S(1)} %pack_left.1.own_ref), channel_id=1, source_target_pairs={{16,24},{8,0},{17,25},{9,1},{18,26},{10,2},{19,27},{11,3},{20,28},... | collective-permute-start | bytes 1843208 | tf_op jit(solution)/shard_map/ppermute | solution.py:474
  57.4 22.4 %collective-permute-start.11 = (bf16[1200,256]{1,0:T(8,128)(2,1)S(1)}, bf16[1200,256]{1,0:T(8,128)(2,1)S(1)}, u32[]{:S(2)}, u32[]{:S(2)}) collective-permute-start(bf16[1200,256]{1,0:T(8,128)(2,1)S(1)} %collective-permute-done.6.ends_ref), channel_id=1, source_target_pairs={{8,16},{16,8},{9,17},{17,9},{10,18},{18,10},{11,19},{19,11},{12,20... | collective-permute-start | bytes 1843208 | tf_op jit(solution)/shard_map/ppermute | solution.py:474
  66.6 26.3 %collective-permute-start.19 = (bf16[1200,256]{1,0:T(8,128)(2,1)S(1)}, bf16[1200,256]{1,0:T(8,128)(2,1)S(1)}, u32[]{:S(2)}, u32[]{:S(2)}) collective-permute-start(bf16[1200,256]{1,0:T(8,128)(2,1)S(1)} %collective-permute-done.14.odd_ref), channel_id=1, source_target_pairs={{16,24},{8,0},{17,25},{9,1},{18,26},{10,2},{19,27},{11,3},{20,28},... | collective-permute-start | bytes 1843208 | tf_op jit(solution)/shard_map/ppermute | solution.py:474
  68.7 19.1 %collective-permute-start.18 = (bf16[1104,256]{1,0:T(8,128)(2,1)S(1)}, bf16[1104,256]{1,0:T(8,128)(2,1)S(1)}, u32[]{:S(2)}, u32[]{:S(2)}) collective-permute-start(bf16[1104,256]{1,0:T(8,128)(2,1)S(1)} %product.12), channel_id=1, source_target_pairs={{0,8},{24,16},{1,9},{25,17},{2,10},{26,18},{3,11},{27,19},{4,12},{... | collective-permute-start | bytes 1695752 | tf_op jit(solution)/shard_map/ppermute | solution.py:488
  74.7 22.9 %collective-permute-start.16 = (bf16[1056,256]{1,0:T(8,128)(2,1)S(1)}, bf16[1056,256]{1,0:T(8,128)(2,1)S(1)}, u32[]{:S(2)}, u32[]{:S(2)}) collective-permute-start(bf16[1056,256]{1,0:T(8,128)(2,1)S(1)} %add.6), channel_id=1, source_target_pairs={{8,16},{16,8},{9,17},{17,9},{10,18},{18,10},{11,19},{19,11},{12,20... | collective-permute-start | bytes 1622024 | tf_op jit(solution)/shard_map/ppermute | solution.py:488
  79.8 17.8 %collective-permute-start.15 = (bf16[1056,256]{1,0:T(8,128)(2,1)S(1)}, bf16[1056,256]{1,0:T(8,128)(2,1)S(1)}, u32[]{:S(2)}, u32[]{:S(2)}) collective-permute-start(bf16[1056,256]{1,0:T(8,128)(2,1)S(1)} %get-tuple-element.87), channel_id=1, source_target_pairs={{0,8},{24,16},{1,9},{25,17},{2,10},{26,18},{3,11},{27,19},{4,12},{... | collective-permute-start | bytes 1622024 | tf_op jit(solution)/shard_map/ppermute | solution.py:488
  85.7 18.5 %collective-permute-start.21 = (bf16[1200,256]{1,0:T(8,128)(2,1)S(1)}, bf16[1200,256]{1,0:T(8,128)(2,1)S(1)}, u32[]{:S(2)}, u32[]{:S(2)}) collective-permute-start(bf16[1200,256]{1,0:T(8,128)(2,1)S(1)} %collective-permute-done.11.refs_1_), channel_id=1, source_target_pairs={{16,24},{8,0},{17,25},{9,1},{18,26},{10,2},{19,27},{11,3},{20,28},... | collective-permute-start | bytes 1843208 | tf_op jit(solution)/shard_map/ppermute | solution.py:474
  93.0 11.3 %collective-permute-start.20 = (bf16[1104,256]{1,0:T(8,128)(2,1)S(1)}, bf16[1104,256]{1,0:T(8,128)(2,1)S(1)}, u32[]{:S(2)}, u32[]{:S(2)}) collective-permute-start(bf16[1104,256]{1,0:T(8,128)(2,1)S(1)} %add.7), channel_id=1, source_target_pairs={{8,16},{16,8},{9,17},{17,9},{10,18},{18,10},{11,19},{19,11},{12,20... | collective-permute-start | bytes 1695752 | tf_op jit(solution)/shard_map/ppermute | solution.py:488
  93.6 19.0 %collective-permute-start.24 = (bf16[1104,256]{1,0:T(8,128)(2,1)S(1)}, bf16[1104,256]{1,0:T(8,128)(2,1)S(1)}, u32[]{:S(2)}, u32[]{:S(2)}) collective-permute-start(bf16[1104,256]{1,0:T(8,128)(2,1)S(1)} %get-tuple-element.120), channel_id=1, source_target_pairs={{0,8},{24,16},{1,9},{25,17},{2,10},{26,18},{3,11},{27,19},{4,12},{... | collective-permute-start | bytes 1695752 | tf_op jit(solution)/shard_map/ppermute | solution.py:488
  97.6 15.1 %collective-permute-start.23 = (bf16[1056,256]{1,0:T(8,128)(2,1)S(1)}, bf16[1056,256]{1,0:T(8,128)(2,1)S(1)}, u32[]{:S(2)}, u32[]{:S(2)}) collective-permute-start(bf16[1056,256]{1,0:T(8,128)(2,1)S(1)} %add.9), channel_id=1, source_target_pairs={{8,16},{16,8},{9,17},{17,9},{10,18},{18,10},{11,19},{19,11},{12,20... | collective-permute-start | bytes 1622024 | tf_op jit(solution)/shard_map/ppermute | solution.py:488
  104.4 25.0 %collective-permute-start.22 = (bf16[1104,256]{1,0:T(8,128)(2,1)S(1)}, bf16[1104,256]{1,0:T(8,128)(2,1)S(1)}, u32[]{:S(2)}, u32[]{:S(2)}) collective-permute-start(bf16[1104,256]{1,0:T(8,128)(2,1)S(1)} %add.8), channel_id=1, source_target_pairs={{0,8},{8,0},{16,24},{24,16},{1,9},{9,1},{17,25},{25,17},{2,10},{10... | collective-permute-start | bytes 1695752 | tf_op jit(solution)/shard_map/ppermute | solution.py:488
  110.5 18.9 %collective-permute-start.17 = (bf16[1056,256]{1,0:T(8,128)(2,1)S(1)}, bf16[1056,256]{1,0:T(8,128)(2,1)S(1)}, u32[]{:S(2)}, u32[]{:S(2)}) collective-permute-start(bf16[1056,256]{1,0:T(8,128)(2,1)S(1)} %get-tuple-element.94), channel_id=1, source_target_pairs={{0,8},{24,16},{1,9},{25,17},{2,10},{26,18},{3,11},{27,19},{4,12},{... | collective-permute-start | bytes 1622024 | tf_op jit(solution)/shard_map/ppermute | solution.py:488
  112.6 2.2 %copy-start.1 = (bf16[1200,256]{1,0:T(8,128)(2,1)S(1)}, bf16[1200,256]{1,0:T(8,128)(2,1)}, u32[]{:S(2)}) copy-start(bf16[1200,256]{1,0:T(8,128)(2,1)} %get-tuple-element.78.refs_0_) | copy-start | bytes 1843204
  112.7 17.0 %collective-permute-start.26 = (bf16[1104,256]{1,0:T(8,128)(2,1)S(1)}, bf16[1104,256]{1,0:T(8,128)(2,1)S(1)}, u32[]{:S(2)}, u32[]{:S(2)}) collective-permute-start(bf16[1104,256]{1,0:T(8,128)(2,1)S(1)} %add.11), channel_id=1, source_target_pairs={{8,16},{16,8},{9,17},{17,9},{10,18},{18,10},{11,19},{19,11},{12,20... | collective-permute-start | bytes 1695752 | tf_op jit(solution)/shard_map/ppermute | solution.py:488
  113.6 16.1 %collective-permute-start.25 = (bf16[1056,256]{1,0:T(8,128)(2,1)S(1)}, bf16[1056,256]{1,0:T(8,128)(2,1)S(1)}, u32[]{:S(2)}, u32[]{:S(2)}) collective-permute-start(bf16[1056,256]{1,0:T(8,128)(2,1)S(1)} %add.10), channel_id=1, source_target_pairs={{8,0},{16,24},{9,1},{17,25},{10,2},{18,26},{11,3},{19,27},{12,4},{... | collective-permute-start | bytes 1622024 | tf_op jit(solution)/shard_map/ppermute | solution.py:488

commit v3 on v2

--- a/solution.py
+++ b/solution.py
@@ -325,13 +325,11 @@
     gap = round_up(block, LANES)
     span = gap + round_up(rest, LANES)
     root = Fold(block, rest, wide, narrow)
-    cut = ffn // 64 * 32
+    cut = ffn - ffn // 64 * 32
     folds = [Fold(rows, rows, wide, narrow) for rows in (cut, ffn - cut)]
     sooner = [n - 2, n - 1] if n > 2 else [1]
-    chains = [
-        Chain(n, 0, sooner + list(range(n - 3, 0, -1)), 0, folds[0]),
-        Chain(n, 1, list(range(n - 1, 0, -1)), cut, folds[1]),
-    ]
+    sooner += list(range(n - 3, 0, -1))
+    chains = [Chain(n, 0, sooner, 0, folds[0]), Chain(n, 1, sooner, cut, folds[1])]
 
     def gather_pairs(k, s):
         up = [(i, i + 1) for i in range(s, n - 1, 2) if i >= k - 1]
@@ -487,62 +485,64 @@
             term = add(chain, t, s, term, sent[chain.half, t - 1, 1 - s])
         sent[chain.half, t, s] = lax.ppermute(term, "dp", chain.pairs(t, s))
 
-    make(one, 1)
-    for s in one.sets(1):
-        go(one, 1, s)
     for k in range(max(2, n - 1), n):
         got.append(hop(k, got[-1]))
+    for chain in chains:
+        make(chain, 1)
+        for s in chain.sets(1):
+            go(chain, 1, s)
     left_odd = hop_one(gather_pairs(1, 1), left)
-    left_rest = hop_one(others, left)
     inner = {target for _, target in ends}
     if all(pair[0] in inner for pair in gather_pairs(2, 1)):
         left_even = left_ends
     else:
+        left_rest = hop_one(others, left)
         z = lax.axis_index("dp")
         left_even = jnp.where((z == 1) | (z == n - 2), left_ends, left_rest)
     second = [None, hop_one(gather_pairs(2, 1), left_even)]
     own = [product(chain, 0, value, got)[0] for chain in chains]
 
-    got, value, left_odd = wait([(0, 1, s) for s in one.sets(1)], (), (got, value, left_odd))
-    make(two, 1)
+    got, value, left, left_odd = wait([(0, 1, s) for s in one.sets(1)], (), (got, value, left, left_odd))
     make(one, 2)
-    for s in two.sets(1):
-        go(two, 1, s)
     if n == 4:
+        go(one, 2, 0)
         go(one, 2, 1)
+        left_rest = hop_one(others, left)
+        make(two, 2)
+        second[1], terms[1, 2] = wait([(1, 1, 0)], (), (second[1], terms[1, 2]))
+        go(two, 2, 0)
         second[0] = hop_one(gather_pairs(2, 0), left_odd)
-        left_rest, second[1], terms[0, 2] = wait([], (), (left_rest, second[1], terms[0, 2]))
-        go(one, 2, 0)
+        make(one, 3)
+        left_rest, terms[0, 3] = wait([(0, 2, 0)], (), (left_rest, terms[0, 3]))
+        go(one, 3, 1)
         third = hop_one(gather_pairs(3, 0), second[1])
-        make(two, 2)
-        second[0], terms[1, 2] = wait([(1, 1, 0)], (), (second[0], terms[1, 2]))
-        go(two, 2, 1)
-        go(two, 2, 0)
-        make(one, 3)
-        terms[0, 3] = wait([(0, 2, 0), (0, 2, 1)], (), terms[0, 3])
-        go(one, 3, 1)
+        terms[0, 3] = wait([(0, 2, 1)], (), terms[0, 3])
         go(one, 3, 0)
         make(two, 3)
-        third, terms[1, 3] = wait([(1, 2, 1)], (), (third, terms[1, 3]))
+        second[0], terms[1, 3], terms[1, 2] = wait([(1, 2, 0)], (), (second[0], terms[1, 3], terms[1, 2]))
+        go(two, 3, 1)
+        go(two, 2, 1)
+        make(one, 4)
+        terms[0, 4] = wait([(0, 3, 1)], (), terms[0, 4])
+        go(one, 4, 0)
+        third, terms[1, 3] = wait([], (), (third, terms[1, 3]))
         go(two, 3, 0)
-        make(one, 4)
-        terms[0, 4], terms[1, 3] = wait([(0, 3, 1), (1, 2, 0)], (), (terms[0, 4], terms[1, 3]))
-        go(one, 4, 0)
-        go(two, 3, 1)
+        make(two, 4)
+        terms[1, 4] = wait([(1, 3, 1), (0, 3, 0)], (), terms[1, 4])
+        go(two, 4, 0)
         lefts = [[left, left], [left_even, left_odd], second, [third, third]]
     else:
-        for s in one.sets(2):
-            go(one, 2, s)
+        left_rest = hop_one(others, left)
         second[0] = hop_one(gather_pairs(2, 0), left_odd)
         lefts = [[left, left], [left_even, left_odd], second]
-        for t in range(2, max(chain.steps for chain in chains) + 1):
+        for t in range(2, one.steps + 1):
             for chain in chains:
-                if t <= chain.steps and (chain.half, t) != (0, 2):
+                if (chain.half, t) != (0, 2):
                     make(chain, t)
-                    before = [(chain.half, t - 1, s) for s in chain.sets(t - 1)]
-                    terms[chain.half, t] = wait(before, (), terms[chain.half, t])
-                    for s in chain.sets(t):
-                        go(chain, t, s)
+                before = [(chain.half, t - 1, s) for s in chain.sets(t - 1)]
+                terms[chain.half, t] = wait(before, (), terms[chain.half, t])
+                for s in chain.sets(t):
+                    go(chain, t, s)
             if 2 < t < n:
                 lefts.append(hop(t, wait([], (), lefts[-1])))
 
@@ -561,7 +561,7 @@
     )(*left_inputs)
 
     keys = sorted({(chain.half, t, s) for chain in chains for here in range(n) for t, s in chain.arrivals(here)})
-    last = [(0, one.steps, s) for s in one.sets(one.steps)] + [(1, two.steps, 1)]
+    last = [(1, two.steps, s) for s in two.sets(two.steps)]
     early = [key for key in keys if key not in last]
     last = [key for key in keys if key in last]
     own = wait(early, (left_w, left_n), own)

time: 133 us -> 137 us (1.030)
  starting transfers between devices: 59.6 us -> 72.5 us
  waiting for transfers between devices: 49.2 us -> 39.8 us
    ppermute x5, waiting for transfers between devices: 14.8 us -> 1.07 us  [hop_one(): return lax.ppermute(piece, 'dp', pairs) if pairs else piece]
    ppermute x11 -> x12, starting transfers between devices: 31.9 us -> 44.8 us  [go(): sent[chain.half, t, s] = lax.ppermute(term, 'dp', chain.pairs(t, s))]
    ppermute x11 -> x12, waiting for transfers between devices: 20 us -> 24.6 us  [go(): sent[chain.half, t, s] = lax.ppermute(term, 'dp', chain.pairs(t, s))]
    pallas_call x9 -> x10, Pallas kernels: 6.18 us -> 6.19 us  [product(): pl.pallas_call(functools.partial(product_kernel, chain, t, keys, root, bl...]
  transfers between devices with their start and end apart: 27 -> 28, of which waited for: 13 -> 13; matrix products, arithmetic and copies ran while one was open for 0% -> 0% of each run, Pallas kernels for 11% -> 11%
where the time goes in v3:
time: 137 us; the launch traced here: 136 us
  starting transfers between devices  72.5 us (53%)
  waiting for transfers between devices  39.8 us (29%)
  Pallas kernels  20.6 us (15%)
  local copies, waits for them, and re-layouts  1.95 us (1%)
    ppermute x12, starting transfers between devices, go(): sent[chain.half, t, s] = lax.ppermute(term, 'dp', chain.pairs(t, s))  44.8 us
    ppermute x12, waiting for transfers between devices, go(): sent[chain.half, t, s] = lax.ppermute(term, 'dp', chain.pairs(t, s))  24.6 us
    ppermute x1, starting transfers between devices, body(): left_ends = lax.ppermute(left, 'dp', ends)  9.51 us
    ppermute x5, starting transfers between devices, hop(): lax.ppermute(pieces[1 - s], 'dp', gather_pairs(k, s))  7.04 us
    pallas_call x1, Pallas kernels, partial(): pl.pallas_call(functools.partial(partial_kernel, topk, width, block, gap,...  6.61 us
    pallas_call x10, Pallas kernels, product(): pl.pallas_call(functools.partial(product_kernel, chain, t, keys, root, bl...  6.19 us
    ppermute x2, waiting for transfers between devices, body(): lax.ppermute(tok, 'expert', [(i, i ^ 2 * m) for i in range(experts)])  6.03 us
    ppermute x5, starting transfers between devices, hop_one(): return lax.ppermute(piece, 'dp', pairs) if pairs else piece  5.25 us
  transfers between devices with their start and end apart: 28, of which 13 were waited for; matrix products, arithmetic and copies ran while one was open for 0% of the time, Pallas kernels for 11%

profile of v3, /device:TPU:0, one launch (start us, length us, event | category | flops | bytes accessed | tf_op | source)
XLA Modules:
  0.0 135.9 jit_solution(16891893753844374746)
XLA Ops:
  0.6 2.2 %tokens.1 = (bf16[1456,128]{1,0:T(8,128)(2,1)}, bf16[1200,256]{1,0:T(8,128)(2,1)}) custom-call(bf16[1440,128]{1,0:T(8,128)(2,1)} %bitcast.17, bf16[4,128]{1,0:T(4,128)(2,1)} %bitcast.21, s32[4,128]{1,0:T(4,128)} %bitcast.19, s32[4,128]{1,0:T(4,128)} %bitcast.20, bf16[960,240]{1,0:T(8,128)(2,1)} %bitcast.16, bf16[480,120]{1,0:T(8,128)(2,1)} %bitcast.18), custom_call_target="tpu_custom_call" | custom-call | tf_op jit(solution)/shard_map/tokens/pallas_call | solution.py:344
  2.9 3.1 %collective-permute-start.2 = (bf16[1200,256]{1,0:T(8,128)(2,1)}, bf16[1200,256]{1,0:T(8,128)(2,1)S(1)}, u32[]{:S(2)}, u32[]{:S(2)}) collective-permute-start(bf16[1200,256]{1,0:T(8,128)(2,1)} %get-tuple-element.81.refs_0_), channel_id=1, source_target_pairs={{0,8},{16,24},{8,0},{24,16},{1,9},{17,25},{9,1},{25,17},{2,10},{18... | collective-permute-start | bytes 1843208 | tf_op jit(solution)/shard_map/ppermute | solution.py:340
  6.7 1.6 %collective-permute-start = (bf16[1456,128]{1,0:T(8,128)(2,1)}, bf16[1456,128]{1,0:T(8,128)(2,1)S(1)}, u32[]{:S(2)}, u32[]{:S(2)}) collective-permute-start(bf16[1456,128]{1,0:T(8,128)(2,1)} %get-tuple-element.76.refs_0_), channel_id=1, source_target_pairs={{0,2},{1,3},{2,0},{3,1},{4,6},{5,7},{6,4},{7,5},{8,10},{9,11},{10,... | collective-permute-start | bytes 1118216 | tf_op jit(solution)/shard_map/ppermute | solution.py:444
  8.2 1.5 %collective-permute-start.1 = (bf16[1456,128]{1,0:T(8,128)(2,1)}, bf16[1456,128]{1,0:T(8,128)(2,1)S(1)}, u32[]{:S(2)}, u32[]{:S(2)}) collective-permute-start(bf16[1456,128]{1,0:T(8,128)(2,1)} %get-tuple-element.76.refs_0_), channel_id=1, source_target_pairs={{0,4},{1,5},{2,6},{3,7},{4,0},{5,1},{6,2},{7,3},{8,12},{9,13},{10,... | collective-permute-start | bytes 1118216 | tf_op jit(solution)/shard_map/ppermute | solution.py:444
  9.8 1.0 copy-done.3
  10.8 0.9 copy-done.4
  12.3 4.8 %collective-permute-done.refs_1_ = bf16[1456,128]{1,0:T(8,128)(2,1)S(1)} collective-permute-done((bf16[1456,128]{1,0:T(8,128)(2,1)}, bf16[1456,128]{1,0:T(8,128)(2,1)S(1)}, u32[]{:S(2)}, u32[]{:S(2)}) %collective-permute-start) | collective-permute-done | bytes 372768 | tf_op jit(solution)/shard_map/ppermute | solution.py:444
  17.1 1.2 collective-permute-done.1.refs_2_
  18.3 1.7 %collective-permute-done.2.refs_0_ = bf16[1200,256]{1,0:T(8,128)(2,1)S(1)} collective-permute-done((bf16[1200,256]{1,0:T(8,128)(2,1)}, bf16[1200,256]{1,0:T(8,128)(2,1)S(1)}, u32[]{:S(2)}, u32[]{:S(2)}) %collective-permute-start.2) | collective-permute-done | bytes 614432 | tf_op jit(solution)/shard_map/ppermute | solution.py:340
  20.6 2.7 %collective-permute-start.7 = (bf16[1456,128]{1,0:T(8,128)(2,1)S(1)}, bf16[1456,128]{1,0:T(8,128)(2,1)S(1)}, u32[]{:S(2)}, u32[]{:S(2)}) collective-permute-start(bf16[1456,128]{1,0:T(8,128)(2,1)S(1)} %copy-done.2), channel_id=1, source_target_pairs={{0,6},{1,7},{2,4},{3,5},{4,2},{5,3},{6,0},{7,1},{8,14},{9,15},{10,... | collective-permute-start | bytes 1118216 | tf_op jit(solution)/shard_map/ppermute | solution.py:453
  23.3 1.3 collective-permute-start.4
  24.6 0.7 collective-permute-start.5
  25.3 9.5 %collective-permute-start.6 = (bf16[1200,256]{1,0:T(8,128)(2,1)S(1)}, bf16[1200,256]{1,0:T(8,128)(2,1)S(1)}, u32[]{:S(2)}, u32[]{:S(2)}) collective-permute-start(bf16[1200,256]{1,0:T(8,128)(2,1)S(1)} %pack_left.1.own_ref), channel_id=1, source_target_pairs={{0,8},{24,16},{1,9},{25,17},{2,10},{26,18},{3,11},{27,19},{4,12},{... | collective-permute-start | bytes 1843208 | tf_op jit(solution)/shard_map/ppermute | solution.py:463
  34.9 1.7 %collective-permute-done.9.refs_5_ = bf16[1456,128]{1,0:T(8,128)(2,1)S(1)} collective-permute-done((bf16[1456,128]{1,0:T(8,128)(2,1)S(1)}, bf16[1456,128]{1,0:T(8,128)(2,1)S(1)}, u32[]{:S(2)}, u32[]{:S(2)}) %collective-permute-start.9) | collective-permute-done | bytes 372768 | tf_op jit(solution)/shard_map/ppermute | solution.py:458
  36.6 6.6 %partial.1.partial_ref = bf16[1440,1536]{1,0:T(8,128)(2,1)S(1)} custom-call(bf16[8,1440,128]{2,1,0:T(8,128)(2,1)S(1)} %bitcast.13, bf16[1456,128]{1,0:T(8,128)(2,1)S(1)} %copy-done.2, bf16[1456,128]{1,0:T(8,128)(2,1)S(1)} %collective-permute-done.refs_1_, bf16[1456,128]{1,0:T(8,128)(2,1)S(1)} %collective-permute-done.1.refs_2_, ...), custom_call_target="tpu_custom_call" | custom-call | tf_op jit(solution)/shard_map/partial/pallas_call | solution.py:398
  43.4 4.6 %collective-permute-done.6.ends_ref = bf16[1200,256]{1,0:T(8,128)(2,1)S(1)} collective-permute-done((bf16[1200,256]{1,0:T(8,128)(2,1)S(1)}, bf16[1200,256]{1,0:T(8,128)(2,1)S(1)}, u32[]{:S(2)}, u32[]{:S(2)}) %collective-permute-start.6) | collective-permute-done | bytes 614432 | tf_op jit(solution)/shard_map/ppermute | solution.py:463
  47.9 1.3 collective-permute-start.11
  49.2 0.7 collective-permute-start.12
  49.9 0.8 product.10
  50.7 5.4 %collective-permute-start.10 = (bf16[1104,256]{1,0:T(8,128)(2,1)S(1)}, bf16[1104,256]{1,0:T(8,128)(2,1)S(1)}, u32[]{:S(2)}, u32[]{:S(2)}) collective-permute-start(bf16[1104,256]{1,0:T(8,128)(2,1)S(1)} %product.10), channel_id=1, source_target_pairs={{0,8},{24,16},{1,9},{25,17},{2,10},{26,18},{3,11},{27,19},{4,12},{... | collective-permute-start | bytes 1695752 | tf_op jit(solution)/shard_map/ppermute | solution.py:486
  56.1 0.7 collective-permute-start.17
  56.8 0.7 product.13
  57.5 3.5 %collective-permute-start.16 = (bf16[1056,256]{1,0:T(8,128)(2,1)S(1)}, bf16[1056,256]{1,0:T(8,128)(2,1)S(1)}, u32[]{:S(2)}, u32[]{:S(2)}) collective-permute-start(bf16[1056,256]{1,0:T(8,128)(2,1)S(1)} %product.13), channel_id=1, source_target_pairs={{0,8},{24,16},{1,9},{25,17},{2,10},{26,18},{3,11},{27,19},{4,12},{... | collective-permute-start | bytes 1622024 | tf_op jit(solution)/shard_map/ppermute | solution.py:486
  61.1 8.2 %collective-permute-done.10.got_ref = bf16[1104,256]{1,0:T(8,128)(2,1)S(1)} collective-permute-done((bf16[1104,256]{1,0:T(8,128)(2,1)S(1)}, bf16[1104,256]{1,0:T(8,128)(2,1)S(1)}, u32[]{:S(2)}, u32[]{:S(2)}) %collective-permute-start.10) | collective-permute-done | bytes 565280 | tf_op jit(solution)/shard_map/ppermute | solution.py:486
  69.3 1.3 collective-permute-start.15
  70.6 0.8 product.11
  71.4 4.6 %collective-permute-start.14 = (bf16[1104,256]{1,0:T(8,128)(2,1)S(1)}, bf16[1104,256]{1,0:T(8,128)(2,1)S(1)}, u32[]{:S(2)}, u32[]{:S(2)}) collective-permute-start(bf16[1104,256]{1,0:T(8,128)(2,1)S(1)} %get-tuple-element.91), channel_id=1, source_target_pairs={{0,8},{24,16},{1,9},{25,17},{2,10},{26,18},{3,11},{27,19},{4,12},{... | collective-permute-start | bytes 1695752 | tf_op jit(solution)/shard_map/ppermute | solution.py:486
  76.0 1.3 collective-permute-start.19
  77.3 3.6 %collective-permute-done.16.got_ref = bf16[1056,256]{1,0:T(8,128)(2,1)S(1)} collective-permute-done((bf16[1056,256]{1,0:T(8,128)(2,1)S(1)}, bf16[1056,256]{1,0:T(8,128)(2,1)S(1)}, u32[]{:S(2)}, u32[]{:S(2)}) %collective-permute-start.16) | collective-permute-done | bytes 540704 | tf_op jit(solution)/shard_map/ppermute | solution.py:486
  81.6 0.7 product.14
  82.3 7.4 %collective-permute-start.18 = (bf16[1056,256]{1,0:T(8,128)(2,1)S(1)}, bf16[1056,256]{1,0:T(8,128)(2,1)S(1)}, u32[]{:S(2)}, u32[]{:S(2)}) collective-permute-start(bf16[1056,256]{1,0:T(8,128)(2,1)S(1)} %get-tuple-element.103), channel_id=1, source_target_pairs={{0,8},{24,16},{1,9},{25,17},{2,10},{26,18},{3,11},{27,19},{4,12},{... | collective-permute-start | bytes 1622024 | tf_op jit(solution)/shard_map/ppermute | solution.py:486
  89.7 3.3 %collective-permute-done.14.got_ref = bf16[1104,256]{1,0:T(8,128)(2,1)S(1)} collective-permute-done((bf16[1104,256]{1,0:T(8,128)(2,1)S(1)}, bf16[1104,256]{1,0:T(8,128)(2,1)S(1)}, u32[]{:S(2)}, u32[]{:S(2)}) %collective-permute-start.14) | collective-permute-done | bytes 565280 | tf_op jit(solution)/shard_map/ppermute | solution.py:486
  93.0 1.3 collective-permute-start.25
  94.3 0.8 product.12
  95.1 0.7 collective-permute-start.22
  95.8 7.7 %collective-permute-start.21 = (bf16[1104,256]{1,0:T(8,128)(2,1)S(1)}, bf16[1104,256]{1,0:T(8,128)(2,1)S(1)}, u32[]{:S(2)}, u32[]{:S(2)}) collective-permute-start(bf16[1104,256]{1,0:T(8,128)(2,1)S(1)} %get-tuple-element.110), channel_id=1, source_target_pairs={{0,8},{24,16},{1,9},{25,17},{2,10},{26,18},{3,11},{27,19},{4,12},{... | collective-permute-start | bytes 1695752 | tf_op jit(solution)/shard_map/ppermute | solution.py:486
  103.5 0.7 product.15
  105.5 1.3 collective-permute-start.23
  106.8 0.7 collective-permute-start.24
  107.5 1.1 collective-permute-done.25.refs_2_.refs_3_
  108.6 10.7 %collective-permute-start.26 = (bf16[1056,256]{1,0:T(8,128)(2,1)S(1)}, bf16[1056,256]{1,0:T(8,128)(2,1)S(1)}, u32[]{:S(2)}, u32[]{:S(2)}) collective-permute-start(bf16[1056,256]{1,0:T(8,128)(2,1)S(1)} %get-tuple-element.119), channel_id=1, source_target_pairs={{0,8},{24,16},{1,9},{25,17},{2,10},{26,18},{3,11},{27,19},{4,12},{... | collective-permute-start | bytes 1622024 | tf_op jit(solution)/shard_map/ppermute | solution.py:486
  119.4 1.4 %collective-permute-start.27 = (bf16[1056,256]{1,0:T(8,128)(2,1)S(1)}, bf16[1056,256]{1,0:T(8,128)(2,1)S(1)}, u32[]{:S(2)}, u32[]{:S(2)}) collective-permute-start(bf16[1056,256]{1,0:T(8,128)(2,1)S(1)} %add.11), channel_id=1, source_target_pairs={{8,0},{16,24},{9,1},{17,25},{10,2},{18,26},{11,3},{19,27},{12,4},{... | collective-permute-start | bytes 1622024 | tf_op jit(solution)/shard_map/ppermute | solution.py:486
  120.9 0.7 product.18.refs_0_
  121.6 0.7 product.19.refs_1_
  122.4 1.3 left.1
  123.7 2.5 %collective-permute-done.26.refs_6_ = bf16[1056,256]{1,0:T(8,128)(2,1)S(1)} collective-permute-done((bf16[1056,256]{1,0:T(8,128)(2,1)S(1)}, bf16[1056,256]{1,0:T(8,128)(2,1)S(1)}, u32[]{:S(2)}, u32[]{:S(2)}) %collective-permute-start.26) | collective-permute-done | bytes 540704 | tf_op jit(solution)/shard_map/ppermute | solution.py:486
  126.4 6.7 %collective-permute-done.27.refs_2_ = bf16[1056,256]{1,0:T(8,128)(2,1)S(1)} collective-permute-done((bf16[1056,256]{1,0:T(8,128)(2,1)S(1)}, bf16[1056,256]{1,0:T(8,128)(2,1)S(1)}, u32[]{:S(2)}, u32[]{:S(2)}) %collective-permute-start.27) | collective-permute-done | bytes 540704 | tf_op jit(solution)/shard_map/ppermute | solution.py:486
  133.0 2.8 %final.1 = (f32[1440,240]{1,0:T(8,128)}, f32[1440,120]{1,0:T(8,128)}) custom-call(f32[1104,256]{1,0:T(8,128)S(1)} %get-tuple-element.132.refs_0_, f32[1056,256]{1,0:T(8,128)S(1)} %get-tuple-element.133.refs_1_, bf16[1056,256]{1,0:T(8,128)(2,1)S(1)} %collective-permute-done.27.refs_2_, bf16[960,960]{1,0:T(8,128)(2,1)S(1)} %get-tuple-element.123.refs_3_, ...), custom_call_target="tpu_custom_call" | custom-call | tf_op jit(solution)/shard_map/final/pallas_call | solution.py:577
  (41 shorter events, 4.3 us)
Async XLA Ops:
  2.9 17.2 %copy-start.2 = (bf16[1456,128]{1,0:T(8,128)(2,1)S(1)}, bf16[1456,128]{1,0:T(8,128)(2,1)}, u32[]{:S(2)}) copy-start(bf16[1456,128]{1,0:T(8,128)(2,1)} %get-tuple-element.76.refs_0_) | copy-start | bytes 1118212
  2.9 17.2 %collective-permute-start.2 = (bf16[1200,256]{1,0:T(8,128)(2,1)}, bf16[1200,256]{1,0:T(8,128)(2,1)S(1)}, u32[]{:S(2)}, u32[]{:S(2)}) collective-permute-start(bf16[1200,256]{1,0:T(8,128)(2,1)} %get-tuple-element.81.refs_0_), channel_id=1, source_target_pairs={{0,8},{16,24},{8,0},{24,16},{1,9},{17,25},{9,1},{25,17},{2,10},{18... | collective-permute-start | bytes 1843208 | tf_op jit(solution)/shard_map/ppermute | solution.py:340
  6.0 14.1 %collective-permute-start.3 = (bf16[1200,256]{1,0:T(8,128)(2,1)}, bf16[1200,256]{1,0:T(8,128)(2,1)S(1)}, u32[]{:S(2)}, u32[]{:S(2)}) collective-permute-start(bf16[1200,256]{1,0:T(8,128)(2,1)} %get-tuple-element.81.refs_0_), channel_id=1, source_target_pairs={{8,16},{16,8},{9,17},{17,9},{10,18},{18,10},{11,19},{19,11},{12,20... | collective-permute-start | bytes 1843208 | tf_op jit(solution)/shard_map/ppermute | solution.py:340
  6.7 10.4 %collective-permute-start = (bf16[1456,128]{1,0:T(8,128)(2,1)}, bf16[1456,128]{1,0:T(8,128)(2,1)S(1)}, u32[]{:S(2)}, u32[]{:S(2)}) collective-permute-start(bf16[1456,128]{1,0:T(8,128)(2,1)} %get-tuple-element.76.refs_0_), channel_id=1, source_target_pairs={{0,2},{1,3},{2,0},{3,1},{4,6},{5,7},{6,4},{7,5},{8,10},{9,11},{10,... | collective-permute-start | bytes 1118216 | tf_op jit(solution)/shard_map/ppermute | solution.py:444
  8.2 10.1 %collective-permute-start.1 = (bf16[1456,128]{1,0:T(8,128)(2,1)}, bf16[1456,128]{1,0:T(8,128)(2,1)S(1)}, u32[]{:S(2)}, u32[]{:S(2)}) collective-permute-start(bf16[1456,128]{1,0:T(8,128)(2,1)} %get-tuple-element.76.refs_0_), channel_id=1, source_target_pairs={{0,4},{1,5},{2,6},{3,7},{4,0},{5,1},{6,2},{7,3},{8,12},{9,13},{10,... | collective-permute-start | bytes 1118216 | tf_op jit(solution)/shard_map/ppermute | solution.py:444
  9.8 1.0 copy-start.3
  10.8 0.9 copy-start.4
  11.7 24.9 %copy-start = (bf16[1,1,8,128,1440]{3,4,2,1,0:T(8,128)(2,1)S(1)}, bf16[1,1,8,128,1440]{3,4,2,1,0:T(8,128)(2,1)}, u32[]{:S(2)}) copy-start(bf16[1,1,8,128,1440]{3,4,2,1,0:T(8,128)(2,1)} %param.13) | copy-start | bytes 8847364
  20.6 16.0 %collective-permute-start.8 = (bf16[3,1456,128]{2,1,0:T(8,128)(2,1)S(1)}, bf16[3,1456,128]{2,1,0:T(8,128)(2,1)S(1)}, u32[]{:S(2)}, u32[]{:S(2)}) collective-permute-start(bf16[3,1456,128]{2,1,0:T(8,128)(2,1)S(1)} %collect.1), channel_id=1, source_target_pairs={{0,1},{1,0},{2,3},{3,2},{4,5},{5,4},{6,7},{7,6},{8,9},{9,8},{10,11... | collective-permute-start | bytes 3354632 | tf_op jit(solution)/shard_map/ppermute | solution.py:458
  20.6 14.2 %collective-permute-start.7 = (bf16[1456,128]{1,0:T(8,128)(2,1)S(1)}, bf16[1456,128]{1,0:T(8,128)(2,1)S(1)}, u32[]{:S(2)}, u32[]{:S(2)}) collective-permute-start(bf16[1456,128]{1,0:T(8,128)(2,1)S(1)} %copy-done.2), channel_id=1, source_target_pairs={{0,6},{1,7},{2,4},{3,5},{4,2},{5,3},{6,0},{7,1},{8,14},{9,15},{10,... | collective-permute-start | bytes 1118216 | tf_op jit(solution)/shard_map/ppermute | solution.py:453
  23.3 20.0 %collective-permute-start.4 = (bf16[1200,256]{1,0:T(8,128)(2,1)S(1)}, bf16[1200,256]{1,0:T(8,128)(2,1)S(1)}, u32[]{:S(2)}, u32[]{:S(2)}) collective-permute-start(bf16[1200,256]{1,0:T(8,128)(2,1)S(1)} %collective-permute-done.3.refs_0_), channel_id=1, source_target_pairs={{16,24},{8,0},{17,25},{9,1},{18,26},{10,2},{19,27},{11,3},{20,28},... | collective-permute-start | bytes 1843208 | tf_op jit(solution)/shard_map/ppermute | solution.py:340
  24.6 18.8 %collective-permute-start.5 = (bf16[1200,256]{1,0:T(8,128)(2,1)S(1)}, bf16[1200,256]{1,0:T(8,128)(2,1)S(1)}, u32[]{:S(2)}, u32[]{:S(2)}) collective-permute-start(bf16[1200,256]{1,0:T(8,128)(2,1)S(1)} %collective-permute-done.2.refs_0_), channel_id=1, source_target_pairs={{8,16},{16,8},{9,17},{17,9},{10,18},{18,10},{11,19},{19,11},{12,20... | collective-permute-start | bytes 1843208 | tf_op jit(solution)/shard_map/ppermute | solution.py:340
  25.3 22.6 %collective-permute-start.6 = (bf16[1200,256]{1,0:T(8,128)(2,1)S(1)}, bf16[1200,256]{1,0:T(8,128)(2,1)S(1)}, u32[]{:S(2)}, u32[]{:S(2)}) collective-permute-start(bf16[1200,256]{1,0:T(8,128)(2,1)S(1)} %pack_left.1.own_ref), channel_id=1, source_target_pairs={{0,8},{24,16},{1,9},{25,17},{2,10},{26,18},{3,11},{27,19},{4,12},{... | collective-permute-start | bytes 1843208 | tf_op jit(solution)/shard_map/ppermute | solution.py:463
  34.9 1.8 %collective-permute-start.9 = (bf16[1456,128]{1,0:T(8,128)(2,1)S(1)}, bf16[1456,128]{1,0:T(8,128)(2,1)S(1)}, u32[]{:S(2)}, u32[]{:S(2)}) collective-permute-start(bf16[1456,128]{1,0:T(8,128)(2,1)S(1)} %collective-permute-done.7.refs_3_), channel_id=1, source_target_pairs={{0,1},{1,0},{2,3},{3,2},{4,5},{5,4},{6,7},{7,6},{8,9},{9,8},{10,11... | collective-permute-start | bytes 1118216 | tf_op jit(solution)/shard_map/ppermute | solution.py:458
  47.9 21.4 %collective-permute-start.11 = (bf16[1200,256]{1,0:T(8,128)(2,1)S(1)}, bf16[1200,256]{1,0:T(8,128)(2,1)S(1)}, u32[]{:S(2)}, u32[]{:S(2)}) collective-permute-start(bf16[1200,256]{1,0:T(8,128)(2,1)S(1)} %collective-permute-done.5.refs_1_), channel_id=1, source_target_pairs={{16,24},{8,0},{17,25},{9,1},{18,26},{10,2},{19,27},{11,3},{20,28},... | collective-permute-start | bytes 1843208 | tf_op jit(solution)/shard_map/ppermute | solution.py:340
  49.2 20.1 %collective-permute-start.12 = (bf16[1200,256]{1,0:T(8,128)(2,1)S(1)}, bf16[1200,256]{1,0:T(8,128)(2,1)S(1)}, u32[]{:S(2)}, u32[]{:S(2)}) collective-permute-start(bf16[1200,256]{1,0:T(8,128)(2,1)S(1)} %pack_left.1.own_ref), channel_id=1, source_target_pairs={{8,16},{16,8},{9,17},{17,9},{10,18},{18,10},{11,19},{19,11},{12,20... | collective-permute-start | bytes 1843208 | tf_op jit(solution)/shard_map/ppermute | solution.py:472
  50.7 18.6 %collective-permute-start.10 = (bf16[1104,256]{1,0:T(8,128)(2,1)S(1)}, bf16[1104,256]{1,0:T(8,128)(2,1)S(1)}, u32[]{:S(2)}, u32[]{:S(2)}) collective-permute-start(bf16[1104,256]{1,0:T(8,128)(2,1)S(1)} %product.10), channel_id=1, source_target_pairs={{0,8},{24,16},{1,9},{25,17},{2,10},{26,18},{3,11},{27,19},{4,12},{... | collective-permute-start | bytes 1695752 | tf_op jit(solution)/shard_map/ppermute | solution.py:486
  56.1 26.2 %collective-permute-start.17 = (bf16[1200,256]{1,0:T(8,128)(2,1)S(1)}, bf16[1200,256]{1,0:T(8,128)(2,1)S(1)}, u32[]{:S(2)}, u32[]{:S(2)}) collective-permute-start(bf16[1200,256]{1,0:T(8,128)(2,1)S(1)} %collective-permute-done.6.ends_ref), channel_id=1, source_target_pairs={{8,16},{16,8},{9,17},{17,9},{10,18},{18,10},{11,19},{19,11},{12,20... | collective-permute-start | bytes 1843208 | tf_op jit(solution)/shard_map/ppermute | solution.py:472
  57.5 23.3 %collective-permute-start.16 = (bf16[1056,256]{1,0:T(8,128)(2,1)S(1)}, bf16[1056,256]{1,0:T(8,128)(2,1)S(1)}, u32[]{:S(2)}, u32[]{:S(2)}) collective-permute-start(bf16[1056,256]{1,0:T(8,128)(2,1)S(1)} %product.13), channel_id=1, source_target_pairs={{0,8},{24,16},{1,9},{25,17},{2,10},{26,18},{3,11},{27,19},{4,12},{... | collective-permute-start | bytes 1622024 | tf_op jit(solution)/shard_map/ppermute | solution.py:486
  69.3 25.8 %collective-permute-start.15 = (bf16[1200,256]{1,0:T(8,128)(2,1)S(1)}, bf16[1200,256]{1,0:T(8,128)(2,1)S(1)}, u32[]{:S(2)}, u32[]{:S(2)}) collective-permute-start(bf16[1200,256]{1,0:T(8,128)(2,1)S(1)} %pack_left.1.own_ref), channel_id=1, source_target_pairs={{16,24},{8,0},{17,25},{9,1},{18,26},{10,2},{19,27},{11,3},{20,28},... | collective-permute-start | bytes 1843208 | tf_op jit(solution)/shard_map/ppermute | solution.py:472
  71.4 21.6 %collective-permute-start.14 = (bf16[1104,256]{1,0:T(8,128)(2,1)S(1)}, bf16[1104,256]{1,0:T(8,128)(2,1)S(1)}, u32[]{:S(2)}, u32[]{:S(2)}) collective-permute-start(bf16[1104,256]{1,0:T(8,128)(2,1)S(1)} %get-tuple-element.91), channel_id=1, source_target_pairs={{0,8},{24,16},{1,9},{25,17},{2,10},{26,18},{3,11},{27,19},{4,12},{... | collective-permute-start | bytes 1695752 | tf_op jit(solution)/shard_map/ppermute | solution.py:486
  76.0 28.6 %collective-permute-start.19 = (bf16[1200,256]{1,0:T(8,128)(2,1)S(1)}, bf16[1200,256]{1,0:T(8,128)(2,1)S(1)}, u32[]{:S(2)}, u32[]{:S(2)}) collective-permute-start(bf16[1200,256]{1,0:T(8,128)(2,1)S(1)} %collective-permute-done.12.odd_ref), channel_id=1, source_target_pairs={{16,24},{8,0},{17,25},{9,1},{18,26},{10,2},{19,27},{11,3},{20,28},... | collective-permute-start | bytes 1843208 | tf_op jit(solution)/shard_map/ppermute | solution.py:472
  80.9 14.9 %collective-permute-start.13 = (bf16[1104,256]{1,0:T(8,128)(2,1)S(1)}, bf16[1104,256]{1,0:T(8,128)(2,1)S(1)}, u32[]{:S(2)}, u32[]{:S(2)}) collective-permute-start(bf16[1104,256]{1,0:T(8,128)(2,1)S(1)} %add.6), channel_id=1, source_target_pairs={{8,16},{16,8},{9,17},{17,9},{10,18},{18,10},{11,19},{19,11},{12,20... | collective-permute-start | bytes 1695752 | tf_op jit(solution)/shard_map/ppermute | solution.py:486
  82.3 22.2 %collective-permute-start.18 = (bf16[1056,256]{1,0:T(8,128)(2,1)S(1)}, bf16[1056,256]{1,0:T(8,128)(2,1)S(1)}, u32[]{:S(2)}, u32[]{:S(2)}) collective-permute-start(bf16[1056,256]{1,0:T(8,128)(2,1)S(1)} %get-tuple-element.103), channel_id=1, source_target_pairs={{0,8},{24,16},{1,9},{25,17},{2,10},{26,18},{3,11},{27,19},{4,12},{... | collective-permute-start | bytes 1622024 | tf_op jit(solution)/shard_map/ppermute | solution.py:486
  93.0 15.6 %collective-permute-start.25 = (bf16[1200,256]{1,0:T(8,128)(2,1)S(1)}, bf16[1200,256]{1,0:T(8,128)(2,1)S(1)}, u32[]{:S(2)}, u32[]{:S(2)}) collective-permute-start(bf16[1200,256]{1,0:T(8,128)(2,1)S(1)} %collective-permute-done.17.refs_1_), channel_id=1, source_target_pairs={{16,24},{8,0},{17,25},{9,1},{18,26},{10,2},{19,27},{11,3},{20,28},... | collective-permute-start | bytes 1843208 | tf_op jit(solution)/shard_map/ppermute | solution.py:472
  95.1 10.4 %collective-permute-start.22 = (bf16[1104,256]{1,0:T(8,128)(2,1)S(1)}, bf16[1104,256]{1,0:T(8,128)(2,1)S(1)}, u32[]{:S(2)}, u32[]{:S(2)}) collective-permute-start(bf16[1104,256]{1,0:T(8,128)(2,1)S(1)} %add.8), channel_id=1, source_target_pairs={{8,16},{16,8},{9,17},{17,9},{10,18},{18,10},{11,19},{19,11},{12,20... | collective-permute-start | bytes 1695752 | tf_op jit(solution)/shard_map/ppermute | solution.py:486
  95.8 23.6 %collective-permute-start.21 = (bf16[1104,256]{1,0:T(8,128)(2,1)S(1)}, bf16[1104,256]{1,0:T(8,128)(2,1)S(1)}, u32[]{:S(2)}, u32[]{:S(2)}) collective-permute-start(bf16[1104,256]{1,0:T(8,128)(2,1)S(1)} %get-tuple-element.110), channel_id=1, source_target_pairs={{0,8},{24,16},{1,9},{25,17},{2,10},{26,18},{3,11},{27,19},{4,12},{... | collective-permute-start | bytes 1695752 | tf_op jit(solution)/shard_map/ppermute | solution.py:486
  104.6 14.8 %collective-permute-start.20 = (bf16[1056,256]{1,0:T(8,128)(2,1)S(1)}, bf16[1056,256]{1,0:T(8,128)(2,1)S(1)}, u32[]{:S(2)}, u32[]{:S(2)}) collective-permute-start(bf16[1056,256]{1,0:T(8,128)(2,1)S(1)} %add.7), channel_id=1, source_target_pairs={{8,16},{16,8},{9,17},{17,9},{10,18},{18,10},{11,19},{19,11},{12,20... | collective-permute-start | bytes 1622024 | tf_op jit(solution)/shard_map/ppermute | solution.py:486
  105.5 20.7 %collective-permute-start.23 = (bf16[1104,256]{1,0:T(8,128)(2,1)S(1)}, bf16[1104,256]{1,0:T(8,128)(2,1)S(1)}, u32[]{:S(2)}, u32[]{:S(2)}) collective-permute-start(bf16[1104,256]{1,0:T(8,128)(2,1)S(1)} %add.9), channel_id=1, source_target_pairs={{8,0},{16,24},{9,1},{17,25},{10,2},{18,26},{11,3},{19,27},{12,4},{... | collective-permute-start | bytes 1695752 | tf_op jit(solution)/shard_map/ppermute | solution.py:486
  106.8 16.9 %collective-permute-start.24 = (bf16[1056,256]{1,0:T(8,128)(2,1)S(1)}, bf16[1056,256]{1,0:T(8,128)(2,1)S(1)}, u32[]{:S(2)}, u32[]{:S(2)}) collective-permute-start(bf16[1056,256]{1,0:T(8,128)(2,1)S(1)} %add.10), channel_id=1, source_target_pairs={{8,16},{16,8},{9,17},{17,9},{10,18},{18,10},{11,19},{19,11},{12,20... | collective-permute-start | bytes 1622024 | tf_op jit(solution)/shard_map/ppermute | solution.py:486
  108.6 17.6 %collective-permute-start.26 = (bf16[1056,256]{1,0:T(8,128)(2,1)S(1)}, bf16[1056,256]{1,0:T(8,128)(2,1)S(1)}, u32[]{:S(2)}, u32[]{:S(2)}) collective-permute-start(bf16[1056,256]{1,0:T(8,128)(2,1)S(1)} %get-tuple-element.119), channel_id=1, source_target_pairs={{0,8},{24,16},{1,9},{25,17},{2,10},{26,18},{3,11},{27,19},{4,12},{... | collective-permute-start | bytes 1622024 | tf_op jit(solution)/shard_map/ppermute | solution.py:486
  119.4 1.5 %copy-start.1 = (bf16[1200,256]{1,0:T(8,128)(2,1)S(1)}, bf16[1200,256]{1,0:T(8,128)(2,1)}, u32[]{:S(2)}) copy-start(bf16[1200,256]{1,0:T(8,128)(2,1)} %get-tuple-element.81.refs_0_) | copy-start | bytes 1843204
  119.4 13.6 %collective-permute-start.27 = (bf16[1056,256]{1,0:T(8,128)(2,1)S(1)}, bf16[1056,256]{1,0:T(8,128)(2,1)S(1)}, u32[]{:S(2)}, u32[]{:S(2)}) collective-permute-start(bf16[1056,256]{1,0:T(8,128)(2,1)S(1)} %add.11), channel_id=1, source_target_pairs={{8,0},{16,24},{9,1},{17,25},{10,2},{18,26},{11,3},{19,27},{12,4},{... | collective-permute-start | bytes 1622024 | tf_op jit(solution)/shard_map/ppermute | solution.py:486

commit v4 on v2

--- a/solution.py
+++ b/solution.py
@@ -49,33 +49,66 @@
 
 
 class Fold:
-    def __init__(self, rows_w, rows_n, wide, narrow):
+    def __init__(self, rows_w, rows_n, wide, narrow, tuck=False):
         self.rows_w, self.rows_n, self.wide, self.narrow = rows_w, rows_n, wide, narrow
         self.lanes = round_up(wide, LANES)
         self.step = round_up(narrow, LANES)
         self.ways = max(1, self.lanes // self.step)
         while rows_n % (self.ways * 16):
             self.ways -= 1
-        self.part = rows_n // self.ways
+        self.tucked, self.group = 0, narrow
+        if tuck:
+            for rows in range(16, min(rows_w, rows_n) + 1, 16):
+                group = -(-narrow // (rows_w // rows))
+                if group <= self.lanes - wide and (rows_n - rows) % (self.ways * 16) == 0:
+                    self.tucked, self.group = rows, group
+        self.part = (rows_n - self.tucked) // self.ways
         self.rows = rows_w + self.part
         self.shape = (self.rows, self.lanes)
+
+    def places(self):
+        found = []
+        if self.tucked:
+            for i, start in enumerate(range(0, self.narrow, self.group)):
+                stop = min(self.narrow, start + self.group)
+                found.append(
+                    (
+                        slice(0, self.tucked),
+                        slice(start, stop),
+                        slice(i * self.tucked, (i + 1) * self.tucked),
+                        slice(self.wide, self.wide + stop - start),
+                    )
+                )
+        for way in range(self.ways if self.part else 0):
+            low = self.tucked + way * self.part
+            found.append(
+                (
+                    slice(low, low + self.part),
+                    slice(0, self.narrow),
+                    slice(self.rows_w, self.rows),
+                    slice(way * self.step, way * self.step + self.narrow),
+                )
+            )
+        return found
 
     def write(self, ref, wide_value, narrow_value):
         ref[...] = jnp.zeros(self.shape, ref.dtype)
         ref[0 : self.rows_w, 0 : self.wide] = wide_value
-        for way in range(self.ways):
-            start = way * self.step
-            ref[self.rows_w : self.rows, start : start + self.narrow] = narrow_value[
-                way * self.part : (way + 1) * self.part
-            ]
+        for rows, columns, at_rows, at_lanes in self.places():
+            ref[at_rows, at_lanes] = narrow_value[rows, columns]
 
     def wide_of(self, value):
         return value[0 : self.rows_w, 0 : self.wide]
 
     def narrow_of(self, value):
-        low = value[self.rows_w : self.rows]
-        parts = [low[:, way * self.step : way * self.step + self.narrow] for way in range(self.ways)]
-        return parts[0] if self.ways == 1 else jnp.concatenate(parts, axis=0)
+        parts = [value[at_rows, at_lanes] for _, _, at_rows, at_lanes in self.places()]
+        return parts[0] if len(parts) == 1 else jnp.concatenate(parts, axis=0)
+
+    def put_narrow(self, value, ref, low_row, low_column):
+        for rows, columns, at_rows, at_lanes in self.places():
+            ref[
+                low_row + rows.start : low_row + rows.stop, low_column + columns.start : low_column + columns.stop
+            ] = value[at_rows, at_lanes]
 
 
 def token_kernel(root, cot_ref, gate_ref, route_ref, slot_ref, rw_ref, rn_ref, tok_ref, right_ref,
@@ -266,7 +299,7 @@
     for q in range(n):
         piece = held[q]
         wide_ref[:, q * root.wide : (q + 1) * root.wide] = root.wide_of(piece)
-        narrow_ref[:, q * root.narrow : (q + 1) * root.narrow] = root.narrow_of(piece)
+        root.put_narrow(piece, narrow_ref, 0, q * root.narrow)
 
 
 def add_arrivals(chains, got_refs, own_refs, out_refs, dtype):
@@ -291,12 +324,13 @@
 def final_kernel(chains, block, keys, *refs):
     got_refs = dict(zip(keys, refs[len(chains) :]))
     wide_ref, narrow_ref, out_w_ref, out_n_ref = refs[len(chains) + len(keys) :][:4]
-    totals = refs[len(refs) - len(chains) :]
+    totals, narrow_rows = refs[len(refs) - len(chains) - 1 : -1], refs[-1]
     add_arrivals(chains, got_refs, refs[: len(chains)], totals, BF16)
-    wides = [chain.fold.wide_of(total[...]) for chain, total in zip(chains, totals)]
-    narrows = [chain.fold.narrow_of(total[...]) for chain, total in zip(chains, totals)]
-    for parts, out_ref in ((wides, out_w_ref), (narrows, out_n_ref)):
-        rows = jnp.concatenate(parts, axis=0)
+    values = [total[...] for total in totals]
+    for chain, value in zip(chains, values):
+        chain.fold.put_narrow(value, narrow_rows, chain.low, 0)
+    wide_rows = jnp.concatenate([chain.fold.wide_of(value) for chain, value in zip(chains, values)], axis=0)
+    for rows, out_ref in ((wide_rows, out_w_ref), (narrow_rows[...], out_n_ref)):
         out_ref[0:block, :] = dot_nn(wide_ref[...], rows[0:block])
         out_ref[block:, :] = dot_nn(narrow_ref[...], rows[block:])
 
@@ -325,8 +359,9 @@
     gap = round_up(block, LANES)
     span = gap + round_up(rest, LANES)
     root = Fold(block, rest, wide, narrow)
+    left_root = Fold(block, rest, wide, narrow, True)
     cut = ffn // 64 * 32
-    folds = [Fold(rows, rows, wide, narrow) for rows in (cut, ffn - cut)]
+    folds = [Fold(rows, rows, wide, narrow, True) for rows in (cut, ffn - cut)]
     sooner = [n - 2, n - 1] if n > 2 else [1]
     chains = [
         Chain(n, 0, sooner + list(range(n - 3, 0, -1)), 0, folds[0]),
@@ -380,9 +415,9 @@
 
     def pack_left(wide_piece, narrow_piece):
         return pl.pallas_call(
-            functools.partial(pack_left_kernel, root),
+            functools.partial(pack_left_kernel, left_root),
             in_specs=[ANY] * 2,
-            out_shape=jax.ShapeDtypeStruct(root.shape, BF16),
+            out_shape=jax.ShapeDtypeStruct(left_root.shape, BF16),
             scratch_shapes=[
                 pltpu.VMEM((block, wide), BF16),
                 pltpu.VMEM((rest, narrow), BF16),
@@ -548,13 +583,13 @@
 
     left_inputs = [left, left_ends, left_rest, left_odd] + [item for pair in lefts[2:] for item in pair]
     left_w, left_n = pl.pallas_call(
-        functools.partial(left_kernel, root, n),
+        functools.partial(left_kernel, left_root, n),
         in_specs=[ANY] * len(left_inputs),
         out_shape=(
             jax.ShapeDtypeStruct((block, block), BF16),
             jax.ShapeDtypeStruct((rest, rest), BF16),
         ),
-        scratch_shapes=[pltpu.VMEM((n,) + root.shape, BF16), pltpu.SemaphoreType.DMA((n,))],
+        scratch_shapes=[pltpu.VMEM((n,) + left_root.shape, BF16), pltpu.SemaphoreType.DMA((n,))],
         compiler_params=params(32),
         cost_estimate=cost(),
         name="left",
@@ -579,7 +614,8 @@
         in_specs=[VMEM] * (len(chains) + len(last) + 2),
         out_specs=[VMEM] * 2,
         out_shape=[jax.ShapeDtypeStruct((ffn, wide), F32), jax.ShapeDtypeStruct((ffn, narrow), F32)],
-        scratch_shapes=[pltpu.VMEM(chain.fold.shape, BF16) for chain in chains],
+        scratch_shapes=[pltpu.VMEM(chain.fold.shape, BF16) for chain in chains]
+        + [pltpu.VMEM((ffn, narrow), BF16)],
         compiler_params=params(32),
         cost_estimate=cost(),
         name="final",

time: 133 us -> 132 us (level)
  waiting for transfers between devices: 49.2 us -> 47.3 us
    unnamed x10 -> x12, local copies, waits for them, and re-layouts: 1.95 us -> 2.93 us
  transfers between devices with their start and end apart: 27 -> 27, of which waited for: 13 -> 12; matrix products, arithmetic and copies ran while one was open for 0% -> 0% of each run, Pallas kernels for 11% -> 12%
where the time goes in v4:
time: 132 us; the launch traced here: 131 us
  starting transfers between devices  58.9 us (45%)
  waiting for transfers between devices  47.3 us (36%)
  Pallas kernels  20.9 us (16%)
  local copies, waits for them, and re-layouts  2.93 us (2%)
    ppermute x11, starting transfers between devices, go(): sent[chain.half, t, s] = lax.ppermute(term, 'dp', chain.pairs(t, s))  31.2 us
    ppermute x11, waiting for transfers between devices, go(): sent[chain.half, t, s] = lax.ppermute(term, 'dp', chain.pairs(t, s))  18.9 us
    ppermute x5, waiting for transfers between devices, hop_one(): return lax.ppermute(piece, 'dp', pairs) if pairs else piece  14.2 us
    ppermute x1, starting transfers between devices, body(): left_ends = lax.ppermute(left, 'dp', ends)  9.51 us
    ppermute x5, starting transfers between devices, hop(): lax.ppermute(pieces[1 - s], 'dp', gather_pairs(k, s))  7.04 us
    pallas_call x1, Pallas kernels, partial(): pl.pallas_call(functools.partial(partial_kernel, topk, width, block, gap,...  6.63 us
    pallas_call x9, Pallas kernels, product(): pl.pallas_call(functools.partial(product_kernel, chain, t, keys, root, bl...  6 us
    ppermute x2, waiting for transfers between devices, body(): lax.ppermute(tok, 'expert', [(i, i ^ 2 * m) for i in range(experts)])  5.89 us
  transfers between devices with their start and end apart: 27, of which 12 were waited for; matrix products, arithmetic and copies ran while one was open for 0% of the time, Pallas kernels for 12%

profile of v4, /device:TPU:0, one launch (start us, length us, event | category | flops | bytes accessed | tf_op | source)
XLA Modules:
  0.0 131.0 jit_solution(6083222498609357)
XLA Ops:
  0.6 2.2 %tokens.1 = (bf16[1456,128]{1,0:T(8,128)(2,1)}, bf16[1200,256]{1,0:T(8,128)(2,1)}) custom-call(bf16[1440,128]{1,0:T(8,128)(2,1)} %bitcast.17, bf16[4,128]{1,0:T(4,128)(2,1)} %bitcast.21, s32[4,128]{1,0:T(4,128)} %bitcast.19, s32[4,128]{1,0:T(4,128)} %bitcast.20, bf16[960,240]{1,0:T(8,128)(2,1)} %bitcast.16, bf16[480,120]{1,0:T(8,128)(2,1)} %bitcast.18), custom_call_target="tpu_custom_call" | custom-call | tf_op jit(solution)/shard_map/tokens/pallas_call | solution.py:381
  2.9 3.1 %collective-permute-start.2 = (bf16[1200,256]{1,0:T(8,128)(2,1)}, bf16[1200,256]{1,0:T(8,128)(2,1)S(1)}, u32[]{:S(2)}, u32[]{:S(2)}) collective-permute-start(bf16[1200,256]{1,0:T(8,128)(2,1)} %get-tuple-element.78.refs_0_), channel_id=1, source_target_pairs={{0,8},{16,24},{8,0},{24,16},{1,9},{17,25},{9,1},{25,17},{2,10},{18... | collective-permute-start | bytes 1843208 | tf_op jit(solution)/shard_map/ppermute | solution.py:377
  6.7 1.6 %collective-permute-start = (bf16[1456,128]{1,0:T(8,128)(2,1)}, bf16[1456,128]{1,0:T(8,128)(2,1)S(1)}, u32[]{:S(2)}, u32[]{:S(2)}) collective-permute-start(bf16[1456,128]{1,0:T(8,128)(2,1)} %get-tuple-element.71.refs_0_), channel_id=1, source_target_pairs={{0,2},{1,3},{2,0},{3,1},{4,6},{5,7},{6,4},{7,5},{8,10},{9,11},{10,... | collective-permute-start | bytes 1118216 | tf_op jit(solution)/shard_map/ppermute | solution.py:481
  8.2 1.5 %collective-permute-start.1 = (bf16[1456,128]{1,0:T(8,128)(2,1)}, bf16[1456,128]{1,0:T(8,128)(2,1)S(1)}, u32[]{:S(2)}, u32[]{:S(2)}) collective-permute-start(bf16[1456,128]{1,0:T(8,128)(2,1)} %get-tuple-element.71.refs_0_), channel_id=1, source_target_pairs={{0,4},{1,5},{2,6},{3,7},{4,0},{5,1},{6,2},{7,3},{8,12},{9,13},{10,... | collective-permute-start | bytes 1118216 | tf_op jit(solution)/shard_map/ppermute | solution.py:481
  9.7 1.0 copy-done.4
  10.8 0.9 copy-done.5
  11.7 0.7 pack_left.1.own_ref
  12.4 4.7 %collective-permute-done.refs_1_ = bf16[1456,128]{1,0:T(8,128)(2,1)S(1)} collective-permute-done((bf16[1456,128]{1,0:T(8,128)(2,1)}, bf16[1456,128]{1,0:T(8,128)(2,1)S(1)}, u32[]{:S(2)}, u32[]{:S(2)}) %collective-permute-start) | collective-permute-done | bytes 372768 | tf_op jit(solution)/shard_map/ppermute | solution.py:481
  17.1 1.2 collective-permute-done.1.refs_2_
  18.3 1.7 %collective-permute-done.2.refs_0_ = bf16[1200,256]{1,0:T(8,128)(2,1)S(1)} collective-permute-done((bf16[1200,256]{1,0:T(8,128)(2,1)}, bf16[1200,256]{1,0:T(8,128)(2,1)S(1)}, u32[]{:S(2)}, u32[]{:S(2)}) %collective-permute-start.2) | collective-permute-done | bytes 614432 | tf_op jit(solution)/shard_map/ppermute | solution.py:377
  20.0 1.0 copy-done.2
  21.6 2.7 %collective-permute-start.7 = (bf16[1456,128]{1,0:T(8,128)(2,1)S(1)}, bf16[1456,128]{1,0:T(8,128)(2,1)S(1)}, u32[]{:S(2)}, u32[]{:S(2)}) collective-permute-start(bf16[1456,128]{1,0:T(8,128)(2,1)S(1)} %copy-done.2), channel_id=1, source_target_pairs={{0,6},{1,7},{2,4},{3,5},{4,2},{5,3},{6,0},{7,1},{8,14},{9,15},{10,... | collective-permute-start | bytes 1118216 | tf_op jit(solution)/shard_map/ppermute | solution.py:490
  24.3 1.3 collective-permute-start.4
  25.6 0.7 collective-permute-start.5
  26.3 9.5 %collective-permute-start.6 = (bf16[1152,256]{1,0:T(8,128)(2,1)S(1)}, bf16[1152,256]{1,0:T(8,128)(2,1)S(1)}, u32[]{:S(2)}, u32[]{:S(2)}) collective-permute-start(bf16[1152,256]{1,0:T(8,128)(2,1)S(1)} %pack_left.1.own_ref), channel_id=1, source_target_pairs={{0,8},{24,16},{1,9},{25,17},{2,10},{26,18},{3,11},{27,19},{4,12},{... | collective-permute-start | bytes 1769480 | tf_op jit(solution)/shard_map/ppermute | solution.py:500
  35.9 1.7 %collective-permute-done.9.refs_5_ = bf16[1456,128]{1,0:T(8,128)(2,1)S(1)} collective-permute-done((bf16[1456,128]{1,0:T(8,128)(2,1)S(1)}, bf16[1456,128]{1,0:T(8,128)(2,1)S(1)}, u32[]{:S(2)}, u32[]{:S(2)}) %collective-permute-start.9) | collective-permute-done | bytes 372768 | tf_op jit(solution)/shard_map/ppermute | solution.py:495
  37.6 6.6 %partial.1.partial_ref = bf16[1440,1536]{1,0:T(8,128)(2,1)S(1)} custom-call(bf16[8,1440,128]{2,1,0:T(8,128)(2,1)S(1)} %bitcast.13, bf16[1456,128]{1,0:T(8,128)(2,1)S(1)} %copy-done.3, bf16[1456,128]{1,0:T(8,128)(2,1)S(1)} %collective-permute-done.refs_1_, bf16[1456,128]{1,0:T(8,128)(2,1)S(1)} %collective-permute-done.1.refs_2_, ...), custom_call_target="tpu_custom_call" | custom-call | tf_op jit(solution)/shard_map/partial/pallas_call | solution.py:435
  44.2 4.2 %collective-permute-done.6.ends_ref = bf16[1152,256]{1,0:T(8,128)(2,1)S(1)} collective-permute-done((bf16[1152,256]{1,0:T(8,128)(2,1)S(1)}, bf16[1152,256]{1,0:T(8,128)(2,1)S(1)}, u32[]{:S(2)}, u32[]{:S(2)}) %collective-permute-start.6) | collective-permute-done | bytes 589856 | tf_op jit(solution)/shard_map/ppermute | solution.py:500
  48.4 1.3 collective-permute-start.13
  49.7 0.7 collective-permute-start.14
  50.4 0.7 product.9
  51.1 5.4 %collective-permute-start.12 = (bf16[1024,256]{1,0:T(8,128)(2,1)S(1)}, bf16[1024,256]{1,0:T(8,128)(2,1)S(1)}, u32[]{:S(2)}, u32[]{:S(2)}) collective-permute-start(bf16[1024,256]{1,0:T(8,128)(2,1)S(1)} %product.9), channel_id=1, source_target_pairs={{0,8},{24,16},{1,9},{25,17},{2,10},{26,18},{3,11},{27,19},{4,12},{... | collective-permute-start | bytes 1572872 | tf_op jit(solution)/shard_map/ppermute | solution.py:523
  56.5 1.3 collective-permute-start.10
  57.8 0.7 collective-permute-start.11
  58.6 7.9 %collective-permute-done.12.got_ref = bf16[1024,256]{1,0:T(8,128)(2,1)S(1)} collective-permute-done((bf16[1024,256]{1,0:T(8,128)(2,1)S(1)}, bf16[1024,256]{1,0:T(8,128)(2,1)S(1)}, u32[]{:S(2)}, u32[]{:S(2)}) %collective-permute-start.12) | collective-permute-done | bytes 524320 | tf_op jit(solution)/shard_map/ppermute | solution.py:523
  67.1 1.3 collective-permute-start.19
  68.4 0.8 product.12
  69.1 4.7 %collective-permute-start.18 = (bf16[1072,256]{1,0:T(8,128)(2,1)S(1)}, bf16[1072,256]{1,0:T(8,128)(2,1)S(1)}, u32[]{:S(2)}, u32[]{:S(2)}) collective-permute-start(bf16[1072,256]{1,0:T(8,128)(2,1)S(1)} %product.12), channel_id=1, source_target_pairs={{0,8},{24,16},{1,9},{25,17},{2,10},{26,18},{3,11},{27,19},{4,12},{... | collective-permute-start | bytes 1646600 | tf_op jit(solution)/shard_map/ppermute | solution.py:523
  73.8 0.7 product.10
  74.6 0.7 collective-permute-start.16
  75.3 4.4 %collective-permute-done.10.rest_ref = bf16[1152,256]{1,0:T(8,128)(2,1)S(1)} collective-permute-done((bf16[1152,256]{1,0:T(8,128)(2,1)S(1)}, bf16[1152,256]{1,0:T(8,128)(2,1)S(1)}, u32[]{:S(2)}, u32[]{:S(2)}) %collective-permute-start.10) | collective-permute-done | bytes 589856 | tf_op jit(solution)/shard_map/ppermute | solution.py:509
  79.7 5.4 %collective-permute-start.15 = (bf16[1024,256]{1,0:T(8,128)(2,1)S(1)}, bf16[1024,256]{1,0:T(8,128)(2,1)S(1)}, u32[]{:S(2)}, u32[]{:S(2)}) collective-permute-start(bf16[1024,256]{1,0:T(8,128)(2,1)S(1)} %get-tuple-element.87), channel_id=1, source_target_pairs={{0,8},{24,16},{1,9},{25,17},{2,10},{26,18},{3,11},{27,19},{4,12},{... | collective-permute-start | bytes 1572872 | tf_op jit(solution)/shard_map/ppermute | solution.py:523
  85.1 1.3 collective-permute-start.21
  86.4 0.8 product.13
  87.2 5.2 %collective-permute-done.19.refs_0_ = bf16[1152,256]{1,0:T(8,128)(2,1)S(1)} collective-permute-done((bf16[1152,256]{1,0:T(8,128)(2,1)S(1)}, bf16[1152,256]{1,0:T(8,128)(2,1)S(1)}, u32[]{:S(2)}, u32[]{:S(2)}) %collective-permute-start.19) | collective-permute-done | bytes 589856 | tf_op jit(solution)/shard_map/ppermute | solution.py:509
  93.1 3.1 %collective-permute-start.24 = (bf16[1072,256]{1,0:T(8,128)(2,1)S(1)}, bf16[1072,256]{1,0:T(8,128)(2,1)S(1)}, u32[]{:S(2)}, u32[]{:S(2)}) collective-permute-start(bf16[1072,256]{1,0:T(8,128)(2,1)S(1)} %get-tuple-element.120), channel_id=1, source_target_pairs={{0,8},{24,16},{1,9},{25,17},{2,10},{26,18},{3,11},{27,19},{4,12},{... | collective-permute-start | bytes 1646600 | tf_op jit(solution)/shard_map/ppermute | solution.py:523
  96.2 0.7 product.11
  97.7 0.8 product.14
  98.5 4.6 %collective-permute-done.21.refs_2_.refs_3_ = bf16[1152,256]{1,0:T(8,128)(2,1)S(1)} collective-permute-done((bf16[1152,256]{1,0:T(8,128)(2,1)S(1)}, bf16[1152,256]{1,0:T(8,128)(2,1)S(1)}, u32[]{:S(2)}, u32[]{:S(2)}) %collective-permute-start.21) | collective-permute-done | bytes 589856 | tf_op jit(solution)/shard_map/ppermute | solution.py:509
  103.2 6.3 %collective-permute-start.22 = (bf16[1072,256]{1,0:T(8,128)(2,1)S(1)}, bf16[1072,256]{1,0:T(8,128)(2,1)S(1)}, u32[]{:S(2)}, u32[]{:S(2)}) collective-permute-start(bf16[1072,256]{1,0:T(8,128)(2,1)S(1)} %add.8), channel_id=1, source_target_pairs={{0,8},{8,0},{16,24},{24,16},{1,9},{9,1},{17,25},{25,17},{2,10},{10... | collective-permute-start | bytes 1646600 | tf_op jit(solution)/shard_map/ppermute | solution.py:523
  109.5 2.1 %collective-permute-start.17 = (bf16[1024,256]{1,0:T(8,128)(2,1)S(1)}, bf16[1024,256]{1,0:T(8,128)(2,1)S(1)}, u32[]{:S(2)}, u32[]{:S(2)}) collective-permute-start(bf16[1024,256]{1,0:T(8,128)(2,1)S(1)} %get-tuple-element.94), channel_id=1, source_target_pairs={{0,8},{24,16},{1,9},{25,17},{2,10},{26,18},{3,11},{27,19},{4,12},{... | collective-permute-start | bytes 1572872 | tf_op jit(solution)/shard_map/ppermute | solution.py:523
  111.7 0.8 collective-permute-start.26
  112.6 1.3 collective-permute-start.25
  113.9 0.7 product.16.refs_1_
  114.7 0.7 product.15.refs_0_
  115.4 1.6 %left.1 = (bf16[960,960]{1,0:T(8,128)(2,1)S(1)}, bf16[480,480]{1,0:T(8,128)(2,1)S(1)}) custom-call(bf16[1152,256]{1,0:T(8,128)(2,1)S(1)} %pack_left.1.own_ref, bf16[1152,256]{1,0:T(8,128)(2,1)S(1)} %collective-permute-done.6.ends_ref, bf16[1152,256]{1,0:T(8,128)(2,1)S(1)} %collective-permute-done.10.rest_ref, ...), custom_call_target="tpu_custom_call" | custom-call | tf_op jit(solution)/shard_map/left/pallas_call | solution.py:585
  117.0 10.7 %collective-permute-done.17.refs_3_ = bf16[1024,256]{1,0:T(8,128)(2,1)S(1)} collective-permute-done((bf16[1024,256]{1,0:T(8,128)(2,1)S(1)}, bf16[1024,256]{1,0:T(8,128)(2,1)S(1)}, u32[]{:S(2)}, u32[]{:S(2)}) %collective-permute-start.17) | collective-permute-done | bytes 524320 | tf_op jit(solution)/shard_map/ppermute | solution.py:523
  128.2 2.9 %final.1 = (f32[1440,240]{1,0:T(8,128)}, f32[1440,120]{1,0:T(8,128)}) custom-call(f32[1024,256]{1,0:T(8,128)S(1)} %get-tuple-element.116.refs_0_, f32[1072,256]{1,0:T(8,128)S(1)} %get-tuple-element.117.refs_1_, bf16[1024,256]{1,0:T(8,128)(2,1)S(1)} %collective-permute-done.25.refs_2_, bf16[1072,256]{1,0:T(8,128)(2,1)S(1)} %collective-permute-done.26.refs_3_, ...), custom_call_target="tpu_custom_call" | custom-call | tf_op jit(solution)/shard_map/final/pallas_call | solution.py:612
  (40 shorter events, 4.1 us)
Async XLA Ops:
  2.9 17.2 %collective-permute-start.2 = (bf16[1200,256]{1,0:T(8,128)(2,1)}, bf16[1200,256]{1,0:T(8,128)(2,1)S(1)}, u32[]{:S(2)}, u32[]{:S(2)}) collective-permute-start(bf16[1200,256]{1,0:T(8,128)(2,1)} %get-tuple-element.78.refs_0_), channel_id=1, source_target_pairs={{0,8},{16,24},{8,0},{24,16},{1,9},{17,25},{9,1},{25,17},{2,10},{18... | collective-permute-start | bytes 1843208 | tf_op jit(solution)/shard_map/ppermute | solution.py:377
  6.0 14.1 %collective-permute-start.3 = (bf16[1200,256]{1,0:T(8,128)(2,1)}, bf16[1200,256]{1,0:T(8,128)(2,1)S(1)}, u32[]{:S(2)}, u32[]{:S(2)}) collective-permute-start(bf16[1200,256]{1,0:T(8,128)(2,1)} %get-tuple-element.78.refs_0_), channel_id=1, source_target_pairs={{8,16},{16,8},{9,17},{17,9},{10,18},{18,10},{11,19},{19,11},{12,20... | collective-permute-start | bytes 1843208 | tf_op jit(solution)/shard_map/ppermute | solution.py:377
  6.7 10.4 %collective-permute-start = (bf16[1456,128]{1,0:T(8,128)(2,1)}, bf16[1456,128]{1,0:T(8,128)(2,1)S(1)}, u32[]{:S(2)}, u32[]{:S(2)}) collective-permute-start(bf16[1456,128]{1,0:T(8,128)(2,1)} %get-tuple-element.71.refs_0_), channel_id=1, source_target_pairs={{0,2},{1,3},{2,0},{3,1},{4,6},{5,7},{6,4},{7,5},{8,10},{9,11},{10,... | collective-permute-start | bytes 1118216 | tf_op jit(solution)/shard_map/ppermute | solution.py:481
  8.2 10.1 %collective-permute-start.1 = (bf16[1456,128]{1,0:T(8,128)(2,1)}, bf16[1456,128]{1,0:T(8,128)(2,1)S(1)}, u32[]{:S(2)}, u32[]{:S(2)}) collective-permute-start(bf16[1456,128]{1,0:T(8,128)(2,1)} %get-tuple-element.71.refs_0_), channel_id=1, source_target_pairs={{0,4},{1,5},{2,6},{3,7},{4,0},{5,1},{6,2},{7,3},{8,12},{9,13},{10,... | collective-permute-start | bytes 1118216 | tf_op jit(solution)/shard_map/ppermute | solution.py:481
  9.7 1.0 copy-start.4
  10.8 0.9 copy-start.5
  11.7 25.9 %copy-start = (bf16[1,1,8,128,1440]{3,4,2,1,0:T(8,128)(2,1)S(1)}, bf16[1,1,8,128,1440]{3,4,2,1,0:T(8,128)(2,1)}, u32[]{:S(2)}) copy-start(bf16[1,1,8,128,1440]{3,4,2,1,0:T(8,128)(2,1)} %param.13) | copy-start | bytes 8847364
  20.0 1.0 copy-start.2
  21.0 16.6 %copy-start.3 = (bf16[1456,128]{1,0:T(8,128)(2,1)S(1)}, bf16[1456,128]{1,0:T(8,128)(2,1)}, u32[]{:S(2)}) copy-start(bf16[1456,128]{1,0:T(8,128)(2,1)} %get-tuple-element.71.refs_0_) | copy-start | bytes 1118212
  21.5 16.0 %collective-permute-start.8 = (bf16[3,1456,128]{2,1,0:T(8,128)(2,1)S(1)}, bf16[3,1456,128]{2,1,0:T(8,128)(2,1)S(1)}, u32[]{:S(2)}, u32[]{:S(2)}) collective-permute-start(bf16[3,1456,128]{2,1,0:T(8,128)(2,1)S(1)} %collect.1), channel_id=1, source_target_pairs={{0,1},{1,0},{2,3},{3,2},{4,5},{5,4},{6,7},{7,6},{8,9},{9,8},{10,11... | collective-permute-start | bytes 3354632 | tf_op jit(solution)/shard_map/ppermute | solution.py:495
  21.6 14.2 %collective-permute-start.7 = (bf16[1456,128]{1,0:T(8,128)(2,1)S(1)}, bf16[1456,128]{1,0:T(8,128)(2,1)S(1)}, u32[]{:S(2)}, u32[]{:S(2)}) collective-permute-start(bf16[1456,128]{1,0:T(8,128)(2,1)S(1)} %copy-done.2), channel_id=1, source_target_pairs={{0,6},{1,7},{2,4},{3,5},{4,2},{5,3},{6,0},{7,1},{8,14},{9,15},{10,... | collective-permute-start | bytes 1118216 | tf_op jit(solution)/shard_map/ppermute | solution.py:490
  24.3 24.1 %collective-permute-start.4 = (bf16[1200,256]{1,0:T(8,128)(2,1)S(1)}, bf16[1200,256]{1,0:T(8,128)(2,1)S(1)}, u32[]{:S(2)}, u32[]{:S(2)}) collective-permute-start(bf16[1200,256]{1,0:T(8,128)(2,1)S(1)} %collective-permute-done.3.refs_0_.refs_1_), channel_id=1, source_target_pairs={{16,24},{8,0},{17,25},{9,1},{18,26},{10,2},{19,27},{11,3},{20,28},... | collective-permute-start | bytes 1843208 | tf_op jit(solution)/shard_map/ppermute | solution.py:377
  25.6 22.8 %collective-permute-start.5 = (bf16[1200,256]{1,0:T(8,128)(2,1)S(1)}, bf16[1200,256]{1,0:T(8,128)(2,1)S(1)}, u32[]{:S(2)}, u32[]{:S(2)}) collective-permute-start(bf16[1200,256]{1,0:T(8,128)(2,1)S(1)} %collective-permute-done.2.refs_0_), channel_id=1, source_target_pairs={{8,16},{16,8},{9,17},{17,9},{10,18},{18,10},{11,19},{19,11},{12,20... | collective-permute-start | bytes 1843208 | tf_op jit(solution)/shard_map/ppermute | solution.py:377
  26.3 22.1 %collective-permute-start.6 = (bf16[1152,256]{1,0:T(8,128)(2,1)S(1)}, bf16[1152,256]{1,0:T(8,128)(2,1)S(1)}, u32[]{:S(2)}, u32[]{:S(2)}) collective-permute-start(bf16[1152,256]{1,0:T(8,128)(2,1)S(1)} %pack_left.1.own_ref), channel_id=1, source_target_pairs={{0,8},{24,16},{1,9},{25,17},{2,10},{26,18},{3,11},{27,19},{4,12},{... | collective-permute-start | bytes 1769480 | tf_op jit(solution)/shard_map/ppermute | solution.py:500
  35.8 1.8 %collective-permute-start.9 = (bf16[1456,128]{1,0:T(8,128)(2,1)S(1)}, bf16[1456,128]{1,0:T(8,128)(2,1)S(1)}, u32[]{:S(2)}, u32[]{:S(2)}) collective-permute-start(bf16[1456,128]{1,0:T(8,128)(2,1)S(1)} %collective-permute-done.7.refs_3_), channel_id=1, source_target_pairs={{0,1},{1,0},{2,3},{3,2},{4,5},{5,4},{6,7},{7,6},{8,9},{9,8},{10,11... | collective-permute-start | bytes 1118216 | tf_op jit(solution)/shard_map/ppermute | solution.py:495
  48.4 18.7 %collective-permute-start.13 = (bf16[1200,256]{1,0:T(8,128)(2,1)S(1)}, bf16[1200,256]{1,0:T(8,128)(2,1)S(1)}, u32[]{:S(2)}, u32[]{:S(2)}) collective-permute-start(bf16[1200,256]{1,0:T(8,128)(2,1)S(1)} %collective-permute-done.5.refs_1_), channel_id=1, source_target_pairs={{16,24},{8,0},{17,25},{9,1},{18,26},{10,2},{19,27},{11,3},{20,28},... | collective-permute-start | bytes 1843208 | tf_op jit(solution)/shard_map/ppermute | solution.py:377
  49.7 16.7 %collective-permute-start.14 = (bf16[1152,256]{1,0:T(8,128)(2,1)S(1)}, bf16[1152,256]{1,0:T(8,128)(2,1)S(1)}, u32[]{:S(2)}, u32[]{:S(2)}) collective-permute-start(bf16[1152,256]{1,0:T(8,128)(2,1)S(1)} %pack_left.1.own_ref), channel_id=1, source_target_pairs={{8,16},{16,8},{9,17},{17,9},{10,18},{18,10},{11,19},{19,11},{12,20... | collective-permute-start | bytes 1769480 | tf_op jit(solution)/shard_map/ppermute | solution.py:509
  51.1 15.3 %collective-permute-start.12 = (bf16[1024,256]{1,0:T(8,128)(2,1)S(1)}, bf16[1024,256]{1,0:T(8,128)(2,1)S(1)}, u32[]{:S(2)}, u32[]{:S(2)}) collective-permute-start(bf16[1024,256]{1,0:T(8,128)(2,1)S(1)} %product.9), channel_id=1, source_target_pairs={{0,8},{24,16},{1,9},{25,17},{2,10},{26,18},{3,11},{27,19},{4,12},{... | collective-permute-start | bytes 1572872 | tf_op jit(solution)/shard_map/ppermute | solution.py:523
  56.5 23.2 %collective-permute-start.10 = (bf16[1152,256]{1,0:T(8,128)(2,1)S(1)}, bf16[1152,256]{1,0:T(8,128)(2,1)S(1)}, u32[]{:S(2)}, u32[]{:S(2)}) collective-permute-start(bf16[1152,256]{1,0:T(8,128)(2,1)S(1)} %pack_left.1.own_ref), channel_id=1, source_target_pairs={{16,24},{8,0},{17,25},{9,1},{18,26},{10,2},{19,27},{11,3},{20,28},... | collective-permute-start | bytes 1769480 | tf_op jit(solution)/shard_map/ppermute | solution.py:509
  57.8 21.9 %collective-permute-start.11 = (bf16[1152,256]{1,0:T(8,128)(2,1)S(1)}, bf16[1152,256]{1,0:T(8,128)(2,1)S(1)}, u32[]{:S(2)}, u32[]{:S(2)}) collective-permute-start(bf16[1152,256]{1,0:T(8,128)(2,1)S(1)} %collective-permute-done.6.ends_ref), channel_id=1, source_target_pairs={{8,16},{16,8},{9,17},{17,9},{10,18},{18,10},{11,19},{19,11},{12,20... | collective-permute-start | bytes 1769480 | tf_op jit(solution)/shard_map/ppermute | solution.py:509
  67.1 25.3 %collective-permute-start.19 = (bf16[1152,256]{1,0:T(8,128)(2,1)S(1)}, bf16[1152,256]{1,0:T(8,128)(2,1)S(1)}, u32[]{:S(2)}, u32[]{:S(2)}) collective-permute-start(bf16[1152,256]{1,0:T(8,128)(2,1)S(1)} %collective-permute-done.14.odd_ref), channel_id=1, source_target_pairs={{16,24},{8,0},{17,25},{9,1},{18,26},{10,2},{19,27},{11,3},{20,28},... | collective-permute-start | bytes 1769480 | tf_op jit(solution)/shard_map/ppermute | solution.py:509
  69.1 18.0 %collective-permute-start.18 = (bf16[1072,256]{1,0:T(8,128)(2,1)S(1)}, bf16[1072,256]{1,0:T(8,128)(2,1)S(1)}, u32[]{:S(2)}, u32[]{:S(2)}) collective-permute-start(bf16[1072,256]{1,0:T(8,128)(2,1)S(1)} %product.12), channel_id=1, source_target_pairs={{0,8},{24,16},{1,9},{25,17},{2,10},{26,18},{3,11},{27,19},{4,12},{... | collective-permute-start | bytes 1646600 | tf_op jit(solution)/shard_map/ppermute | solution.py:523
  74.6 22.3 %collective-permute-start.16 = (bf16[1024,256]{1,0:T(8,128)(2,1)S(1)}, bf16[1024,256]{1,0:T(8,128)(2,1)S(1)}, u32[]{:S(2)}, u32[]{:S(2)}) collective-permute-start(bf16[1024,256]{1,0:T(8,128)(2,1)S(1)} %add.6), channel_id=1, source_target_pairs={{8,16},{16,8},{9,17},{17,9},{10,18},{18,10},{11,19},{19,11},{12,20... | collective-permute-start | bytes 1572872 | tf_op jit(solution)/shard_map/ppermute | solution.py:523
  79.7 17.2 %collective-permute-start.15 = (bf16[1024,256]{1,0:T(8,128)(2,1)S(1)}, bf16[1024,256]{1,0:T(8,128)(2,1)S(1)}, u32[]{:S(2)}, u32[]{:S(2)}) collective-permute-start(bf16[1024,256]{1,0:T(8,128)(2,1)S(1)} %get-tuple-element.87), channel_id=1, source_target_pairs={{0,8},{24,16},{1,9},{25,17},{2,10},{26,18},{3,11},{27,19},{4,12},{... | collective-permute-start | bytes 1572872 | tf_op jit(solution)/shard_map/ppermute | solution.py:523
  85.1 18.0 %collective-permute-start.21 = (bf16[1152,256]{1,0:T(8,128)(2,1)S(1)}, bf16[1152,256]{1,0:T(8,128)(2,1)S(1)}, u32[]{:S(2)}, u32[]{:S(2)}) collective-permute-start(bf16[1152,256]{1,0:T(8,128)(2,1)S(1)} %collective-permute-done.11.refs_1_), channel_id=1, source_target_pairs={{16,24},{8,0},{17,25},{9,1},{18,26},{10,2},{19,27},{11,3},{20,28},... | collective-permute-start | bytes 1769480 | tf_op jit(solution)/shard_map/ppermute | solution.py:509
  92.4 10.7 %collective-permute-start.20 = (bf16[1072,256]{1,0:T(8,128)(2,1)S(1)}, bf16[1072,256]{1,0:T(8,128)(2,1)S(1)}, u32[]{:S(2)}, u32[]{:S(2)}) collective-permute-start(bf16[1072,256]{1,0:T(8,128)(2,1)S(1)} %add.7), channel_id=1, source_target_pairs={{8,16},{16,8},{9,17},{17,9},{10,18},{18,10},{11,19},{19,11},{12,20... | collective-permute-start | bytes 1646600 | tf_op jit(solution)/shard_map/ppermute | solution.py:523
  93.1 18.6 %collective-permute-start.24 = (bf16[1072,256]{1,0:T(8,128)(2,1)S(1)}, bf16[1072,256]{1,0:T(8,128)(2,1)S(1)}, u32[]{:S(2)}, u32[]{:S(2)}) collective-permute-start(bf16[1072,256]{1,0:T(8,128)(2,1)S(1)} %get-tuple-element.120), channel_id=1, source_target_pairs={{0,8},{24,16},{1,9},{25,17},{2,10},{26,18},{3,11},{27,19},{4,12},{... | collective-permute-start | bytes 1646600 | tf_op jit(solution)/shard_map/ppermute | solution.py:523
  97.0 14.7 %collective-permute-start.23 = (bf16[1024,256]{1,0:T(8,128)(2,1)S(1)}, bf16[1024,256]{1,0:T(8,128)(2,1)S(1)}, u32[]{:S(2)}, u32[]{:S(2)}) collective-permute-start(bf16[1024,256]{1,0:T(8,128)(2,1)S(1)} %add.9), channel_id=1, source_target_pairs={{8,16},{16,8},{9,17},{17,9},{10,18},{18,10},{11,19},{19,11},{12,20... | collective-permute-start | bytes 1572872 | tf_op jit(solution)/shard_map/ppermute | solution.py:523
  103.2 24.4 %collective-permute-start.22 = (bf16[1072,256]{1,0:T(8,128)(2,1)S(1)}, bf16[1072,256]{1,0:T(8,128)(2,1)S(1)}, u32[]{:S(2)}, u32[]{:S(2)}) collective-permute-start(bf16[1072,256]{1,0:T(8,128)(2,1)S(1)} %add.8), channel_id=1, source_target_pairs={{0,8},{8,0},{16,24},{24,16},{1,9},{9,1},{17,25},{25,17},{2,10},{10... | collective-permute-start | bytes 1646600 | tf_op jit(solution)/shard_map/ppermute | solution.py:523
  109.5 18.2 %collective-permute-start.17 = (bf16[1024,256]{1,0:T(8,128)(2,1)S(1)}, bf16[1024,256]{1,0:T(8,128)(2,1)S(1)}, u32[]{:S(2)}, u32[]{:S(2)}) collective-permute-start(bf16[1024,256]{1,0:T(8,128)(2,1)S(1)} %get-tuple-element.94), channel_id=1, source_target_pairs={{0,8},{24,16},{1,9},{25,17},{2,10},{26,18},{3,11},{27,19},{4,12},{... | collective-permute-start | bytes 1572872 | tf_op jit(solution)/shard_map/ppermute | solution.py:523
  111.7 2.2 %copy-start.1 = (bf16[1200,256]{1,0:T(8,128)(2,1)S(1)}, bf16[1200,256]{1,0:T(8,128)(2,1)}, u32[]{:S(2)}) copy-start(bf16[1200,256]{1,0:T(8,128)(2,1)} %get-tuple-element.78.refs_0_) | copy-start | bytes 1843204
  111.7 16.4 %collective-permute-start.26 = (bf16[1072,256]{1,0:T(8,128)(2,1)S(1)}, bf16[1072,256]{1,0:T(8,128)(2,1)S(1)}, u32[]{:S(2)}, u32[]{:S(2)}) collective-permute-start(bf16[1072,256]{1,0:T(8,128)(2,1)S(1)} %add.11), channel_id=1, source_target_pairs={{8,16},{16,8},{9,17},{17,9},{10,18},{18,10},{11,19},{19,11},{12,20... | collective-permute-start | bytes 1646600 | tf_op jit(solution)/shard_map/ppermute | solution.py:523
  112.6 15.6 %collective-permute-start.25 = (bf16[1024,256]{1,0:T(8,128)(2,1)S(1)}, bf16[1024,256]{1,0:T(8,128)(2,1)S(1)}, u32[]{:S(2)}, u32[]{:S(2)}) collective-permute-start(bf16[1024,256]{1,0:T(8,128)(2,1)S(1)} %add.10), channel_id=1, source_target_pairs={{8,0},{16,24},{9,1},{17,25},{10,2},{18,26},{11,3},{19,27},{12,4},{... | collective-permute-start | bytes 1572872 | tf_op jit(solution)/shard_map/ppermute | solution.py:523

commit v5 on v4

--- a/solution.py
+++ b/solution.py
@@ -316,7 +316,7 @@
                 out_ref[...] = value.astype(dtype)
 
 
-def total_kernel(chains, keys, *refs):
+def total_kernel(chains, keys, order_ref, *refs):
     got_refs = dict(zip(keys, refs[len(chains) :]))
     add_arrivals(chains, got_refs, refs[: len(chains)], refs[len(chains) + len(keys) :], F32)
 
@@ -561,9 +561,10 @@
         third, terms[1, 3] = wait([(1, 2, 1)], (), (third, terms[1, 3]))
         go(two, 3, 0)
         make(one, 4)
-        terms[0, 4], terms[1, 3] = wait([(0, 3, 1), (1, 2, 0)], (), (terms[0, 4], terms[1, 3]))
+        terms[1, 3] = wait([(1, 2, 0)], (), terms[1, 3])
+        go(two, 3, 1)
+        terms[0, 4] = wait([(0, 3, 1)], (), terms[0, 4])
         go(one, 4, 0)
-        go(two, 3, 1)
         lefts = [[left, left], [left_even, left_odd], second, [third, third]]
     else:
         for s in one.sets(2):
@@ -582,6 +583,8 @@
                 lefts.append(hop(t, wait([], (), lefts[-1])))
 
     left_inputs = [left, left_ends, left_rest, left_odd] + [item for pair in lefts[2:] for item in pair]
+    if n == 4:
+        left_inputs = wait([(0, 3, 0)], (), left_inputs)
     left_w, left_n = pl.pallas_call(
         functools.partial(left_kernel, left_root, n),
         in_specs=[ANY] * len(left_inputs),
@@ -591,7 +594,7 @@
         ),
         scratch_shapes=[pltpu.VMEM((n,) + left_root.shape, BF16), pltpu.SemaphoreType.DMA((n,))],
         compiler_params=params(32),
-        cost_estimate=cost(),
+        cost_estimate=cost(3),
         name="left",
     )(*left_inputs)
 
@@ -602,13 +605,13 @@
     own = wait(early, (left_w, left_n), own)
     totals = pl.pallas_call(
         functools.partial(total_kernel, chains, early),
-        in_specs=[VMEM] * (len(chains) + len(early)),
+        in_specs=[ANY] + [VMEM] * (len(chains) + len(early)),
         out_specs=[VMEM] * len(chains),
         out_shape=[jax.ShapeDtypeStruct(chain.fold.shape, F32) for chain in chains],
         compiler_params=params(32),
         cost_estimate=cost(3),
         name="total",
-    )(*own, *[sent[key] for key in early])
+    )(order.tick, *own, *[sent[key] for key in early])
     out_w, out_n = pl.pallas_call(
         functools.partial(final_kernel, chains, block, last),
         in_specs=[VMEM] * (len(chains) + len(last) + 2),

time: 132 us -> 141 us (1.068)
  local copies, waits for them, and re-layouts: 2.93 us -> 10.9 us
  waiting for transfers between devices: 47.3 us -> 44.1 us
  starting transfers between devices: 58.9 us -> 61.4 us
  Pallas kernels: 20.9 us -> 23 us
    unnamed x12 -> x30, local copies, waits for them, and re-layouts: 2.93 us -> 9.52 us
    ppermute x5, waiting for transfers between devices: 14.2 us -> 10.2 us  [hop_one(): return lax.ppermute(piece, 'dp', pairs) if pairs else piece]
    ppermute x11, starting transfers between devices: 31.2 us -> 33.7 us  [go(): sent[chain.half, t, s] = lax.ppermute(term, 'dp', chain.pairs(t, s))]
  transfers between devices with their start and end apart: 27 -> 27, of which waited for: 12 -> 11; matrix products, arithmetic and copies ran while one was open for 0% -> 1% of each run, Pallas kernels for 12% -> 12%
where the time goes in v5:
time: 141 us; the launch traced here: 140 us
  starting transfers between devices  61.4 us (44%)
  waiting for transfers between devices  44.1 us (31%)
  Pallas kernels  23 us (16%)
  local copies, waits for them, and re-layouts  10.9 us (8%)
    ppermute x11, starting transfers between devices, go(): sent[chain.half, t, s] = lax.ppermute(term, 'dp', chain.pairs(t, s))  33.7 us
    ppermute x11, waiting for transfers between devices, go(): sent[chain.half, t, s] = lax.ppermute(term, 'dp', chain.pairs(t, s))  19.8 us
    ppermute x5, waiting for transfers between devices, hop_one(): return lax.ppermute(piece, 'dp', pairs) if pairs else piece  10.2 us
    unnamed x30, local copies, waits for them, and re-layouts  9.52 us
    ppermute x1, starting transfers between devices, body(): left_ends = lax.ppermute(left, 'dp', ends)  9.51 us
    ppermute x5, starting transfers between devices, hop(): lax.ppermute(pieces[1 - s], 'dp', gather_pairs(k, s))  7.04 us
    pallas_call x1, Pallas kernels, partial(): pl.pallas_call(functools.partial(partial_kernel, topk, width, block, gap,...  6.63 us
    pallas_call x9, Pallas kernels, product(): pl.pallas_call(functools.partial(product_kernel, chain, t, keys, root, bl...  6.01 us
  transfers between devices with their start and end apart: 27, of which 11 were waited for; matrix products, arithmetic and copies ran while one was open for 1% of the time, Pallas kernels for 12%

profile of v5, /device:TPU:0, one launch (start us, length us, event | category | flops | bytes accessed | tf_op | source)
XLA Modules:
  0.0 140.5 jit_solution(12191233570068957390)
XLA Ops:
  0.6 2.2 %tokens.1 = (bf16[1456,128]{1,0:T(8,128)(2,1)}, bf16[1200,256]{1,0:T(8,128)(2,1)}) custom-call(bf16[1440,128]{1,0:T(8,128)(2,1)} %bitcast.17, bf16[4,128]{1,0:T(4,128)(2,1)} %bitcast.21, s32[4,128]{1,0:T(4,128)} %bitcast.20, s32[4,128]{1,0:T(4,128)} %bitcast.19, bf16[960,240]{1,0:T(8,128)(2,1)} %bitcast.16, bf16[480,120]{1,0:T(8,128)(2,1)} %bitcast.18), custom_call_target="tpu_custom_call" | custom-call | tf_op jit(solution)/shard_map/tokens/pallas_call | solution.py:381
  2.9 3.1 %collective-permute-start.2 = (bf16[1200,256]{1,0:T(8,128)(2,1)}, bf16[1200,256]{1,0:T(8,128)(2,1)S(1)}, u32[]{:S(2)}, u32[]{:S(2)}) collective-permute-start(bf16[1200,256]{1,0:T(8,128)(2,1)} %get-tuple-element.98.refs_0_), channel_id=1, source_target_pairs={{0,8},{16,24},{8,0},{24,16},{1,9},{17,25},{9,1},{25,17},{2,10},{18... | collective-permute-start | bytes 1843208 | tf_op jit(solution)/shard_map/ppermute | solution.py:377
  6.7 1.6 %collective-permute-start = (bf16[1456,128]{1,0:T(8,128)(2,1)}, bf16[1456,128]{1,0:T(8,128)(2,1)S(1)}, u32[]{:S(2)}, u32[]{:S(2)}) collective-permute-start(bf16[1456,128]{1,0:T(8,128)(2,1)} %get-tuple-element.92.refs_0_), channel_id=1, source_target_pairs={{0,2},{1,3},{2,0},{3,1},{4,6},{5,7},{6,4},{7,5},{8,10},{9,11},{10,... | collective-permute-start | bytes 1118216 | tf_op jit(solution)/shard_map/ppermute | solution.py:481
  8.2 1.5 %collective-permute-start.1 = (bf16[1456,128]{1,0:T(8,128)(2,1)}, bf16[1456,128]{1,0:T(8,128)(2,1)S(1)}, u32[]{:S(2)}, u32[]{:S(2)}) collective-permute-start(bf16[1456,128]{1,0:T(8,128)(2,1)} %get-tuple-element.92.refs_0_), channel_id=1, source_target_pairs={{0,4},{1,5},{2,6},{3,7},{4,0},{5,1},{6,2},{7,3},{8,12},{9,13},{10,... | collective-permute-start | bytes 1118216 | tf_op jit(solution)/shard_map/ppermute | solution.py:481
  9.7 1.0 copy-done.6
  10.8 0.9 copy-done.7
  12.4 4.7 %collective-permute-done.refs_1_ = bf16[1456,128]{1,0:T(8,128)(2,1)S(1)} collective-permute-done((bf16[1456,128]{1,0:T(8,128)(2,1)}, bf16[1456,128]{1,0:T(8,128)(2,1)S(1)}, u32[]{:S(2)}, u32[]{:S(2)}) %collective-permute-start) | collective-permute-done | bytes 372768 | tf_op jit(solution)/shard_map/ppermute | solution.py:481
  17.1 1.2 collective-permute-done.1.refs_2_
  18.3 1.7 %collective-permute-done.2.refs_0_ = bf16[1200,256]{1,0:T(8,128)(2,1)S(1)} collective-permute-done((bf16[1200,256]{1,0:T(8,128)(2,1)}, bf16[1200,256]{1,0:T(8,128)(2,1)S(1)}, u32[]{:S(2)}, u32[]{:S(2)}) %collective-permute-start.2) | collective-permute-done | bytes 614432 | tf_op jit(solution)/shard_map/ppermute | solution.py:377
  20.0 1.0 copy-done.2
  21.6 2.7 %collective-permute-start.7 = (bf16[1456,128]{1,0:T(8,128)(2,1)S(1)}, bf16[1456,128]{1,0:T(8,128)(2,1)S(1)}, u32[]{:S(2)}, u32[]{:S(2)}) collective-permute-start(bf16[1456,128]{1,0:T(8,128)(2,1)S(1)} %copy-done.2), channel_id=1, source_target_pairs={{0,6},{1,7},{2,4},{3,5},{4,2},{5,3},{6,0},{7,1},{8,14},{9,15},{10,... | collective-permute-start | bytes 1118216 | tf_op jit(solution)/shard_map/ppermute | solution.py:490
  24.3 1.3 collective-permute-start.4
  26.3 9.5 %collective-permute-start.6 = (bf16[1152,256]{1,0:T(8,128)(2,1)S(1)}, bf16[1152,256]{1,0:T(8,128)(2,1)S(1)}, u32[]{:S(2)}, u32[]{:S(2)}) collective-permute-start(bf16[1152,256]{1,0:T(8,128)(2,1)S(1)} %pack_left.1.own_ref), channel_id=1, source_target_pairs={{0,8},{24,16},{1,9},{25,17},{2,10},{26,18},{3,11},{27,19},{4,12},{... | collective-permute-start | bytes 1769480 | tf_op jit(solution)/shard_map/ppermute | solution.py:500
  35.9 1.7 %collective-permute-done.9.refs_5_ = bf16[1456,128]{1,0:T(8,128)(2,1)S(1)} collective-permute-done((bf16[1456,128]{1,0:T(8,128)(2,1)S(1)}, bf16[1456,128]{1,0:T(8,128)(2,1)S(1)}, u32[]{:S(2)}, u32[]{:S(2)}) %collective-permute-start.9) | collective-permute-done | bytes 372768 | tf_op jit(solution)/shard_map/ppermute | solution.py:495
  37.6 6.6 %partial.1.partial_ref = bf16[1440,1536]{1,0:T(8,128)(2,1)S(1)} custom-call(bf16[8,1440,128]{2,1,0:T(8,128)(2,1)S(1)} %bitcast.13, bf16[1456,128]{1,0:T(8,128)(2,1)S(1)} %copy-done.3, bf16[1456,128]{1,0:T(8,128)(2,1)S(1)} %collective-permute-done.refs_1_, bf16[1456,128]{1,0:T(8,128)(2,1)S(1)} %collective-permute-done.1.refs_2_, ...), custom_call_target="tpu_custom_call" | custom-call | tf_op jit(solution)/shard_map/partial/pallas_call | solution.py:435
  44.2 4.2 %collective-permute-done.6.ends_ref = bf16[1152,256]{1,0:T(8,128)(2,1)S(1)} collective-permute-done((bf16[1152,256]{1,0:T(8,128)(2,1)S(1)}, bf16[1152,256]{1,0:T(8,128)(2,1)S(1)}, u32[]{:S(2)}, u32[]{:S(2)}) %collective-permute-start.6) | collective-permute-done | bytes 589856 | tf_op jit(solution)/shard_map/ppermute | solution.py:500
  48.4 1.3 collective-permute-start.11
  51.1 5.4 %collective-permute-start.10 = (bf16[1024,256]{1,0:T(8,128)(2,1)S(1)}, bf16[1024,256]{1,0:T(8,128)(2,1)S(1)}, u32[]{:S(2)}, u32[]{:S(2)}) collective-permute-start(bf16[1024,256]{1,0:T(8,128)(2,1)S(1)} %product.9), channel_id=1, source_target_pairs={{0,8},{24,16},{1,9},{25,17},{2,10},{26,18},{3,11},{27,19},{4,12},{... | collective-permute-start | bytes 1572872 | tf_op jit(solution)/shard_map/ppermute | solution.py:523
  56.5 1.3 collective-permute-start.13
  58.6 7.9 %collective-permute-done.10.got_ref = bf16[1024,256]{1,0:T(8,128)(2,1)S(1)} collective-permute-done((bf16[1024,256]{1,0:T(8,128)(2,1)S(1)}, bf16[1024,256]{1,0:T(8,128)(2,1)S(1)}, u32[]{:S(2)}, u32[]{:S(2)}) %collective-permute-start.10) | collective-permute-done | bytes 524320 | tf_op jit(solution)/shard_map/ppermute | solution.py:523
  67.1 1.3 collective-permute-start.16
  68.4 0.8 product.11
  69.1 4.7 %collective-permute-start.15 = (bf16[1072,256]{1,0:T(8,128)(2,1)S(1)}, bf16[1072,256]{1,0:T(8,128)(2,1)S(1)}, u32[]{:S(2)}, u32[]{:S(2)}) collective-permute-start(bf16[1072,256]{1,0:T(8,128)(2,1)S(1)} %product.11), channel_id=1, source_target_pairs={{0,8},{24,16},{1,9},{25,17},{2,10},{26,18},{3,11},{27,19},{4,12},{... | collective-permute-start | bytes 1646600 | tf_op jit(solution)/shard_map/ppermute | solution.py:523
  74.6 5.1 %collective-permute-done.13.rest_ref = bf16[1152,256]{1,0:T(8,128)(2,1)S(1)} collective-permute-done((bf16[1152,256]{1,0:T(8,128)(2,1)S(1)}, bf16[1152,256]{1,0:T(8,128)(2,1)S(1)}, u32[]{:S(2)}, u32[]{:S(2)}) %collective-permute-start.13) | collective-permute-done | bytes 589856 | tf_op jit(solution)/shard_map/ppermute | solution.py:509
  80.4 4.9 %collective-permute-start.17 = (bf16[1024,256]{1,0:T(8,128)(2,1)S(1)}, bf16[1024,256]{1,0:T(8,128)(2,1)S(1)}, u32[]{:S(2)}, u32[]{:S(2)}) collective-permute-start(bf16[1024,256]{1,0:T(8,128)(2,1)S(1)} %get-tuple-element.117), channel_id=1, source_target_pairs={{0,8},{24,16},{1,9},{25,17},{2,10},{26,18},{3,11},{27,19},{4,12},{... | collective-permute-start | bytes 1572872 | tf_op jit(solution)/shard_map/ppermute | solution.py:523
  85.3 1.3 collective-permute-start.20
  86.6 0.8 product.12
  87.4 5.0 %collective-permute-done.16.refs_0_ = bf16[1152,256]{1,0:T(8,128)(2,1)S(1)} collective-permute-done((bf16[1152,256]{1,0:T(8,128)(2,1)S(1)}, bf16[1152,256]{1,0:T(8,128)(2,1)S(1)}, u32[]{:S(2)}, u32[]{:S(2)}) %collective-permute-start.16) | collective-permute-done | bytes 589856 | tf_op jit(solution)/shard_map/ppermute | solution.py:509
  93.1 3.1 %collective-permute-start.21 = (bf16[1072,256]{1,0:T(8,128)(2,1)S(1)}, bf16[1072,256]{1,0:T(8,128)(2,1)S(1)}, u32[]{:S(2)}, u32[]{:S(2)}) collective-permute-start(bf16[1072,256]{1,0:T(8,128)(2,1)S(1)} %get-tuple-element.129), channel_id=1, source_target_pairs={{0,8},{24,16},{1,9},{25,17},{2,10},{26,18},{3,11},{27,19},{4,12},{... | collective-permute-start | bytes 1646600 | tf_op jit(solution)/shard_map/ppermute | solution.py:523
  97.6 6.7 %collective-permute-start.23 = (bf16[1024,256]{1,0:T(8,128)(2,1)S(1)}, bf16[1024,256]{1,0:T(8,128)(2,1)S(1)}, u32[]{:S(2)}, u32[]{:S(2)}) collective-permute-start(bf16[1024,256]{1,0:T(8,128)(2,1)S(1)} %get-tuple-element.136), channel_id=1, source_target_pairs={{0,8},{24,16},{1,9},{25,17},{2,10},{26,18},{3,11},{27,19},{4,12},{... | collective-permute-start | bytes 1572872 | tf_op jit(solution)/shard_map/ppermute | solution.py:523
  104.3 0.8 product.14
  105.4 4.3 %collective-permute-start.24 = (bf16[1072,256]{1,0:T(8,128)(2,1)S(1)}, bf16[1072,256]{1,0:T(8,128)(2,1)S(1)}, u32[]{:S(2)}, u32[]{:S(2)}) collective-permute-start(bf16[1072,256]{1,0:T(8,128)(2,1)S(1)} %add.9), channel_id=1, source_target_pairs={{0,8},{8,0},{16,24},{24,16},{1,9},{9,1},{17,25},{25,17},{2,10},{10... | collective-permute-start | bytes 1646600 | tf_op jit(solution)/shard_map/ppermute | solution.py:523
  109.7 0.7 product.17.refs_1_
  111.2 0.8 copy-done.4
  112.0 1.5 %collective-permute-start.26 = (bf16[1072,256]{1,0:T(8,128)(2,1)S(1)}, bf16[1072,256]{1,0:T(8,128)(2,1)}, u32[]{:S(2)}, u32[]{:S(2)}) collective-permute-start(bf16[1072,256]{1,0:T(8,128)(2,1)S(1)} %add.11), channel_id=1, source_target_pairs={{8,16},{16,8},{9,17},{17,9},{10,18},{18,10},{11,19},{19,11},{12,20... | collective-permute-start | bytes 1646600 | tf_op jit(solution)/shard_map/ppermute | solution.py:523
  113.5 0.8 add.10
  114.3 1.3 collective-permute-start.25
  115.5 4.7 %collective-permute-done.23.refs_3_ = bf16[1024,256]{1,0:T(8,128)(2,1)S(1)} collective-permute-done((bf16[1024,256]{1,0:T(8,128)(2,1)S(1)}, bf16[1024,256]{1,0:T(8,128)(2,1)S(1)}, u32[]{:S(2)}, u32[]{:S(2)}) %collective-permute-start.23) | collective-permute-done | bytes 524320 | tf_op jit(solution)/shard_map/ppermute | solution.py:523
  120.2 1.6 %left.1 = (bf16[960,960]{1,0:T(8,128)(2,1)S(1)}, bf16[480,480]{1,0:T(8,128)(2,1)S(1)}) custom-call(bf16[1152,256]{1,0:T(8,128)(2,1)S(1)} %pack_left.1.own_ref, bf16[1152,256]{1,0:T(8,128)(2,1)S(1)} %collective-permute-done.6.ends_ref, bf16[1152,256]{1,0:T(8,128)(2,1)S(1)} %collective-permute-done.13.rest_ref, ...), custom_call_target="tpu_custom_call" | custom-call | flops 3449999872 | tf_op jit(solution)/shard_map/left/pallas_call | solution.py:588
  121.8 7.2 %collective-permute-done.24.refs_4_ = bf16[1072,256]{1,0:T(8,128)(2,1)S(1)} collective-permute-done((bf16[1072,256]{1,0:T(8,128)(2,1)S(1)}, bf16[1072,256]{1,0:T(8,128)(2,1)S(1)}, u32[]{:S(2)}, u32[]{:S(2)}) %collective-permute-start.24) | collective-permute-done | bytes 548896 | tf_op jit(solution)/shard_map/ppermute | solution.py:523
  129.0 0.8 copy-done.9
  129.8 1.4 copy.11.order_ref
  131.2 1.0 copy-done.5
  132.2 0.8 copy-done.8
  133.1 1.0 copy-done.10
  134.1 1.0 copy-done.12
  135.2 1.0 copy-done.14
  136.4 4.1 %final.1 = (f32[1440,240]{1,0:T(8,128)}, f32[1440,120]{1,0:T(8,128)}) custom-call(f32[1024,256]{1,0:T(8,128)S(1)} %get-tuple-element.160.refs_0_, f32[1072,256]{1,0:T(8,128)S(1)} %get-tuple-element.161.refs_1_, bf16[1024,256]{1,0:T(8,128)(2,1)} %collective-permute-done.25.refs_2_, bf16[1072,256]{1,0:T(8,128)(2,1)} %collective-permute-done.26.refs_3_, ...), custom_call_target="tpu_custom_call" | custom-call | tf_op jit(solution)/shard_map/final/pallas_call | solution.py:615
  (59 shorter events, 10.4 us)
Async XLA Ops:
  2.9 17.2 %collective-permute-start.2 = (bf16[1200,256]{1,0:T(8,128)(2,1)}, bf16[1200,256]{1,0:T(8,128)(2,1)S(1)}, u32[]{:S(2)}, u32[]{:S(2)}) collective-permute-start(bf16[1200,256]{1,0:T(8,128)(2,1)} %get-tuple-element.98.refs_0_), channel_id=1, source_target_pairs={{0,8},{16,24},{8,0},{24,16},{1,9},{17,25},{9,1},{25,17},{2,10},{18... | collective-permute-start | bytes 1843208 | tf_op jit(solution)/shard_map/ppermute | solution.py:377
  6.0 14.1 %collective-permute-start.3 = (bf16[1200,256]{1,0:T(8,128)(2,1)}, bf16[1200,256]{1,0:T(8,128)(2,1)S(1)}, u32[]{:S(2)}, u32[]{:S(2)}) collective-permute-start(bf16[1200,256]{1,0:T(8,128)(2,1)} %get-tuple-element.98.refs_0_), channel_id=1, source_target_pairs={{8,16},{16,8},{9,17},{17,9},{10,18},{18,10},{11,19},{19,11},{12,20... | collective-permute-start | bytes 1843208 | tf_op jit(solution)/shard_map/ppermute | solution.py:377
  6.7 10.4 %collective-permute-start = (bf16[1456,128]{1,0:T(8,128)(2,1)}, bf16[1456,128]{1,0:T(8,128)(2,1)S(1)}, u32[]{:S(2)}, u32[]{:S(2)}) collective-permute-start(bf16[1456,128]{1,0:T(8,128)(2,1)} %get-tuple-element.92.refs_0_), channel_id=1, source_target_pairs={{0,2},{1,3},{2,0},{3,1},{4,6},{5,7},{6,4},{7,5},{8,10},{9,11},{10,... | collective-permute-start | bytes 1118216 | tf_op jit(solution)/shard_map/ppermute | solution.py:481
  8.2 10.1 %collective-permute-start.1 = (bf16[1456,128]{1,0:T(8,128)(2,1)}, bf16[1456,128]{1,0:T(8,128)(2,1)S(1)}, u32[]{:S(2)}, u32[]{:S(2)}) collective-permute-start(bf16[1456,128]{1,0:T(8,128)(2,1)} %get-tuple-element.92.refs_0_), channel_id=1, source_target_pairs={{0,4},{1,5},{2,6},{3,7},{4,0},{5,1},{6,2},{7,3},{8,12},{9,13},{10,... | collective-permute-start | bytes 1118216 | tf_op jit(solution)/shard_map/ppermute | solution.py:481
  9.7 1.0 copy-start.6
  10.8 0.9 copy-start.7
  11.7 25.9 %copy-start = (bf16[1,1,8,128,1440]{3,4,2,1,0:T(8,128)(2,1)S(1)}, bf16[1,1,8,128,1440]{3,4,2,1,0:T(8,128)(2,1)}, u32[]{:S(2)}) copy-start(bf16[1,1,8,128,1440]{3,4,2,1,0:T(8,128)(2,1)} %param.13) | copy-start | bytes 8847364
  20.0 1.0 copy-start.2
  21.0 16.6 %copy-start.3 = (bf16[1456,128]{1,0:T(8,128)(2,1)S(1)}, bf16[1456,128]{1,0:T(8,128)(2,1)}, u32[]{:S(2)}) copy-start(bf16[1456,128]{1,0:T(8,128)(2,1)} %get-tuple-element.92.refs_0_) | copy-start | bytes 1118212
  21.5 16.0 %collective-permute-start.8 = (bf16[3,1456,128]{2,1,0:T(8,128)(2,1)S(1)}, bf16[3,1456,128]{2,1,0:T(8,128)(2,1)S(1)}, u32[]{:S(2)}, u32[]{:S(2)}) collective-permute-start(bf16[3,1456,128]{2,1,0:T(8,128)(2,1)S(1)} %collect.1), channel_id=1, source_target_pairs={{0,1},{1,0},{2,3},{3,2},{4,5},{5,4},{6,7},{7,6},{8,9},{9,8},{10,11... | collective-permute-start | bytes 3354632 | tf_op jit(solution)/shard_map/ppermute | solution.py:495
  21.6 14.2 %collective-permute-start.7 = (bf16[1456,128]{1,0:T(8,128)(2,1)S(1)}, bf16[1456,128]{1,0:T(8,128)(2,1)S(1)}, u32[]{:S(2)}, u32[]{:S(2)}) collective-permute-start(bf16[1456,128]{1,0:T(8,128)(2,1)S(1)} %copy-done.2), channel_id=1, source_target_pairs={{0,6},{1,7},{2,4},{3,5},{4,2},{5,3},{6,0},{7,1},{8,14},{9,15},{10,... | collective-permute-start | bytes 1118216 | tf_op jit(solution)/shard_map/ppermute | solution.py:490
  24.3 24.1 %collective-permute-start.4 = (bf16[1200,256]{1,0:T(8,128)(2,1)S(1)}, bf16[1200,256]{1,0:T(8,128)(2,1)S(1)}, u32[]{:S(2)}, u32[]{:S(2)}) collective-permute-start(bf16[1200,256]{1,0:T(8,128)(2,1)S(1)} %collective-permute-done.3.refs_0_.refs_1_), channel_id=1, source_target_pairs={{16,24},{8,0},{17,25},{9,1},{18,26},{10,2},{19,27},{11,3},{20,28},... | collective-permute-start | bytes 1843208 | tf_op jit(solution)/shard_map/ppermute | solution.py:377
  25.6 22.8 %collective-permute-start.5 = (bf16[1200,256]{1,0:T(8,128)(2,1)S(1)}, bf16[1200,256]{1,0:T(8,128)(2,1)S(1)}, u32[]{:S(2)}, u32[]{:S(2)}) collective-permute-start(bf16[1200,256]{1,0:T(8,128)(2,1)S(1)} %collective-permute-done.2.refs_0_), channel_id=1, source_target_pairs={{8,16},{16,8},{9,17},{17,9},{10,18},{18,10},{11,19},{19,11},{12,20... | collective-permute-start | bytes 1843208 | tf_op jit(solution)/shard_map/ppermute | solution.py:377
  26.3 22.1 %collective-permute-start.6 = (bf16[1152,256]{1,0:T(8,128)(2,1)S(1)}, bf16[1152,256]{1,0:T(8,128)(2,1)S(1)}, u32[]{:S(2)}, u32[]{:S(2)}) collective-permute-start(bf16[1152,256]{1,0:T(8,128)(2,1)S(1)} %pack_left.1.own_ref), channel_id=1, source_target_pairs={{0,8},{24,16},{1,9},{25,17},{2,10},{26,18},{3,11},{27,19},{4,12},{... | collective-permute-start | bytes 1769480 | tf_op jit(solution)/shard_map/ppermute | solution.py:500
  35.8 1.8 %collective-permute-start.9 = (bf16[1456,128]{1,0:T(8,128)(2,1)S(1)}, bf16[1456,128]{1,0:T(8,128)(2,1)S(1)}, u32[]{:S(2)}, u32[]{:S(2)}) collective-permute-start(bf16[1456,128]{1,0:T(8,128)(2,1)S(1)} %collective-permute-done.7.refs_3_), channel_id=1, source_target_pairs={{0,1},{1,0},{2,3},{3,2},{4,5},{5,4},{6,7},{7,6},{8,9},{9,8},{10,11... | collective-permute-start | bytes 1118216 | tf_op jit(solution)/shard_map/ppermute | solution.py:495
  48.4 18.7 %collective-permute-start.11 = (bf16[1200,256]{1,0:T(8,128)(2,1)S(1)}, bf16[1200,256]{1,0:T(8,128)(2,1)S(1)}, u32[]{:S(2)}, u32[]{:S(2)}) collective-permute-start(bf16[1200,256]{1,0:T(8,128)(2,1)S(1)} %collective-permute-done.5.refs_1_), channel_id=1, source_target_pairs={{16,24},{8,0},{17,25},{9,1},{18,26},{10,2},{19,27},{11,3},{20,28},... | collective-permute-start | bytes 1843208 | tf_op jit(solution)/shard_map/ppermute | solution.py:377
  49.7 16.7 %collective-permute-start.12 = (bf16[1152,256]{1,0:T(8,128)(2,1)S(1)}, bf16[1152,256]{1,0:T(8,128)(2,1)S(1)}, u32[]{:S(2)}, u32[]{:S(2)}) collective-permute-start(bf16[1152,256]{1,0:T(8,128)(2,1)S(1)} %pack_left.1.own_ref), channel_id=1, source_target_pairs={{8,16},{16,8},{9,17},{17,9},{10,18},{18,10},{11,19},{19,11},{12,20... | collective-permute-start | bytes 1769480 | tf_op jit(solution)/shard_map/ppermute | solution.py:509
  51.1 15.3 %collective-permute-start.10 = (bf16[1024,256]{1,0:T(8,128)(2,1)S(1)}, bf16[1024,256]{1,0:T(8,128)(2,1)S(1)}, u32[]{:S(2)}, u32[]{:S(2)}) collective-permute-start(bf16[1024,256]{1,0:T(8,128)(2,1)S(1)} %product.9), channel_id=1, source_target_pairs={{0,8},{24,16},{1,9},{25,17},{2,10},{26,18},{3,11},{27,19},{4,12},{... | collective-permute-start | bytes 1572872 | tf_op jit(solution)/shard_map/ppermute | solution.py:523
  56.5 23.2 %collective-permute-start.13 = (bf16[1152,256]{1,0:T(8,128)(2,1)S(1)}, bf16[1152,256]{1,0:T(8,128)(2,1)S(1)}, u32[]{:S(2)}, u32[]{:S(2)}) collective-permute-start(bf16[1152,256]{1,0:T(8,128)(2,1)S(1)} %pack_left.1.own_ref), channel_id=1, source_target_pairs={{16,24},{8,0},{17,25},{9,1},{18,26},{10,2},{19,27},{11,3},{20,28},... | collective-permute-start | bytes 1769480 | tf_op jit(solution)/shard_map/ppermute | solution.py:509
  57.8 21.9 %collective-permute-start.14 = (bf16[1152,256]{1,0:T(8,128)(2,1)S(1)}, bf16[1152,256]{1,0:T(8,128)(2,1)S(1)}, u32[]{:S(2)}, u32[]{:S(2)}) collective-permute-start(bf16[1152,256]{1,0:T(8,128)(2,1)S(1)} %collective-permute-done.6.ends_ref), channel_id=1, source_target_pairs={{8,16},{16,8},{9,17},{17,9},{10,18},{18,10},{11,19},{19,11},{12,20... | collective-permute-start | bytes 1769480 | tf_op jit(solution)/shard_map/ppermute | solution.py:509
  67.1 25.3 %collective-permute-start.16 = (bf16[1152,256]{1,0:T(8,128)(2,1)S(1)}, bf16[1152,256]{1,0:T(8,128)(2,1)S(1)}, u32[]{:S(2)}, u32[]{:S(2)}) collective-permute-start(bf16[1152,256]{1,0:T(8,128)(2,1)S(1)} %collective-permute-done.12.odd_ref), channel_id=1, source_target_pairs={{16,24},{8,0},{17,25},{9,1},{18,26},{10,2},{19,27},{11,3},{20,28},... | collective-permute-start | bytes 1769480 | tf_op jit(solution)/shard_map/ppermute | solution.py:509
  69.1 18.2 %collective-permute-start.15 = (bf16[1072,256]{1,0:T(8,128)(2,1)S(1)}, bf16[1072,256]{1,0:T(8,128)(2,1)S(1)}, u32[]{:S(2)}, u32[]{:S(2)}) collective-permute-start(bf16[1072,256]{1,0:T(8,128)(2,1)S(1)} %product.11), channel_id=1, source_target_pairs={{0,8},{24,16},{1,9},{25,17},{2,10},{26,18},{3,11},{27,19},{4,12},{... | collective-permute-start | bytes 1646600 | tf_op jit(solution)/shard_map/ppermute | solution.py:523
  79.7 17.1 %collective-permute-start.18 = (bf16[1024,256]{1,0:T(8,128)(2,1)S(1)}, bf16[1024,256]{1,0:T(8,128)(2,1)S(1)}, u32[]{:S(2)}, u32[]{:S(2)}) collective-permute-start(bf16[1024,256]{1,0:T(8,128)(2,1)S(1)} %add.6), channel_id=1, source_target_pairs={{8,16},{16,8},{9,17},{17,9},{10,18},{18,10},{11,19},{19,11},{12,20... | collective-permute-start | bytes 1572872 | tf_op jit(solution)/shard_map/ppermute | solution.py:523
  80.4 16.5 %collective-permute-start.17 = (bf16[1024,256]{1,0:T(8,128)(2,1)S(1)}, bf16[1024,256]{1,0:T(8,128)(2,1)S(1)}, u32[]{:S(2)}, u32[]{:S(2)}) collective-permute-start(bf16[1024,256]{1,0:T(8,128)(2,1)S(1)} %get-tuple-element.117), channel_id=1, source_target_pairs={{0,8},{24,16},{1,9},{25,17},{2,10},{26,18},{3,11},{27,19},{4,12},{... | collective-permute-start | bytes 1572872 | tf_op jit(solution)/shard_map/ppermute | solution.py:523
  85.3 19.8 %collective-permute-start.20 = (bf16[1152,256]{1,0:T(8,128)(2,1)S(1)}, bf16[1152,256]{1,0:T(8,128)(2,1)S(1)}, u32[]{:S(2)}, u32[]{:S(2)}) collective-permute-start(bf16[1152,256]{1,0:T(8,128)(2,1)S(1)} %collective-permute-done.14.refs_1_), channel_id=1, source_target_pairs={{16,24},{8,0},{17,25},{9,1},{18,26},{10,2},{19,27},{11,3},{20,28},... | collective-permute-start | bytes 1769480 | tf_op jit(solution)/shard_map/ppermute | solution.py:509
  92.4 12.7 %collective-permute-start.19 = (bf16[1072,256]{1,0:T(8,128)(2,1)S(1)}, bf16[1072,256]{1,0:T(8,128)(2,1)S(1)}, u32[]{:S(2)}, u32[]{:S(2)}) collective-permute-start(bf16[1072,256]{1,0:T(8,128)(2,1)S(1)} %add.7), channel_id=1, source_target_pairs={{8,16},{16,8},{9,17},{17,9},{10,18},{18,10},{11,19},{19,11},{12,20... | collective-permute-start | bytes 1646600 | tf_op jit(solution)/shard_map/ppermute | solution.py:523
  93.1 18.9 %collective-permute-start.21 = (bf16[1072,256]{1,0:T(8,128)(2,1)S(1)}, bf16[1072,256]{1,0:T(8,128)(2,1)S(1)}, u32[]{:S(2)}, u32[]{:S(2)}) collective-permute-start(bf16[1072,256]{1,0:T(8,128)(2,1)S(1)} %get-tuple-element.129), channel_id=1, source_target_pairs={{0,8},{24,16},{1,9},{25,17},{2,10},{26,18},{3,11},{27,19},{4,12},{... | collective-permute-start | bytes 1646600 | tf_op jit(solution)/shard_map/ppermute | solution.py:523
  96.9 8.2 %copy-start.11 = (bf16[1024,256]{1,0:T(8,128)(2,1)}, bf16[1024,256]{1,0:T(8,128)(2,1)S(1)}, u32[]{:S(2)}) copy-start(bf16[1024,256]{1,0:T(8,128)(2,1)S(1)} %collective-permute-done.18.refs_2_) | copy-start | bytes 1572868
  96.9 16.5 %collective-permute-start.22 = (bf16[1024,256]{1,0:T(8,128)(2,1)S(1)}, bf16[1024,256]{1,0:T(8,128)(2,1)S(1)}, u32[]{:S(2)}, u32[]{:S(2)}) collective-permute-start(bf16[1024,256]{1,0:T(8,128)(2,1)S(1)} %add.8), channel_id=1, source_target_pairs={{8,16},{16,8},{9,17},{17,9},{10,18},{18,10},{11,19},{19,11},{12,20... | collective-permute-start | bytes 1572872 | tf_op jit(solution)/shard_map/ppermute | solution.py:523
  97.6 22.6 %collective-permute-start.23 = (bf16[1024,256]{1,0:T(8,128)(2,1)S(1)}, bf16[1024,256]{1,0:T(8,128)(2,1)S(1)}, u32[]{:S(2)}, u32[]{:S(2)}) collective-permute-start(bf16[1024,256]{1,0:T(8,128)(2,1)S(1)} %get-tuple-element.136), channel_id=1, source_target_pairs={{0,8},{24,16},{1,9},{25,17},{2,10},{26,18},{3,11},{27,19},{4,12},{... | collective-permute-start | bytes 1572872 | tf_op jit(solution)/shard_map/ppermute | solution.py:523
  105.1 4.6 %copy-start.1 = (bf16[1200,256]{1,0:T(8,128)(2,1)S(1)}, bf16[1200,256]{1,0:T(8,128)(2,1)}, u32[]{:S(2)}) copy-start(bf16[1200,256]{1,0:T(8,128)(2,1)} %get-tuple-element.98.refs_0_) | copy-start | bytes 1843204
  105.4 23.5 %collective-permute-start.24 = (bf16[1072,256]{1,0:T(8,128)(2,1)S(1)}, bf16[1072,256]{1,0:T(8,128)(2,1)S(1)}, u32[]{:S(2)}, u32[]{:S(2)}) collective-permute-start(bf16[1072,256]{1,0:T(8,128)(2,1)S(1)} %add.9), channel_id=1, source_target_pairs={{0,8},{8,0},{16,24},{24,16},{1,9},{9,1},{17,25},{25,17},{2,10},{10... | collective-permute-start | bytes 1646600 | tf_op jit(solution)/shard_map/ppermute | solution.py:523
  111.2 0.8 copy-start.4
  112.0 24.4 %collective-permute-start.26 = (bf16[1072,256]{1,0:T(8,128)(2,1)S(1)}, bf16[1072,256]{1,0:T(8,128)(2,1)}, u32[]{:S(2)}, u32[]{:S(2)}) collective-permute-start(bf16[1072,256]{1,0:T(8,128)(2,1)S(1)} %add.11), channel_id=1, source_target_pairs={{8,16},{16,8},{9,17},{17,9},{10,18},{18,10},{11,19},{19,11},{12,20... | collective-permute-start | bytes 1646600 | tf_op jit(solution)/shard_map/ppermute | solution.py:523
  114.3 22.1 %collective-permute-start.25 = (bf16[1024,256]{1,0:T(8,128)(2,1)}, bf16[1024,256]{1,0:T(8,128)(2,1)}, u32[]{:S(2)}, u32[]{:S(2)}) collective-permute-start(bf16[1024,256]{1,0:T(8,128)(2,1)} %add.10), channel_id=1, source_target_pairs={{8,0},{16,24},{9,1},{17,25},{10,2},{18,26},{11,3},{19,27},{12,4},{... | collective-permute-start | bytes 1572872 | tf_op jit(solution)/shard_map/ppermute | solution.py:523
  120.2 1.6 %copy-start.13 = (bf16[1024,256]{1,0:T(8,128)(2,1)}, bf16[1024,256]{1,0:T(8,128)(2,1)S(1)}, u32[]{:S(2)}) copy-start(bf16[1024,256]{1,0:T(8,128)(2,1)S(1)} %collective-permute-done.23.refs_3_) | copy-start | bytes 1572868
  129.0 0.8 copy-start.9
  131.2 1.0 copy-start.5
  132.2 0.8 copy-start.8
  133.1 1.1 copy-start.10
  134.1 1.0 copy-start.12
  135.2 1.0 copy-start.14

commit v6 on v5

--- a/solution.py
+++ b/solution.py
@@ -230,7 +230,7 @@
         return found
 
 
-def product_kernel(chain, t, keys, root, block, gap, partial_ref, *refs):
+def product_kernel(chain, t, sets, keys, root, block, gap, partial_ref, *refs):
     root_refs = dict(zip(keys, refs))
     out_refs, piece_ref = refs[len(keys) : -1], refs[-1]
     z = lax.axis_index("dp")
@@ -249,7 +249,7 @@
     if t == 0:
         product(root_refs[0, 0], out_refs[0])
         return
-    for s, out_ref in zip(chain.sets(t), out_refs):
+    for s, out_ref in zip(sets, out_refs):
         by_far = {}
         for here in range(chain.n):
             far = chain.distance(t, here, s)
@@ -445,20 +445,20 @@
             name="partial",
         )(hidden, *mine, theirs_first, *theirs_later)
 
-    def product(chain, t, value, got):
+    def product(chain, t, value, got, sets=None, micros=0):
+        sets = sets or (chain.sets(t) if t else [0])
         keys = [(0, 0)]
         if t:
-            keys = sorted({(chain.distance(t, z, s), s) for z in range(n) for s in (0, 1)})
+            keys = sorted({(chain.distance(t, z, s), s) for z in range(n) for s in sets})
             keys = [key for key in keys if key[0]]
-        sets = chain.sets(t) if t else [0]
         made = pl.pallas_call(
-            functools.partial(product_kernel, chain, t, keys, root, block, gap),
+            functools.partial(product_kernel, chain, t, sets, keys, root, block, gap),
             in_specs=[VMEM] * (1 + len(keys)),
             out_specs=[VMEM] * len(sets),
             out_shape=[jax.ShapeDtypeStruct(chain.fold.shape, BF16)] * len(sets),
             scratch_shapes=[pltpu.VMEM(root.shape, BF16)],
             compiler_params=params(16),
-            cost_estimate=cost(),
+            cost_estimate=cost(micros),
             name="product",
         )(value, *[got[far][s] for far, s in keys])
         return dict(zip(sets, made))
@@ -474,7 +474,7 @@
             name="add",
         )(term, got)
 
-    order = Order(slots)
+    order = Order(slots.T)
     straight = [m for m in range(1, chips) if m & (m - 1) == 0]
     mine = {0: tok}
     for m in straight:
@@ -500,7 +500,7 @@
     left_ends = lax.ppermute(left, "dp", ends)
     theirs_later = [sibling(mine[m]) for m in later]
     value = partial(first, later, [mine[m] for m in first + later], theirs_first, theirs_later)
-    got, left, left_ends, value = order.gate((), (got, left, left_ends, value))
+    got, left, value = order.gate((), (got, left, value))
 
     one, two = chains
     sent, terms = {}, {}
@@ -508,8 +508,8 @@
     def hop_one(pairs, piece):
         return lax.ppermute(piece, "dp", pairs) if pairs else piece
 
-    def make(chain, t):
-        terms[chain.half, t] = product(chain, t, value, got)
+    def make(chain, t, sets=None, micros=0):
+        terms.setdefault((chain.half, t), {}).update(product(chain, t, value, got, sets, micros))
 
     def wait(keys, more=(), values=()):
         ready, _, values = order.gate((), ([sent[key] for key in keys], more, values))
@@ -529,6 +529,7 @@
         got.append(hop(k, got[-1]))
     left_odd = hop_one(gather_pairs(1, 1), left)
     left_rest = hop_one(others, left)
+    left_ends, value = wait([], (), (left_ends, value))
     inner = {target for _, target in ends}
     if all(pair[0] in inner for pair in gather_pairs(2, 1)):
         left_even = left_ends
@@ -538,20 +539,27 @@
     second = [None, hop_one(gather_pairs(2, 1), left_even)]
     own = [product(chain, 0, value, got)[0] for chain in chains]
 
-    got, value, left_odd = wait([(0, 1, s) for s in one.sets(1)], (), (got, value, left_odd))
+    if n == 4:
+        make(one, 2, [1], 4)
+        got, value, terms[0, 2] = wait([(0, 1, 0)], (), (got, value, terms[0, 2]))
+    else:
+        got, value, left_odd = wait([(0, 1, s) for s in one.sets(1)], (), (got, value, left_odd))
+        make(one, 2)
     make(two, 1)
-    make(one, 2)
     for s in two.sets(1):
         go(two, 1, s)
     if n == 4:
         go(one, 2, 1)
+        make(one, 2, [0])
+        left_rest, left_odd, terms[0, 2] = wait([], (), (left_rest, left_odd, terms[0, 2]))
+        go(one, 2, 0)
         second[0] = hop_one(gather_pairs(2, 0), left_odd)
-        left_rest, second[1], terms[0, 2] = wait([], (), (left_rest, second[1], terms[0, 2]))
-        go(one, 2, 0)
+        make(two, 2)
+        terms[1, 2] = wait([(1, 1, 0)], (), terms[1, 2])
+        go(two, 2, 1)
+        second[1] = wait([], (), second[1])
         third = hop_one(gather_pairs(3, 0), second[1])
-        make(two, 2)
-        second[0], terms[1, 2] = wait([(1, 1, 0)], (), (second[0], terms[1, 2]))
-        go(two, 2, 1)
+        second[0], terms[1, 2] = wait([], (), (second[0], terms[1, 2]))
         go(two, 2, 0)
         make(one, 3)
         terms[0, 3] = wait([(0, 2, 0), (0, 2, 1)], (), terms[0, 3])
@@ -583,8 +591,6 @@
                 lefts.append(hop(t, wait([], (), lefts[-1])))
 
     left_inputs = [left, left_ends, left_rest, left_odd] + [item for pair in lefts[2:] for item in pair]
-    if n == 4:
-        left_inputs = wait([(0, 3, 0)], (), left_inputs)
     left_w, left_n = pl.pallas_call(
         functools.partial(left_kernel, left_root, n),
         in_specs=[ANY] * len(left_inputs),
@@ -594,7 +600,7 @@
         ),
         scratch_shapes=[pltpu.VMEM((n,) + left_root.shape, BF16), pltpu.SemaphoreType.DMA((n,))],
         compiler_params=params(32),
-        cost_estimate=cost(3),
+        cost_estimate=cost(),
         name="left",
     )(*left_inputs)
 

time: 141 us -> 133 us (0.943)
  waiting for transfers between devices: 44.1 us -> 58.2 us
  starting transfers between devices: 61.4 us -> 49.6 us
  local copies, waits for them, and re-layouts: 10.9 us -> 2.94 us
  Pallas kernels: 23 us -> 20.9 us
    ppermute x5, waiting for transfers between devices: 10.2 us -> 22.9 us  [hop_one(): return lax.ppermute(piece, 'dp', pairs) if pairs else piece]
    ppermute x11, starting transfers between devices: 33.7 us -> 23.6 us  [go(): sent[chain.half, t, s] = lax.ppermute(term, 'dp', chain.pairs(t, s))]
    unnamed x30 -> x14, local copies, waits for them, and re-layouts: 9.52 us -> 2.94 us
    ppermute x1, waiting for transfers between devices: 4.17 us -> 0.01 us  [body(): left_ends = lax.ppermute(left, 'dp', ends)]
    ppermute x1, starting transfers between devices: 9.51 us -> 5.38 us  [body(): left_ends = lax.ppermute(left, 'dp', ends)]
    ppermute x5, waiting for transfers between devices: 2.4 us -> 6.31 us  [hop(): lax.ppermute(pieces[1 - s], 'dp', gather_pairs(k, s))]
    ppermute x5, starting transfers between devices: 7.04 us -> 9.83 us  [hop(): lax.ppermute(pieces[1 - s], 'dp', gather_pairs(k, s))]
    ppermute x1, waiting for transfers between devices: 0.01 us -> 2.1 us  [body(): lax.ppermute(mine[0], 'expert', [(i, i ^ 2 * m) for i in range(experts)])]
  transfers between devices with their start and end apart: 27 -> 27, of which waited for: 11 -> 13; matrix products, arithmetic and copies ran while one was open for 1% -> 0% of each run, Pallas kernels for 12% -> 12%
where the time goes in v6:
time: 133 us
  waiting for transfers between devices  58.2 us (44%)
  starting transfers between devices  49.6 us (37%)
  Pallas kernels  20.9 us (16%)
  local copies, waits for them, and re-layouts  2.94 us (2%)
    ppermute x11, starting transfers between devices, go(): sent[chain.half, t, s] = lax.ppermute(term, 'dp', chain.pairs(t, s))  23.6 us
    ppermute x5, waiting for transfers between devices, hop_one(): return lax.ppermute(piece, 'dp', pairs) if pairs else piece  22.9 us
    ppermute x11, waiting for transfers between devices, go(): sent[chain.half, t, s] = lax.ppermute(term, 'dp', chain.pairs(t, s))  19.6 us
    ppermute x5, starting transfers between devices, hop(): lax.ppermute(pieces[1 - s], 'dp', gather_pairs(k, s))  9.83 us
    pallas_call x1, Pallas kernels, partial(): pl.pallas_call(functools.partial(partial_kernel, topk, width, block, gap,...  6.63 us
    ppermute x5, waiting for transfers between devices, hop(): lax.ppermute(pieces[1 - s], 'dp', gather_pairs(k, s))  6.31 us
    pallas_call x10, Pallas kernels, product(): pl.pallas_call(functools.partial(product_kernel, chain, t, sets, keys, ro...  6 us
    ppermute x2, waiting for transfers between devices, body(): lax.ppermute(tok, 'expert', [(i, i ^ 2 * m) for i in range(experts)])  5.64 us
  transfers between devices with their start and end apart: 27, of which 13 were waited for; matrix products, arithmetic and copies ran while one was open for 0% of the time, Pallas kernels for 12%

profile of v6, /device:TPU:0, one launch (start us, length us, event | category | flops | bytes accessed | tf_op | source)
XLA Modules:
  0.0 132.8 jit_solution(2315257900246139233)
XLA Ops:
  0.6 2.2 %tokens.1 = (bf16[1456,128]{1,0:T(8,128)(2,1)}, bf16[1200,256]{1,0:T(8,128)(2,1)}) custom-call(bf16[1440,128]{1,0:T(8,128)(2,1)} %bitcast.19, bf16[4,128]{1,0:T(4,128)(2,1)} %bitcast.22, s32[4,128]{1,0:T(4,128)} %bitcast.21, s32[4,128]{1,0:T(4,128)} %bitcast.16, bf16[960,240]{1,0:T(8,128)(2,1)} %bitcast.18, bf16[480,120]{1,0:T(8,128)(2,1)} %bitcast.20), custom_call_target="tpu_custom_call" | custom-call | tf_op jit(solution)/shard_map/tokens/pallas_call | solution.py:381
  2.9 0.7 collective-permute-start.3
  3.6 5.9 %collective-permute-start.2 = (bf16[1200,256]{1,0:T(8,128)(2,1)}, bf16[1200,256]{1,0:T(8,128)(2,1)S(1)}, u32[]{:S(2)}, u32[]{:S(2)}) collective-permute-start(bf16[1200,256]{1,0:T(8,128)(2,1)} %get-tuple-element.93.refs_0_), channel_id=1, source_target_pairs={{0,8},{16,24},{8,0},{24,16},{1,9},{17,25},{9,1},{25,17},{2,10},{18... | collective-permute-start | bytes 1843208 | tf_op jit(solution)/shard_map/ppermute | solution.py:377
  9.5 1.5 %collective-permute-start.1 = (bf16[1456,128]{1,0:T(8,128)(2,1)}, bf16[1456,128]{1,0:T(8,128)(2,1)S(1)}, u32[]{:S(2)}, u32[]{:S(2)}) collective-permute-start(bf16[1456,128]{1,0:T(8,128)(2,1)} %get-tuple-element.86.refs_0_), channel_id=1, source_target_pairs={{0,4},{1,5},{2,6},{3,7},{4,0},{5,1},{6,2},{7,3},{8,12},{9,13},{10,... | collective-permute-start | bytes 1118216 | tf_op jit(solution)/shard_map/ppermute | solution.py:481
  11.0 1.5 %collective-permute-start = (bf16[1456,128]{1,0:T(8,128)(2,1)}, bf16[1456,128]{1,0:T(8,128)(2,1)S(1)}, u32[]{:S(2)}, u32[]{:S(2)}) collective-permute-start(bf16[1456,128]{1,0:T(8,128)(2,1)} %get-tuple-element.86.refs_0_), channel_id=1, source_target_pairs={{0,2},{1,3},{2,0},{3,1},{4,6},{5,7},{6,4},{7,5},{8,10},{9,11},{10,... | collective-permute-start | bytes 1118216 | tf_op jit(solution)/shard_map/ppermute | solution.py:481
  12.5 1.0 copy-done.4
  13.5 0.9 copy-done.5
  14.4 0.7 pack_left.1.own_ref
  15.1 4.4 %collective-permute-done.1.refs_2_ = bf16[1456,128]{1,0:T(8,128)(2,1)S(1)} collective-permute-done((bf16[1456,128]{1,0:T(8,128)(2,1)}, bf16[1456,128]{1,0:T(8,128)(2,1)S(1)}, u32[]{:S(2)}, u32[]{:S(2)}) %collective-permute-start.1) | collective-permute-done | bytes 372768 | tf_op jit(solution)/shard_map/ppermute | solution.py:481
  19.5 1.2 collective-permute-done.refs_1_
  20.8 2.5 %collective-permute-done.2.refs_0_ = bf16[1200,256]{1,0:T(8,128)(2,1)S(1)} collective-permute-done((bf16[1200,256]{1,0:T(8,128)(2,1)}, bf16[1200,256]{1,0:T(8,128)(2,1)S(1)}, u32[]{:S(2)}, u32[]{:S(2)}) %collective-permute-start.2) | collective-permute-done | bytes 614432 | tf_op jit(solution)/shard_map/ppermute | solution.py:377
  23.2 1.0 copy-done.2
  24.8 2.5 %collective-permute-start.6 = (bf16[1456,128]{1,0:T(8,128)(2,1)S(1)}, bf16[1456,128]{1,0:T(8,128)(2,1)S(1)}, u32[]{:S(2)}, u32[]{:S(2)}) collective-permute-start(bf16[1456,128]{1,0:T(8,128)(2,1)S(1)} %copy-done.2), channel_id=1, source_target_pairs={{0,6},{1,7},{2,4},{3,5},{4,2},{5,3},{6,0},{7,1},{8,14},{9,15},{10,... | collective-permute-start | bytes 1118216 | tf_op jit(solution)/shard_map/ppermute | solution.py:490
  28.0 1.3 collective-permute-start.4
  29.3 5.4 %collective-permute-start.9 = (bf16[1152,256]{1,0:T(8,128)(2,1)S(1)}, bf16[1152,256]{1,0:T(8,128)(2,1)S(1)}, u32[]{:S(2)}, u32[]{:S(2)}) collective-permute-start(bf16[1152,256]{1,0:T(8,128)(2,1)S(1)} %pack_left.1.own_ref), channel_id=1, source_target_pairs={{0,8},{24,16},{1,9},{25,17},{2,10},{26,18},{3,11},{27,19},{4,12},{... | collective-permute-start | bytes 1769480 | tf_op jit(solution)/shard_map/ppermute | solution.py:500
  34.7 2.1 %collective-permute-done.6.refs_3_ = bf16[1456,128]{1,0:T(8,128)(2,1)S(1)} collective-permute-done((bf16[1456,128]{1,0:T(8,128)(2,1)S(1)}, bf16[1456,128]{1,0:T(8,128)(2,1)S(1)}, u32[]{:S(2)}, u32[]{:S(2)}) %collective-permute-start.6) | collective-permute-done | bytes 372768 | tf_op jit(solution)/shard_map/ppermute | solution.py:490
  36.8 1.7 %collective-permute-done.8.refs_5_ = bf16[1456,128]{1,0:T(8,128)(2,1)S(1)} collective-permute-done((bf16[1456,128]{1,0:T(8,128)(2,1)S(1)}, bf16[1456,128]{1,0:T(8,128)(2,1)S(1)}, u32[]{:S(2)}, u32[]{:S(2)}) %collective-permute-start.8) | collective-permute-done | bytes 372768 | tf_op jit(solution)/shard_map/ppermute | solution.py:495
  38.5 6.6 %partial.1.partial_ref = bf16[1440,1536]{1,0:T(8,128)(2,1)S(1)} custom-call(bf16[8,1440,128]{2,1,0:T(8,128)(2,1)S(1)} %bitcast.13, bf16[1456,128]{1,0:T(8,128)(2,1)S(1)} %copy-done.3, bf16[1456,128]{1,0:T(8,128)(2,1)S(1)} %collective-permute-done.refs_1_, bf16[1456,128]{1,0:T(8,128)(2,1)S(1)} %collective-permute-done.1.refs_2_, ...), custom_call_target="tpu_custom_call" | custom-call | tf_op jit(solution)/shard_map/partial/pallas_call | solution.py:435
  45.2 1.4 %collective-permute-done.4.refs_0_ = bf16[1200,256]{1,0:T(8,128)(2,1)S(1)} collective-permute-done((bf16[1200,256]{1,0:T(8,128)(2,1)S(1)}, bf16[1200,256]{1,0:T(8,128)(2,1)S(1)}, u32[]{:S(2)}, u32[]{:S(2)}) %collective-permute-start.4) | collective-permute-done | bytes 614432 | tf_op jit(solution)/shard_map/ppermute | solution.py:377
  46.6 1.3 collective-permute-start.11
  47.9 0.7 product.10
  48.6 3.9 %collective-permute-start.10 = (bf16[1024,256]{1,0:T(8,128)(2,1)S(1)}, bf16[1024,256]{1,0:T(8,128)(2,1)S(1)}, u32[]{:S(2)}, u32[]{:S(2)}) collective-permute-start(bf16[1024,256]{1,0:T(8,128)(2,1)S(1)} %product.10), channel_id=1, source_target_pairs={{0,8},{24,16},{1,9},{25,17},{2,10},{26,18},{3,11},{27,19},{4,12},{... | collective-permute-start | bytes 1572872 | tf_op jit(solution)/shard_map/ppermute | solution.py:523
  52.5 0.7 collective-permute-start.13
  53.3 1.3 collective-permute-start.12
  55.3 7.6 %collective-permute-done.10.got_ref = bf16[1024,256]{1,0:T(8,128)(2,1)S(1)} collective-permute-done((bf16[1024,256]{1,0:T(8,128)(2,1)S(1)}, bf16[1024,256]{1,0:T(8,128)(2,1)S(1)}, u32[]{:S(2)}, u32[]{:S(2)}) %collective-permute-start.10) | collective-permute-done | bytes 524320 | tf_op jit(solution)/shard_map/ppermute | solution.py:523
  62.9 2.4 %collective-permute-done.11.refs_0_ = bf16[1200,256]{1,0:T(8,128)(2,1)S(1)} collective-permute-done((bf16[1200,256]{1,0:T(8,128)(2,1)S(1)}, bf16[1200,256]{1,0:T(8,128)(2,1)S(1)}, u32[]{:S(2)}, u32[]{:S(2)}) %collective-permute-start.11) | collective-permute-done | bytes 614432 | tf_op jit(solution)/shard_map/ppermute | solution.py:377
  65.3 0.7 product.13
  66.0 1.3 collective-permute-start.14
  67.4 0.7 product.12
  68.1 8.1 %collective-permute-done.12.rest_ref = bf16[1152,256]{1,0:T(8,128)(2,1)S(1)} collective-permute-done((bf16[1152,256]{1,0:T(8,128)(2,1)S(1)}, bf16[1152,256]{1,0:T(8,128)(2,1)S(1)}, u32[]{:S(2)}, u32[]{:S(2)}) %collective-permute-start.12) | collective-permute-done | bytes 589856 | tf_op jit(solution)/shard_map/ppermute | solution.py:509
  76.2 1.3 collective-permute-start.16
  77.5 4.7 %collective-permute-start.17 = (bf16[1024,256]{1,0:T(8,128)(2,1)S(1)}, bf16[1024,256]{1,0:T(8,128)(2,1)S(1)}, u32[]{:S(2)}, u32[]{:S(2)}) collective-permute-start(bf16[1024,256]{1,0:T(8,128)(2,1)S(1)} %product.12), channel_id=1, source_target_pairs={{0,8},{24,16},{1,9},{25,17},{2,10},{26,18},{3,11},{27,19},{4,12},{... | collective-permute-start | bytes 1572872 | tf_op jit(solution)/shard_map/ppermute | solution.py:523
  83.0 0.8 product.14
  83.8 1.3 collective-permute-start.20
  85.8 8.6 %collective-permute-done.16.refs_0_ = bf16[1152,256]{1,0:T(8,128)(2,1)S(1)} collective-permute-done((bf16[1152,256]{1,0:T(8,128)(2,1)S(1)}, bf16[1152,256]{1,0:T(8,128)(2,1)S(1)}, u32[]{:S(2)}, u32[]{:S(2)}) %collective-permute-start.16) | collective-permute-done | bytes 589856 | tf_op jit(solution)/shard_map/ppermute | solution.py:509
  94.4 1.5 %collective-permute-start.21 = (bf16[1072,256]{1,0:T(8,128)(2,1)S(1)}, bf16[1072,256]{1,0:T(8,128)(2,1)S(1)}, u32[]{:S(2)}, u32[]{:S(2)}) collective-permute-start(bf16[1072,256]{1,0:T(8,128)(2,1)S(1)} %get-tuple-element.127), channel_id=1, source_target_pairs={{0,8},{24,16},{1,9},{25,17},{2,10},{26,18},{3,11},{27,19},{4,12},{... | collective-permute-start | bytes 1646600 | tf_op jit(solution)/shard_map/ppermute | solution.py:523
  95.9 0.7 product.15
  97.4 0.8 product.16
  98.1 6.3 %collective-permute-done.20.refs_2_.refs_3_ = bf16[1152,256]{1,0:T(8,128)(2,1)S(1)} collective-permute-done((bf16[1152,256]{1,0:T(8,128)(2,1)S(1)}, bf16[1152,256]{1,0:T(8,128)(2,1)S(1)}, u32[]{:S(2)}, u32[]{:S(2)}) %collective-permute-start.20) | collective-permute-done | bytes 589856 | tf_op jit(solution)/shard_map/ppermute | solution.py:509
  104.5 5.8 %collective-permute-start.24 = (bf16[1072,256]{1,0:T(8,128)(2,1)S(1)}, bf16[1072,256]{1,0:T(8,128)(2,1)S(1)}, u32[]{:S(2)}, u32[]{:S(2)}) collective-permute-start(bf16[1072,256]{1,0:T(8,128)(2,1)S(1)} %add.9), channel_id=1, source_target_pairs={{0,8},{8,0},{16,24},{24,16},{1,9},{9,1},{17,25},{25,17},{2,10},{10... | collective-permute-start | bytes 1646600 | tf_op jit(solution)/shard_map/ppermute | solution.py:523
  110.4 2.1 %collective-permute-start.23 = (bf16[1024,256]{1,0:T(8,128)(2,1)S(1)}, bf16[1024,256]{1,0:T(8,128)(2,1)S(1)}, u32[]{:S(2)}, u32[]{:S(2)}) collective-permute-start(bf16[1024,256]{1,0:T(8,128)(2,1)S(1)} %get-tuple-element.135), channel_id=1, source_target_pairs={{0,8},{24,16},{1,9},{25,17},{2,10},{26,18},{3,11},{27,19},{4,12},{... | collective-permute-start | bytes 1572872 | tf_op jit(solution)/shard_map/ppermute | solution.py:523
  113.3 1.4 %collective-permute-start.25 = (bf16[1024,256]{1,0:T(8,128)(2,1)S(1)}, bf16[1024,256]{1,0:T(8,128)(2,1)S(1)}, u32[]{:S(2)}, u32[]{:S(2)}) collective-permute-start(bf16[1024,256]{1,0:T(8,128)(2,1)S(1)} %add.10), channel_id=1, source_target_pairs={{8,0},{16,24},{9,1},{17,25},{10,2},{18,26},{11,3},{19,27},{12,4},{... | collective-permute-start | bytes 1572872 | tf_op jit(solution)/shard_map/ppermute | solution.py:523
  114.7 0.7 product.18.refs_0_
  115.5 0.7 product.19.refs_1_
  116.2 1.6 %left.1 = (bf16[960,960]{1,0:T(8,128)(2,1)S(1)}, bf16[480,480]{1,0:T(8,128)(2,1)S(1)}) custom-call(bf16[1152,256]{1,0:T(8,128)(2,1)S(1)} %pack_left.1.own_ref, bf16[1152,256]{1,0:T(8,128)(2,1)S(1)} %collective-permute-done.9.ends_ref, bf16[1152,256]{1,0:T(8,128)(2,1)S(1)} %collective-permute-done.12.rest_ref, ...), custom_call_target="tpu_custom_call" | custom-call | tf_op jit(solution)/shard_map/left/pallas_call | solution.py:594
  117.8 9.9 %collective-permute-done.23.refs_3_ = bf16[1024,256]{1,0:T(8,128)(2,1)S(1)} collective-permute-done((bf16[1024,256]{1,0:T(8,128)(2,1)S(1)}, bf16[1024,256]{1,0:T(8,128)(2,1)S(1)}, u32[]{:S(2)}, u32[]{:S(2)}) %collective-permute-start.23) | collective-permute-done | bytes 524320 | tf_op jit(solution)/shard_map/ppermute | solution.py:523
  128.0 2.0 %collective-permute-done.25.refs_2_ = bf16[1024,256]{1,0:T(8,128)(2,1)S(1)} collective-permute-done((bf16[1024,256]{1,0:T(8,128)(2,1)S(1)}, bf16[1024,256]{1,0:T(8,128)(2,1)S(1)}, u32[]{:S(2)}, u32[]{:S(2)}) %collective-permute-start.25) | collective-permute-done | bytes 524320 | tf_op jit(solution)/shard_map/ppermute | solution.py:523
  130.0 2.9 %final.1 = (f32[1440,240]{1,0:T(8,128)}, f32[1440,120]{1,0:T(8,128)}) custom-call(f32[1024,256]{1,0:T(8,128)S(1)} %get-tuple-element.148.refs_0_, f32[1072,256]{1,0:T(8,128)S(1)} %get-tuple-element.149.refs_1_, bf16[1024,256]{1,0:T(8,128)(2,1)S(1)} %collective-permute-done.25.refs_2_, bf16[1072,256]{1,0:T(8,128)(2,1)S(1)} %collective-permute-done.26.refs_3_, ...), custom_call_target="tpu_custom_call" | custom-call | tf_op jit(solution)/shard_map/final/pallas_call | solution.py:621
  (43 shorter events, 5.2 us)
Async XLA Ops:
  2.9 17.9 %collective-permute-start.3 = (bf16[1200,256]{1,0:T(8,128)(2,1)}, bf16[1200,256]{1,0:T(8,128)(2,1)S(1)}, u32[]{:S(2)}, u32[]{:S(2)}) collective-permute-start(bf16[1200,256]{1,0:T(8,128)(2,1)} %get-tuple-element.93.refs_0_), channel_id=1, source_target_pairs={{8,16},{16,8},{9,17},{17,9},{10,18},{18,10},{11,19},{19,11},{12,20... | collective-permute-start | bytes 1843208 | tf_op jit(solution)/shard_map/ppermute | solution.py:377
  3.6 19.7 %collective-permute-start.2 = (bf16[1200,256]{1,0:T(8,128)(2,1)}, bf16[1200,256]{1,0:T(8,128)(2,1)S(1)}, u32[]{:S(2)}, u32[]{:S(2)}) collective-permute-start(bf16[1200,256]{1,0:T(8,128)(2,1)} %get-tuple-element.93.refs_0_), channel_id=1, source_target_pairs={{0,8},{16,24},{8,0},{24,16},{1,9},{17,25},{9,1},{25,17},{2,10},{18... | collective-permute-start | bytes 1843208 | tf_op jit(solution)/shard_map/ppermute | solution.py:377
  9.5 10.1 %collective-permute-start.1 = (bf16[1456,128]{1,0:T(8,128)(2,1)}, bf16[1456,128]{1,0:T(8,128)(2,1)S(1)}, u32[]{:S(2)}, u32[]{:S(2)}) collective-permute-start(bf16[1456,128]{1,0:T(8,128)(2,1)} %get-tuple-element.86.refs_0_), channel_id=1, source_target_pairs={{0,4},{1,5},{2,6},{3,7},{4,0},{5,1},{6,2},{7,3},{8,12},{9,13},{10,... | collective-permute-start | bytes 1118216 | tf_op jit(solution)/shard_map/ppermute | solution.py:481
  11.0 9.8 %collective-permute-start = (bf16[1456,128]{1,0:T(8,128)(2,1)}, bf16[1456,128]{1,0:T(8,128)(2,1)S(1)}, u32[]{:S(2)}, u32[]{:S(2)}) collective-permute-start(bf16[1456,128]{1,0:T(8,128)(2,1)} %get-tuple-element.86.refs_0_), channel_id=1, source_target_pairs={{0,2},{1,3},{2,0},{3,1},{4,6},{5,7},{6,4},{7,5},{8,10},{9,11},{10,... | collective-permute-start | bytes 1118216 | tf_op jit(solution)/shard_map/ppermute | solution.py:481
  12.5 1.0 copy-start.4
  13.5 0.9 copy-start.5
  14.4 24.1 %copy-start = (bf16[1,1,8,128,1440]{3,4,2,1,0:T(8,128)(2,1)S(1)}, bf16[1,1,8,128,1440]{3,4,2,1,0:T(8,128)(2,1)}, u32[]{:S(2)}) copy-start(bf16[1,1,8,128,1440]{3,4,2,1,0:T(8,128)(2,1)} %param.13) | copy-start | bytes 8847364
  23.2 1.0 copy-start.2
  24.2 14.3 %copy-start.3 = (bf16[1456,128]{1,0:T(8,128)(2,1)S(1)}, bf16[1456,128]{1,0:T(8,128)(2,1)}, u32[]{:S(2)}) copy-start(bf16[1456,128]{1,0:T(8,128)(2,1)} %get-tuple-element.86.refs_0_) | copy-start | bytes 1118212
  24.8 13.8 %collective-permute-start.7 = (bf16[3,1456,128]{2,1,0:T(8,128)(2,1)S(1)}, bf16[3,1456,128]{2,1,0:T(8,128)(2,1)S(1)}, u32[]{:S(2)}, u32[]{:S(2)}) collective-permute-start(bf16[3,1456,128]{2,1,0:T(8,128)(2,1)S(1)} %collect.1), channel_id=1, source_target_pairs={{0,1},{1,0},{2,3},{3,2},{4,5},{5,4},{6,7},{7,6},{8,9},{9,8},{10,11... | collective-permute-start | bytes 3354632 | tf_op jit(solution)/shard_map/ppermute | solution.py:495
  24.8 12.0 %collective-permute-start.6 = (bf16[1456,128]{1,0:T(8,128)(2,1)S(1)}, bf16[1456,128]{1,0:T(8,128)(2,1)S(1)}, u32[]{:S(2)}, u32[]{:S(2)}) collective-permute-start(bf16[1456,128]{1,0:T(8,128)(2,1)S(1)} %copy-done.2), channel_id=1, source_target_pairs={{0,6},{1,7},{2,4},{3,5},{4,2},{5,3},{6,0},{7,1},{8,14},{9,15},{10,... | collective-permute-start | bytes 1118216 | tf_op jit(solution)/shard_map/ppermute | solution.py:490
  27.3 17.8 %collective-permute-start.5 = (bf16[1200,256]{1,0:T(8,128)(2,1)S(1)}, bf16[1200,256]{1,0:T(8,128)(2,1)S(1)}, u32[]{:S(2)}, u32[]{:S(2)}) collective-permute-start(bf16[1200,256]{1,0:T(8,128)(2,1)S(1)} %collective-permute-done.2.refs_0_), channel_id=1, source_target_pairs={{8,16},{16,8},{9,17},{17,9},{10,18},{18,10},{11,19},{19,11},{12,20... | collective-permute-start | bytes 1843208 | tf_op jit(solution)/shard_map/ppermute | solution.py:377
  28.0 18.6 %collective-permute-start.4 = (bf16[1200,256]{1,0:T(8,128)(2,1)S(1)}, bf16[1200,256]{1,0:T(8,128)(2,1)S(1)}, u32[]{:S(2)}, u32[]{:S(2)}) collective-permute-start(bf16[1200,256]{1,0:T(8,128)(2,1)S(1)} %collective-permute-done.3.refs_0_.refs_1_), channel_id=1, source_target_pairs={{16,24},{8,0},{17,25},{9,1},{18,26},{10,2},{19,27},{11,3},{20,28},... | collective-permute-start | bytes 1843208 | tf_op jit(solution)/shard_map/ppermute | solution.py:377
  29.3 25.2 %collective-permute-start.9 = (bf16[1152,256]{1,0:T(8,128)(2,1)S(1)}, bf16[1152,256]{1,0:T(8,128)(2,1)S(1)}, u32[]{:S(2)}, u32[]{:S(2)}) collective-permute-start(bf16[1152,256]{1,0:T(8,128)(2,1)S(1)} %pack_left.1.own_ref), channel_id=1, source_target_pairs={{0,8},{24,16},{1,9},{25,17},{2,10},{26,18},{3,11},{27,19},{4,12},{... | collective-permute-start | bytes 1769480 | tf_op jit(solution)/shard_map/ppermute | solution.py:500
  36.8 1.7 %collective-permute-start.8 = (bf16[1456,128]{1,0:T(8,128)(2,1)S(1)}, bf16[1456,128]{1,0:T(8,128)(2,1)S(1)}, u32[]{:S(2)}, u32[]{:S(2)}) collective-permute-start(bf16[1456,128]{1,0:T(8,128)(2,1)S(1)} %collective-permute-done.6.refs_3_), channel_id=1, source_target_pairs={{0,1},{1,0},{2,3},{3,2},{4,5},{5,4},{6,7},{7,6},{8,9},{9,8},{10,11... | collective-permute-start | bytes 1118216 | tf_op jit(solution)/shard_map/ppermute | solution.py:495
  46.6 18.7 %collective-permute-start.11 = (bf16[1200,256]{1,0:T(8,128)(2,1)S(1)}, bf16[1200,256]{1,0:T(8,128)(2,1)S(1)}, u32[]{:S(2)}, u32[]{:S(2)}) collective-permute-start(bf16[1200,256]{1,0:T(8,128)(2,1)S(1)} %collective-permute-done.5.refs_1_), channel_id=1, source_target_pairs={{16,24},{8,0},{17,25},{9,1},{18,26},{10,2},{19,27},{11,3},{20,28},... | collective-permute-start | bytes 1843208 | tf_op jit(solution)/shard_map/ppermute | solution.py:377
  48.6 14.3 %collective-permute-start.10 = (bf16[1024,256]{1,0:T(8,128)(2,1)S(1)}, bf16[1024,256]{1,0:T(8,128)(2,1)S(1)}, u32[]{:S(2)}, u32[]{:S(2)}) collective-permute-start(bf16[1024,256]{1,0:T(8,128)(2,1)S(1)} %product.10), channel_id=1, source_target_pairs={{0,8},{24,16},{1,9},{25,17},{2,10},{26,18},{3,11},{27,19},{4,12},{... | collective-permute-start | bytes 1572872 | tf_op jit(solution)/shard_map/ppermute | solution.py:523
  52.5 15.6 %collective-permute-start.13 = (bf16[1152,256]{1,0:T(8,128)(2,1)S(1)}, bf16[1152,256]{1,0:T(8,128)(2,1)S(1)}, u32[]{:S(2)}, u32[]{:S(2)}) collective-permute-start(bf16[1152,256]{1,0:T(8,128)(2,1)S(1)} %pack_left.1.own_ref), channel_id=1, source_target_pairs={{8,16},{16,8},{9,17},{17,9},{10,18},{18,10},{11,19},{19,11},{12,20... | collective-permute-start | bytes 1769480 | tf_op jit(solution)/shard_map/ppermute | solution.py:509
  53.3 23.0 %collective-permute-start.12 = (bf16[1152,256]{1,0:T(8,128)(2,1)S(1)}, bf16[1152,256]{1,0:T(8,128)(2,1)S(1)}, u32[]{:S(2)}, u32[]{:S(2)}) collective-permute-start(bf16[1152,256]{1,0:T(8,128)(2,1)S(1)} %pack_left.1.own_ref), channel_id=1, source_target_pairs={{16,24},{8,0},{17,25},{9,1},{18,26},{10,2},{19,27},{11,3},{20,28},... | collective-permute-start | bytes 1769480 | tf_op jit(solution)/shard_map/ppermute | solution.py:509
  54.6 29.2 %collective-permute-start.15 = (bf16[1152,256]{1,0:T(8,128)(2,1)S(1)}, bf16[1152,256]{1,0:T(8,128)(2,1)S(1)}, u32[]{:S(2)}, u32[]{:S(2)}) collective-permute-start(bf16[1152,256]{1,0:T(8,128)(2,1)S(1)} %collective-permute-done.9.ends_ref), channel_id=1, source_target_pairs={{8,16},{16,8},{9,17},{17,9},{10,18},{18,10},{11,19},{19,11},{12,20... | collective-permute-start | bytes 1769480 | tf_op jit(solution)/shard_map/ppermute | solution.py:509
  66.0 17.7 %collective-permute-start.14 = (bf16[1072,256]{1,0:T(8,128)(2,1)S(1)}, bf16[1072,256]{1,0:T(8,128)(2,1)S(1)}, u32[]{:S(2)}, u32[]{:S(2)}) collective-permute-start(bf16[1072,256]{1,0:T(8,128)(2,1)S(1)} %product.13), channel_id=1, source_target_pairs={{0,8},{24,16},{1,9},{25,17},{2,10},{26,18},{3,11},{27,19},{4,12},{... | collective-permute-start | bytes 1646600 | tf_op jit(solution)/shard_map/ppermute | solution.py:523
  76.2 18.1 %collective-permute-start.16 = (bf16[1152,256]{1,0:T(8,128)(2,1)S(1)}, bf16[1152,256]{1,0:T(8,128)(2,1)S(1)}, u32[]{:S(2)}, u32[]{:S(2)}) collective-permute-start(bf16[1152,256]{1,0:T(8,128)(2,1)S(1)} %collective-permute-done.13.odd_ref), channel_id=1, source_target_pairs={{16,24},{8,0},{17,25},{9,1},{18,26},{10,2},{19,27},{11,3},{20,28},... | collective-permute-start | bytes 1769480 | tf_op jit(solution)/shard_map/ppermute | solution.py:509
  77.5 19.1 %collective-permute-start.17 = (bf16[1024,256]{1,0:T(8,128)(2,1)S(1)}, bf16[1024,256]{1,0:T(8,128)(2,1)S(1)}, u32[]{:S(2)}, u32[]{:S(2)}) collective-permute-start(bf16[1024,256]{1,0:T(8,128)(2,1)S(1)} %product.12), channel_id=1, source_target_pairs={{0,8},{24,16},{1,9},{25,17},{2,10},{26,18},{3,11},{27,19},{4,12},{... | collective-permute-start | bytes 1572872 | tf_op jit(solution)/shard_map/ppermute | solution.py:523
  82.3 14.3 %collective-permute-start.18 = (bf16[1024,256]{1,0:T(8,128)(2,1)S(1)}, bf16[1024,256]{1,0:T(8,128)(2,1)S(1)}, u32[]{:S(2)}, u32[]{:S(2)}) collective-permute-start(bf16[1024,256]{1,0:T(8,128)(2,1)S(1)} %add.6), channel_id=1, source_target_pairs={{8,16},{16,8},{9,17},{17,9},{10,18},{18,10},{11,19},{19,11},{12,20... | collective-permute-start | bytes 1572872 | tf_op jit(solution)/shard_map/ppermute | solution.py:523
  83.8 20.6 %collective-permute-start.20 = (bf16[1152,256]{1,0:T(8,128)(2,1)S(1)}, bf16[1152,256]{1,0:T(8,128)(2,1)S(1)}, u32[]{:S(2)}, u32[]{:S(2)}) collective-permute-start(bf16[1152,256]{1,0:T(8,128)(2,1)S(1)} %collective-permute-done.15.refs_1_), channel_id=1, source_target_pairs={{16,24},{8,0},{17,25},{9,1},{18,26},{10,2},{19,27},{11,3},{20,28},... | collective-permute-start | bytes 1769480 | tf_op jit(solution)/shard_map/ppermute | solution.py:509
  85.1 13.0 %collective-permute-start.19 = (bf16[1072,256]{1,0:T(8,128)(2,1)S(1)}, bf16[1072,256]{1,0:T(8,128)(2,1)S(1)}, u32[]{:S(2)}, u32[]{:S(2)}) collective-permute-start(bf16[1072,256]{1,0:T(8,128)(2,1)S(1)} %add.7), channel_id=1, source_target_pairs={{8,16},{16,8},{9,17},{17,9},{10,18},{18,10},{11,19},{19,11},{12,20... | collective-permute-start | bytes 1646600 | tf_op jit(solution)/shard_map/ppermute | solution.py:523
  94.4 18.1 %collective-permute-start.21 = (bf16[1072,256]{1,0:T(8,128)(2,1)S(1)}, bf16[1072,256]{1,0:T(8,128)(2,1)S(1)}, u32[]{:S(2)}, u32[]{:S(2)}) collective-permute-start(bf16[1072,256]{1,0:T(8,128)(2,1)S(1)} %get-tuple-element.127), channel_id=1, source_target_pairs={{0,8},{24,16},{1,9},{25,17},{2,10},{26,18},{3,11},{27,19},{4,12},{... | collective-permute-start | bytes 1646600 | tf_op jit(solution)/shard_map/ppermute | solution.py:523
  96.7 16.6 %collective-permute-start.22 = (bf16[1024,256]{1,0:T(8,128)(2,1)S(1)}, bf16[1024,256]{1,0:T(8,128)(2,1)S(1)}, u32[]{:S(2)}, u32[]{:S(2)}) collective-permute-start(bf16[1024,256]{1,0:T(8,128)(2,1)S(1)} %add.8), channel_id=1, source_target_pairs={{8,16},{16,8},{9,17},{17,9},{10,18},{18,10},{11,19},{19,11},{12,20... | collective-permute-start | bytes 1572872 | tf_op jit(solution)/shard_map/ppermute | solution.py:523
  104.5 23.2 %collective-permute-start.24 = (bf16[1072,256]{1,0:T(8,128)(2,1)S(1)}, bf16[1072,256]{1,0:T(8,128)(2,1)S(1)}, u32[]{:S(2)}, u32[]{:S(2)}) collective-permute-start(bf16[1072,256]{1,0:T(8,128)(2,1)S(1)} %add.9), channel_id=1, source_target_pairs={{0,8},{8,0},{16,24},{24,16},{1,9},{9,1},{17,25},{25,17},{2,10},{10... | collective-permute-start | bytes 1646600 | tf_op jit(solution)/shard_map/ppermute | solution.py:523
  110.4 17.4 %collective-permute-start.23 = (bf16[1024,256]{1,0:T(8,128)(2,1)S(1)}, bf16[1024,256]{1,0:T(8,128)(2,1)S(1)}, u32[]{:S(2)}, u32[]{:S(2)}) collective-permute-start(bf16[1024,256]{1,0:T(8,128)(2,1)S(1)} %get-tuple-element.135), channel_id=1, source_target_pairs={{0,8},{24,16},{1,9},{25,17},{2,10},{26,18},{3,11},{27,19},{4,12},{... | collective-permute-start | bytes 1572872 | tf_op jit(solution)/shard_map/ppermute | solution.py:523
  112.5 17.4 %collective-permute-start.26 = (bf16[1072,256]{1,0:T(8,128)(2,1)S(1)}, bf16[1072,256]{1,0:T(8,128)(2,1)S(1)}, u32[]{:S(2)}, u32[]{:S(2)}) collective-permute-start(bf16[1072,256]{1,0:T(8,128)(2,1)S(1)} %add.11), channel_id=1, source_target_pairs={{8,16},{16,8},{9,17},{17,9},{10,18},{18,10},{11,19},{19,11},{12,20... | collective-permute-start | bytes 1646600 | tf_op jit(solution)/shard_map/ppermute | solution.py:523
  113.3 1.5 %copy-start.1 = (bf16[1200,256]{1,0:T(8,128)(2,1)S(1)}, bf16[1200,256]{1,0:T(8,128)(2,1)}, u32[]{:S(2)}) copy-start(bf16[1200,256]{1,0:T(8,128)(2,1)} %get-tuple-element.93.refs_0_) | copy-start | bytes 1843204
  113.3 16.6 %collective-permute-start.25 = (bf16[1024,256]{1,0:T(8,128)(2,1)S(1)}, bf16[1024,256]{1,0:T(8,128)(2,1)S(1)}, u32[]{:S(2)}, u32[]{:S(2)}) collective-permute-start(bf16[1024,256]{1,0:T(8,128)(2,1)S(1)} %add.10), channel_id=1, source_target_pairs={{8,0},{16,24},{9,1},{17,25},{10,2},{18,26},{11,3},{19,27},{12,4},{... | collective-permute-start | bytes 1572872 | tf_op jit(solution)/shard_map/ppermute | solution.py:523
  116.2 11.6 %copy-start.6 = (s32[128,4]{0,1:T(4,128)S(1)}, s32[128,4]{0,1:T(4,128)}, u32[]{:S(2)}) copy-start(s32[128,4]{0,1:T(4,128)} %param.12) | copy-start | bytes 6148

commit v7 on v6

--- a/solution.py
+++ b/solution.py
@@ -559,16 +559,16 @@
         go(two, 2, 1)
         second[1] = wait([], (), second[1])
         third = hop_one(gather_pairs(3, 0), second[1])
-        second[0], terms[1, 2] = wait([], (), (second[0], terms[1, 2]))
         go(two, 2, 0)
         make(one, 3)
-        terms[0, 3] = wait([(0, 2, 0), (0, 2, 1)], (), terms[0, 3])
+        terms[0, 3], value = wait([(0, 2, 1)], (), (terms[0, 3], value))
+        make(one, 4, None, 1)
+        second[0], terms[0, 3], terms[0, 4] = wait([(0, 2, 0)], (), (second[0], terms[0, 3], terms[0, 4]))
         go(one, 3, 1)
         go(one, 3, 0)
         make(two, 3)
         third, terms[1, 3] = wait([(1, 2, 1)], (), (third, terms[1, 3]))
         go(two, 3, 0)
-        make(one, 4)
         terms[1, 3] = wait([(1, 2, 0)], (), terms[1, 3])
         go(two, 3, 1)
         terms[0, 4] = wait([(0, 3, 1)], (), terms[0, 4])

time: 133 us -> 131 us (0.985)
  waiting for transfers between devices: 58.2 us -> 51.3 us
  starting transfers between devices: 49.6 us -> 54.1 us
    ppermute x5, waiting for transfers between devices: 22.9 us -> 14.2 us  [hop_one(): return lax.ppermute(piece, 'dp', pairs) if pairs else piece]
    ppermute x11, starting transfers between devices: 23.6 us -> 28.1 us  [go(): sent[chain.half, t, s] = lax.ppermute(term, 'dp', chain.pairs(t, s))]
    ppermute x11, waiting for transfers between devices: 19.6 us -> 21.4 us  [go(): sent[chain.half, t, s] = lax.ppermute(term, 'dp', chain.pairs(t, s))]
  transfers between devices with their start and end apart: 27 -> 27, of which waited for: 13 -> 12; matrix products, arithmetic and copies ran while one was open for 0% -> 0% of each run, Pallas kernels for 12% -> 12%
where the time goes in v7:
time: 131 us
  starting transfers between devices  54.1 us (41%)
  waiting for transfers between devices  51.3 us (39%)
  Pallas kernels  21.1 us (16%)
  local copies, waits for them, and re-layouts  2.94 us (2%)
    ppermute x11, starting transfers between devices, go(): sent[chain.half, t, s] = lax.ppermute(term, 'dp', chain.pairs(t, s))  28.1 us
    ppermute x11, waiting for transfers between devices, go(): sent[chain.half, t, s] = lax.ppermute(term, 'dp', chain.pairs(t, s))  21.4 us
    ppermute x5, waiting for transfers between devices, hop_one(): return lax.ppermute(piece, 'dp', pairs) if pairs else piece  14.2 us
    ppermute x5, starting transfers between devices, hop(): lax.ppermute(pieces[1 - s], 'dp', gather_pairs(k, s))  9.83 us
    pallas_call x1, Pallas kernels, partial(): pl.pallas_call(functools.partial(partial_kernel, topk, width, block, gap,...  6.63 us
    ppermute x5, waiting for transfers between devices, hop(): lax.ppermute(pieces[1 - s], 'dp', gather_pairs(k, s))  6.31 us
    pallas_call x10, Pallas kernels, product(): pl.pallas_call(functools.partial(product_kernel, chain, t, sets, keys, ro...  6.19 us
    ppermute x2, waiting for transfers between devices, body(): lax.ppermute(tok, 'expert', [(i, i ^ 2 * m) for i in range(experts)])  5.64 us
  transfers between devices with their start and end apart: 27, of which 12 were waited for; matrix products, arithmetic and copies ran while one was open for 0% of the time, Pallas kernels for 12%

profile of v7, /device:TPU:0, one launch (start us, length us, event | category | flops | bytes accessed | tf_op | source)
XLA Modules:
  0.0 130.6 jit_solution(9869542733091790342)
XLA Ops:
  0.6 2.2 %tokens.1 = (bf16[1456,128]{1,0:T(8,128)(2,1)}, bf16[1200,256]{1,0:T(8,128)(2,1)}) custom-call(bf16[1440,128]{1,0:T(8,128)(2,1)} %bitcast.19, bf16[4,128]{1,0:T(4,128)(2,1)} %bitcast.22, s32[4,128]{1,0:T(4,128)} %bitcast.21, s32[4,128]{1,0:T(4,128)} %bitcast.16, bf16[960,240]{1,0:T(8,128)(2,1)} %bitcast.18, bf16[480,120]{1,0:T(8,128)(2,1)} %bitcast.20), custom_call_target="tpu_custom_call" | custom-call | tf_op jit(solution)/shard_map/tokens/pallas_call | solution.py:381
  2.9 0.7 collective-permute-start.3
  3.6 5.9 %collective-permute-start.2 = (bf16[1200,256]{1,0:T(8,128)(2,1)}, bf16[1200,256]{1,0:T(8,128)(2,1)S(1)}, u32[]{:S(2)}, u32[]{:S(2)}) collective-permute-start(bf16[1200,256]{1,0:T(8,128)(2,1)} %get-tuple-element.96.refs_0_), channel_id=1, source_target_pairs={{0,8},{16,24},{8,0},{24,16},{1,9},{17,25},{9,1},{25,17},{2,10},{18... | collective-permute-start | bytes 1843208 | tf_op jit(solution)/shard_map/ppermute | solution.py:377
  9.5 1.5 %collective-permute-start.1 = (bf16[1456,128]{1,0:T(8,128)(2,1)}, bf16[1456,128]{1,0:T(8,128)(2,1)S(1)}, u32[]{:S(2)}, u32[]{:S(2)}) collective-permute-start(bf16[1456,128]{1,0:T(8,128)(2,1)} %get-tuple-element.89.refs_0_), channel_id=1, source_target_pairs={{0,4},{1,5},{2,6},{3,7},{4,0},{5,1},{6,2},{7,3},{8,12},{9,13},{10,... | collective-permute-start | bytes 1118216 | tf_op jit(solution)/shard_map/ppermute | solution.py:481
  11.0 1.5 %collective-permute-start = (bf16[1456,128]{1,0:T(8,128)(2,1)}, bf16[1456,128]{1,0:T(8,128)(2,1)S(1)}, u32[]{:S(2)}, u32[]{:S(2)}) collective-permute-start(bf16[1456,128]{1,0:T(8,128)(2,1)} %get-tuple-element.89.refs_0_), channel_id=1, source_target_pairs={{0,2},{1,3},{2,0},{3,1},{4,6},{5,7},{6,4},{7,5},{8,10},{9,11},{10,... | collective-permute-start | bytes 1118216 | tf_op jit(solution)/shard_map/ppermute | solution.py:481
  12.5 1.0 copy-done.4
  13.5 0.9 copy-done.5
  14.4 0.7 pack_left.1.own_ref
  15.1 4.4 %collective-permute-done.1.refs_2_ = bf16[1456,128]{1,0:T(8,128)(2,1)S(1)} collective-permute-done((bf16[1456,128]{1,0:T(8,128)(2,1)}, bf16[1456,128]{1,0:T(8,128)(2,1)S(1)}, u32[]{:S(2)}, u32[]{:S(2)}) %collective-permute-start.1) | collective-permute-done | bytes 372768 | tf_op jit(solution)/shard_map/ppermute | solution.py:481
  19.5 1.2 collective-permute-done.refs_1_
  20.8 2.5 %collective-permute-done.2.refs_0_ = bf16[1200,256]{1,0:T(8,128)(2,1)S(1)} collective-permute-done((bf16[1200,256]{1,0:T(8,128)(2,1)}, bf16[1200,256]{1,0:T(8,128)(2,1)S(1)}, u32[]{:S(2)}, u32[]{:S(2)}) %collective-permute-start.2) | collective-permute-done | bytes 614432 | tf_op jit(solution)/shard_map/ppermute | solution.py:377
  23.2 1.0 copy-done.2
  24.8 2.5 %collective-permute-start.6 = (bf16[1456,128]{1,0:T(8,128)(2,1)S(1)}, bf16[1456,128]{1,0:T(8,128)(2,1)S(1)}, u32[]{:S(2)}, u32[]{:S(2)}) collective-permute-start(bf16[1456,128]{1,0:T(8,128)(2,1)S(1)} %copy-done.2), channel_id=1, source_target_pairs={{0,6},{1,7},{2,4},{3,5},{4,2},{5,3},{6,0},{7,1},{8,14},{9,15},{10,... | collective-permute-start | bytes 1118216 | tf_op jit(solution)/shard_map/ppermute | solution.py:490
  28.0 1.3 collective-permute-start.4
  29.3 5.4 %collective-permute-start.9 = (bf16[1152,256]{1,0:T(8,128)(2,1)S(1)}, bf16[1152,256]{1,0:T(8,128)(2,1)S(1)}, u32[]{:S(2)}, u32[]{:S(2)}) collective-permute-start(bf16[1152,256]{1,0:T(8,128)(2,1)S(1)} %pack_left.1.own_ref), channel_id=1, source_target_pairs={{0,8},{24,16},{1,9},{25,17},{2,10},{26,18},{3,11},{27,19},{4,12},{... | collective-permute-start | bytes 1769480 | tf_op jit(solution)/shard_map/ppermute | solution.py:500
  34.7 2.1 %collective-permute-done.6.refs_3_ = bf16[1456,128]{1,0:T(8,128)(2,1)S(1)} collective-permute-done((bf16[1456,128]{1,0:T(8,128)(2,1)S(1)}, bf16[1456,128]{1,0:T(8,128)(2,1)S(1)}, u32[]{:S(2)}, u32[]{:S(2)}) %collective-permute-start.6) | collective-permute-done | bytes 372768 | tf_op jit(solution)/shard_map/ppermute | solution.py:490
  36.8 1.7 %collective-permute-done.8.refs_5_ = bf16[1456,128]{1,0:T(8,128)(2,1)S(1)} collective-permute-done((bf16[1456,128]{1,0:T(8,128)(2,1)S(1)}, bf16[1456,128]{1,0:T(8,128)(2,1)S(1)}, u32[]{:S(2)}, u32[]{:S(2)}) %collective-permute-start.8) | collective-permute-done | bytes 372768 | tf_op jit(solution)/shard_map/ppermute | solution.py:495
  38.5 6.6 %partial.1.partial_ref = bf16[1440,1536]{1,0:T(8,128)(2,1)S(1)} custom-call(bf16[8,1440,128]{2,1,0:T(8,128)(2,1)S(1)} %bitcast.13, bf16[1456,128]{1,0:T(8,128)(2,1)S(1)} %copy-done.3, bf16[1456,128]{1,0:T(8,128)(2,1)S(1)} %collective-permute-done.refs_1_, bf16[1456,128]{1,0:T(8,128)(2,1)S(1)} %collective-permute-done.1.refs_2_, ...), custom_call_target="tpu_custom_call" | custom-call | tf_op jit(solution)/shard_map/partial/pallas_call | solution.py:435
  45.2 1.4 %collective-permute-done.4.refs_0_ = bf16[1200,256]{1,0:T(8,128)(2,1)S(1)} collective-permute-done((bf16[1200,256]{1,0:T(8,128)(2,1)S(1)}, bf16[1200,256]{1,0:T(8,128)(2,1)S(1)}, u32[]{:S(2)}, u32[]{:S(2)}) %collective-permute-start.4) | collective-permute-done | bytes 614432 | tf_op jit(solution)/shard_map/ppermute | solution.py:377
  46.6 1.3 collective-permute-start.11
  47.9 0.7 product.10
  48.6 3.9 %collective-permute-start.10 = (bf16[1024,256]{1,0:T(8,128)(2,1)S(1)}, bf16[1024,256]{1,0:T(8,128)(2,1)S(1)}, u32[]{:S(2)}, u32[]{:S(2)}) collective-permute-start(bf16[1024,256]{1,0:T(8,128)(2,1)S(1)} %product.10), channel_id=1, source_target_pairs={{0,8},{24,16},{1,9},{25,17},{2,10},{26,18},{3,11},{27,19},{4,12},{... | collective-permute-start | bytes 1572872 | tf_op jit(solution)/shard_map/ppermute | solution.py:523
  52.5 0.7 collective-permute-start.13
  53.3 1.3 collective-permute-start.12
  54.6 0.7 collective-permute-start.15
  55.3 7.6 %collective-permute-done.10.got_ref = bf16[1024,256]{1,0:T(8,128)(2,1)S(1)} collective-permute-done((bf16[1024,256]{1,0:T(8,128)(2,1)S(1)}, bf16[1024,256]{1,0:T(8,128)(2,1)S(1)}, u32[]{:S(2)}, u32[]{:S(2)}) %collective-permute-start.10) | collective-permute-done | bytes 524320 | tf_op jit(solution)/shard_map/ppermute | solution.py:523
  62.9 2.4 %collective-permute-done.11.refs_0_ = bf16[1200,256]{1,0:T(8,128)(2,1)S(1)} collective-permute-done((bf16[1200,256]{1,0:T(8,128)(2,1)S(1)}, bf16[1200,256]{1,0:T(8,128)(2,1)S(1)}, u32[]{:S(2)}, u32[]{:S(2)}) %collective-permute-start.11) | collective-permute-done | bytes 614432 | tf_op jit(solution)/shard_map/ppermute | solution.py:377
  65.3 0.7 product.13
  66.0 1.3 %collective-permute-start.14 = (bf16[1072,256]{1,0:T(8,128)(2,1)S(1)}, bf16[1072,256]{1,0:T(8,128)(2,1)S(1)}, u32[]{:S(2)}, u32[]{:S(2)}) collective-permute-start(bf16[1072,256]{1,0:T(8,128)(2,1)S(1)} %product.13), channel_id=1, source_target_pairs={{0,8},{24,16},{1,9},{25,17},{2,10},{26,18},{3,11},{27,19},{4,12},{... | collective-permute-start | bytes 1646600 | tf_op jit(solution)/shard_map/ppermute | solution.py:523
  68.1 0.7 product.12
  68.9 7.4 %collective-permute-done.12.rest_ref = bf16[1152,256]{1,0:T(8,128)(2,1)S(1)} collective-permute-done((bf16[1152,256]{1,0:T(8,128)(2,1)S(1)}, bf16[1152,256]{1,0:T(8,128)(2,1)S(1)}, u32[]{:S(2)}, u32[]{:S(2)}) %collective-permute-start.12) | collective-permute-done | bytes 589856 | tf_op jit(solution)/shard_map/ppermute | solution.py:509
  76.2 1.3 collective-permute-start.18
  77.5 4.6 %collective-permute-start.17 = (bf16[1024,256]{1,0:T(8,128)(2,1)S(1)}, bf16[1024,256]{1,0:T(8,128)(2,1)S(1)}, u32[]{:S(2)}, u32[]{:S(2)}) collective-permute-start(bf16[1024,256]{1,0:T(8,128)(2,1)S(1)} %product.12), channel_id=1, source_target_pairs={{0,8},{24,16},{1,9},{25,17},{2,10},{26,18},{3,11},{27,19},{4,12},{... | collective-permute-start | bytes 1572872 | tf_op jit(solution)/shard_map/ppermute | solution.py:523
  82.1 0.8 product.14
  82.9 1.3 collective-permute-start.20
  85.0 0.7 product.15
  85.7 10.1 %collective-permute-start.21 = (bf16[1072,256]{1,0:T(8,128)(2,1)S(1)}, bf16[1072,256]{1,0:T(8,128)(2,1)S(1)}, u32[]{:S(2)}, u32[]{:S(2)}) collective-permute-start(bf16[1072,256]{1,0:T(8,128)(2,1)S(1)} %get-tuple-element.132), channel_id=1, source_target_pairs={{0,8},{24,16},{1,9},{25,17},{2,10},{26,18},{3,11},{27,19},{4,12},{... | collective-permute-start | bytes 1646600 | tf_op jit(solution)/shard_map/ppermute | solution.py:523
  96.6 0.9 product.17
  97.6 6.8 %collective-permute-done.20.refs_2_.refs_3_ = bf16[1152,256]{1,0:T(8,128)(2,1)S(1)} collective-permute-done((bf16[1152,256]{1,0:T(8,128)(2,1)S(1)}, bf16[1152,256]{1,0:T(8,128)(2,1)S(1)}, u32[]{:S(2)}, u32[]{:S(2)}) %collective-permute-start.20) | collective-permute-done | bytes 589856 | tf_op jit(solution)/shard_map/ppermute | solution.py:509
  104.5 1.4 %collective-permute-start.24 = (bf16[1072,256]{1,0:T(8,128)(2,1)S(1)}, bf16[1072,256]{1,0:T(8,128)(2,1)S(1)}, u32[]{:S(2)}, u32[]{:S(2)}) collective-permute-start(bf16[1072,256]{1,0:T(8,128)(2,1)S(1)} %add.9), channel_id=1, source_target_pairs={{0,8},{8,0},{16,24},{24,16},{1,9},{9,1},{17,25},{25,17},{2,10},{10... | collective-permute-start | bytes 1646600 | tf_op jit(solution)/shard_map/ppermute | solution.py:523
  105.9 2.6 %collective-permute-start.23 = (bf16[1024,256]{1,0:T(8,128)(2,1)S(1)}, bf16[1024,256]{1,0:T(8,128)(2,1)S(1)}, u32[]{:S(2)}, u32[]{:S(2)}) collective-permute-start(bf16[1024,256]{1,0:T(8,128)(2,1)S(1)} %get-tuple-element.141), channel_id=1, source_target_pairs={{0,8},{24,16},{1,9},{25,17},{2,10},{26,18},{3,11},{27,19},{4,12},{... | collective-permute-start | bytes 1572872 | tf_op jit(solution)/shard_map/ppermute | solution.py:523
  108.6 0.7 collective-permute-start.26
  109.3 1.3 collective-permute-start.25
  110.7 0.7 product.18.refs_0_
  111.4 0.8 product.19.refs_1_
  112.2 1.6 %left.1 = (bf16[960,960]{1,0:T(8,128)(2,1)S(1)}, bf16[480,480]{1,0:T(8,128)(2,1)S(1)}) custom-call(bf16[1152,256]{1,0:T(8,128)(2,1)S(1)} %pack_left.1.own_ref, bf16[1152,256]{1,0:T(8,128)(2,1)S(1)} %collective-permute-done.9.ends_ref, bf16[1152,256]{1,0:T(8,128)(2,1)S(1)} %collective-permute-done.12.rest_ref, ...), custom_call_target="tpu_custom_call" | custom-call | tf_op jit(solution)/shard_map/left/pallas_call | solution.py:594
  113.7 13.1 %collective-permute-done.23.refs_3_ = bf16[1024,256]{1,0:T(8,128)(2,1)S(1)} collective-permute-done((bf16[1024,256]{1,0:T(8,128)(2,1)S(1)}, bf16[1024,256]{1,0:T(8,128)(2,1)S(1)}, u32[]{:S(2)}, u32[]{:S(2)}) %collective-permute-start.23) | collective-permute-done | bytes 524320 | tf_op jit(solution)/shard_map/ppermute | solution.py:523
  127.7 2.9 %final.1 = (f32[1440,240]{1,0:T(8,128)}, f32[1440,120]{1,0:T(8,128)}) custom-call(f32[1024,256]{1,0:T(8,128)S(1)} %get-tuple-element.154.refs_0_, f32[1072,256]{1,0:T(8,128)S(1)} %get-tuple-element.155.refs_1_, bf16[1024,256]{1,0:T(8,128)(2,1)S(1)} %collective-permute-done.25.refs_2_, bf16[1072,256]{1,0:T(8,128)(2,1)S(1)} %collective-permute-done.26.refs_3_, ...), custom_call_target="tpu_custom_call" | custom-call | tf_op jit(solution)/shard_map/final/pallas_call | solution.py:621
  (43 shorter events, 4.5 us)
Async XLA Ops:
  2.9 17.9 %collective-permute-start.3 = (bf16[1200,256]{1,0:T(8,128)(2,1)}, bf16[1200,256]{1,0:T(8,128)(2,1)S(1)}, u32[]{:S(2)}, u32[]{:S(2)}) collective-permute-start(bf16[1200,256]{1,0:T(8,128)(2,1)} %get-tuple-element.96.refs_0_), channel_id=1, source_target_pairs={{8,16},{16,8},{9,17},{17,9},{10,18},{18,10},{11,19},{19,11},{12,20... | collective-permute-start | bytes 1843208 | tf_op jit(solution)/shard_map/ppermute | solution.py:377
  3.6 19.7 %collective-permute-start.2 = (bf16[1200,256]{1,0:T(8,128)(2,1)}, bf16[1200,256]{1,0:T(8,128)(2,1)S(1)}, u32[]{:S(2)}, u32[]{:S(2)}) collective-permute-start(bf16[1200,256]{1,0:T(8,128)(2,1)} %get-tuple-element.96.refs_0_), channel_id=1, source_target_pairs={{0,8},{16,24},{8,0},{24,16},{1,9},{17,25},{9,1},{25,17},{2,10},{18... | collective-permute-start | bytes 1843208 | tf_op jit(solution)/shard_map/ppermute | solution.py:377
  9.5 10.1 %collective-permute-start.1 = (bf16[1456,128]{1,0:T(8,128)(2,1)}, bf16[1456,128]{1,0:T(8,128)(2,1)S(1)}, u32[]{:S(2)}, u32[]{:S(2)}) collective-permute-start(bf16[1456,128]{1,0:T(8,128)(2,1)} %get-tuple-element.89.refs_0_), channel_id=1, source_target_pairs={{0,4},{1,5},{2,6},{3,7},{4,0},{5,1},{6,2},{7,3},{8,12},{9,13},{10,... | collective-permute-start | bytes 1118216 | tf_op jit(solution)/shard_map/ppermute | solution.py:481
  11.0 9.8 %collective-permute-start = (bf16[1456,128]{1,0:T(8,128)(2,1)}, bf16[1456,128]{1,0:T(8,128)(2,1)S(1)}, u32[]{:S(2)}, u32[]{:S(2)}) collective-permute-start(bf16[1456,128]{1,0:T(8,128)(2,1)} %get-tuple-element.89.refs_0_), channel_id=1, source_target_pairs={{0,2},{1,3},{2,0},{3,1},{4,6},{5,7},{6,4},{7,5},{8,10},{9,11},{10,... | collective-permute-start | bytes 1118216 | tf_op jit(solution)/shard_map/ppermute | solution.py:481
  12.5 1.0 copy-start.4
  13.5 0.9 copy-start.5
  14.4 24.1 %copy-start = (bf16[1,1,8,128,1440]{3,4,2,1,0:T(8,128)(2,1)S(1)}, bf16[1,1,8,128,1440]{3,4,2,1,0:T(8,128)(2,1)}, u32[]{:S(2)}) copy-start(bf16[1,1,8,128,1440]{3,4,2,1,0:T(8,128)(2,1)} %param.13) | copy-start | bytes 8847364
  23.2 1.0 copy-start.2
  24.2 14.3 %copy-start.3 = (bf16[1456,128]{1,0:T(8,128)(2,1)S(1)}, bf16[1456,128]{1,0:T(8,128)(2,1)}, u32[]{:S(2)}) copy-start(bf16[1456,128]{1,0:T(8,128)(2,1)} %get-tuple-element.89.refs_0_) | copy-start | bytes 1118212
  24.8 13.8 %collective-permute-start.7 = (bf16[3,1456,128]{2,1,0:T(8,128)(2,1)S(1)}, bf16[3,1456,128]{2,1,0:T(8,128)(2,1)S(1)}, u32[]{:S(2)}, u32[]{:S(2)}) collective-permute-start(bf16[3,1456,128]{2,1,0:T(8,128)(2,1)S(1)} %collect.1), channel_id=1, source_target_pairs={{0,1},{1,0},{2,3},{3,2},{4,5},{5,4},{6,7},{7,6},{8,9},{9,8},{10,11... | collective-permute-start | bytes 3354632 | tf_op jit(solution)/shard_map/ppermute | solution.py:495
  24.8 12.0 %collective-permute-start.6 = (bf16[1456,128]{1,0:T(8,128)(2,1)S(1)}, bf16[1456,128]{1,0:T(8,128)(2,1)S(1)}, u32[]{:S(2)}, u32[]{:S(2)}) collective-permute-start(bf16[1456,128]{1,0:T(8,128)(2,1)S(1)} %copy-done.2), channel_id=1, source_target_pairs={{0,6},{1,7},{2,4},{3,5},{4,2},{5,3},{6,0},{7,1},{8,14},{9,15},{10,... | collective-permute-start | bytes 1118216 | tf_op jit(solution)/shard_map/ppermute | solution.py:490
  27.3 17.8 %collective-permute-start.5 = (bf16[1200,256]{1,0:T(8,128)(2,1)S(1)}, bf16[1200,256]{1,0:T(8,128)(2,1)S(1)}, u32[]{:S(2)}, u32[]{:S(2)}) collective-permute-start(bf16[1200,256]{1,0:T(8,128)(2,1)S(1)} %collective-permute-done.2.refs_0_), channel_id=1, source_target_pairs={{8,16},{16,8},{9,17},{17,9},{10,18},{18,10},{11,19},{19,11},{12,20... | collective-permute-start | bytes 1843208 | tf_op jit(solution)/shard_map/ppermute | solution.py:377
  28.0 18.6 %collective-permute-start.4 = (bf16[1200,256]{1,0:T(8,128)(2,1)S(1)}, bf16[1200,256]{1,0:T(8,128)(2,1)S(1)}, u32[]{:S(2)}, u32[]{:S(2)}) collective-permute-start(bf16[1200,256]{1,0:T(8,128)(2,1)S(1)} %collective-permute-done.3.refs_0_.refs_1_), channel_id=1, source_target_pairs={{16,24},{8,0},{17,25},{9,1},{18,26},{10,2},{19,27},{11,3},{20,28},... | collective-permute-start | bytes 1843208 | tf_op jit(solution)/shard_map/ppermute | solution.py:377
  29.3 25.2 %collective-permute-start.9 = (bf16[1152,256]{1,0:T(8,128)(2,1)S(1)}, bf16[1152,256]{1,0:T(8,128)(2,1)S(1)}, u32[]{:S(2)}, u32[]{:S(2)}) collective-permute-start(bf16[1152,256]{1,0:T(8,128)(2,1)S(1)} %pack_left.1.own_ref), channel_id=1, source_target_pairs={{0,8},{24,16},{1,9},{25,17},{2,10},{26,18},{3,11},{27,19},{4,12},{... | collective-permute-start | bytes 1769480 | tf_op jit(solution)/shard_map/ppermute | solution.py:500
  36.8 1.7 %collective-permute-start.8 = (bf16[1456,128]{1,0:T(8,128)(2,1)S(1)}, bf16[1456,128]{1,0:T(8,128)(2,1)S(1)}, u32[]{:S(2)}, u32[]{:S(2)}) collective-permute-start(bf16[1456,128]{1,0:T(8,128)(2,1)S(1)} %collective-permute-done.6.refs_3_), channel_id=1, source_target_pairs={{0,1},{1,0},{2,3},{3,2},{4,5},{5,4},{6,7},{7,6},{8,9},{9,8},{10,11... | collective-permute-start | bytes 1118216 | tf_op jit(solution)/shard_map/ppermute | solution.py:495
  46.6 18.7 %collective-permute-start.11 = (bf16[1200,256]{1,0:T(8,128)(2,1)S(1)}, bf16[1200,256]{1,0:T(8,128)(2,1)S(1)}, u32[]{:S(2)}, u32[]{:S(2)}) collective-permute-start(bf16[1200,256]{1,0:T(8,128)(2,1)S(1)} %collective-permute-done.5.refs_1_), channel_id=1, source_target_pairs={{16,24},{8,0},{17,25},{9,1},{18,26},{10,2},{19,27},{11,3},{20,28},... | collective-permute-start | bytes 1843208 | tf_op jit(solution)/shard_map/ppermute | solution.py:377
  48.6 14.3 %collective-permute-start.10 = (bf16[1024,256]{1,0:T(8,128)(2,1)S(1)}, bf16[1024,256]{1,0:T(8,128)(2,1)S(1)}, u32[]{:S(2)}, u32[]{:S(2)}) collective-permute-start(bf16[1024,256]{1,0:T(8,128)(2,1)S(1)} %product.10), channel_id=1, source_target_pairs={{0,8},{24,16},{1,9},{25,17},{2,10},{26,18},{3,11},{27,19},{4,12},{... | collective-permute-start | bytes 1572872 | tf_op jit(solution)/shard_map/ppermute | solution.py:523
  52.5 16.3 %collective-permute-start.13 = (bf16[1152,256]{1,0:T(8,128)(2,1)S(1)}, bf16[1152,256]{1,0:T(8,128)(2,1)S(1)}, u32[]{:S(2)}, u32[]{:S(2)}) collective-permute-start(bf16[1152,256]{1,0:T(8,128)(2,1)S(1)} %pack_left.1.own_ref), channel_id=1, source_target_pairs={{8,16},{16,8},{9,17},{17,9},{10,18},{18,10},{11,19},{19,11},{12,20... | collective-permute-start | bytes 1769480 | tf_op jit(solution)/shard_map/ppermute | solution.py:509
  53.3 23.0 %collective-permute-start.12 = (bf16[1152,256]{1,0:T(8,128)(2,1)S(1)}, bf16[1152,256]{1,0:T(8,128)(2,1)S(1)}, u32[]{:S(2)}, u32[]{:S(2)}) collective-permute-start(bf16[1152,256]{1,0:T(8,128)(2,1)S(1)} %pack_left.1.own_ref), channel_id=1, source_target_pairs={{16,24},{8,0},{17,25},{9,1},{18,26},{10,2},{19,27},{11,3},{20,28},... | collective-permute-start | bytes 1769480 | tf_op jit(solution)/shard_map/ppermute | solution.py:509
  54.6 28.4 %collective-permute-start.15 = (bf16[1152,256]{1,0:T(8,128)(2,1)S(1)}, bf16[1152,256]{1,0:T(8,128)(2,1)S(1)}, u32[]{:S(2)}, u32[]{:S(2)}) collective-permute-start(bf16[1152,256]{1,0:T(8,128)(2,1)S(1)} %collective-permute-done.9.ends_ref), channel_id=1, source_target_pairs={{8,16},{16,8},{9,17},{17,9},{10,18},{18,10},{11,19},{19,11},{12,20... | collective-permute-start | bytes 1769480 | tf_op jit(solution)/shard_map/ppermute | solution.py:509
  66.0 16.9 %collective-permute-start.14 = (bf16[1072,256]{1,0:T(8,128)(2,1)S(1)}, bf16[1072,256]{1,0:T(8,128)(2,1)S(1)}, u32[]{:S(2)}, u32[]{:S(2)}) collective-permute-start(bf16[1072,256]{1,0:T(8,128)(2,1)S(1)} %product.13), channel_id=1, source_target_pairs={{0,8},{24,16},{1,9},{25,17},{2,10},{26,18},{3,11},{27,19},{4,12},{... | collective-permute-start | bytes 1646600 | tf_op jit(solution)/shard_map/ppermute | solution.py:523
  67.4 18.3 %collective-permute-start.16 = (bf16[1024,256]{1,0:T(8,128)(2,1)S(1)}, bf16[1024,256]{1,0:T(8,128)(2,1)S(1)}, u32[]{:S(2)}, u32[]{:S(2)}) collective-permute-start(bf16[1024,256]{1,0:T(8,128)(2,1)S(1)} %add.6), channel_id=1, source_target_pairs={{8,16},{16,8},{9,17},{17,9},{10,18},{18,10},{11,19},{19,11},{12,20... | collective-permute-start | bytes 1572872 | tf_op jit(solution)/shard_map/ppermute | solution.py:523
  76.2 19.7 %collective-permute-start.18 = (bf16[1152,256]{1,0:T(8,128)(2,1)S(1)}, bf16[1152,256]{1,0:T(8,128)(2,1)S(1)}, u32[]{:S(2)}, u32[]{:S(2)}) collective-permute-start(bf16[1152,256]{1,0:T(8,128)(2,1)S(1)} %collective-permute-done.13.odd_ref), channel_id=1, source_target_pairs={{16,24},{8,0},{17,25},{9,1},{18,26},{10,2},{19,27},{11,3},{20,28},... | collective-permute-start | bytes 1769480 | tf_op jit(solution)/shard_map/ppermute | solution.py:509
  77.5 18.4 %collective-permute-start.17 = (bf16[1024,256]{1,0:T(8,128)(2,1)S(1)}, bf16[1024,256]{1,0:T(8,128)(2,1)S(1)}, u32[]{:S(2)}, u32[]{:S(2)}) collective-permute-start(bf16[1024,256]{1,0:T(8,128)(2,1)S(1)} %product.12), channel_id=1, source_target_pairs={{0,8},{24,16},{1,9},{25,17},{2,10},{26,18},{3,11},{27,19},{4,12},{... | collective-permute-start | bytes 1572872 | tf_op jit(solution)/shard_map/ppermute | solution.py:523
  82.9 21.5 %collective-permute-start.20 = (bf16[1152,256]{1,0:T(8,128)(2,1)S(1)}, bf16[1152,256]{1,0:T(8,128)(2,1)S(1)}, u32[]{:S(2)}, u32[]{:S(2)}) collective-permute-start(bf16[1152,256]{1,0:T(8,128)(2,1)S(1)} %collective-permute-done.15.refs_1_), channel_id=1, source_target_pairs={{16,24},{8,0},{17,25},{9,1},{18,26},{10,2},{19,27},{11,3},{20,28},... | collective-permute-start | bytes 1769480 | tf_op jit(solution)/shard_map/ppermute | solution.py:509
  84.3 13.3 %collective-permute-start.19 = (bf16[1072,256]{1,0:T(8,128)(2,1)S(1)}, bf16[1072,256]{1,0:T(8,128)(2,1)S(1)}, u32[]{:S(2)}, u32[]{:S(2)}) collective-permute-start(bf16[1072,256]{1,0:T(8,128)(2,1)S(1)} %add.7), channel_id=1, source_target_pairs={{8,16},{16,8},{9,17},{17,9},{10,18},{18,10},{11,19},{19,11},{12,20... | collective-permute-start | bytes 1646600 | tf_op jit(solution)/shard_map/ppermute | solution.py:523
  85.7 22.9 %collective-permute-start.21 = (bf16[1072,256]{1,0:T(8,128)(2,1)S(1)}, bf16[1072,256]{1,0:T(8,128)(2,1)S(1)}, u32[]{:S(2)}, u32[]{:S(2)}) collective-permute-start(bf16[1072,256]{1,0:T(8,128)(2,1)S(1)} %get-tuple-element.132), channel_id=1, source_target_pairs={{0,8},{24,16},{1,9},{25,17},{2,10},{26,18},{3,11},{27,19},{4,12},{... | collective-permute-start | bytes 1646600 | tf_op jit(solution)/shard_map/ppermute | solution.py:523
  95.9 13.4 %collective-permute-start.22 = (bf16[1024,256]{1,0:T(8,128)(2,1)S(1)}, bf16[1024,256]{1,0:T(8,128)(2,1)S(1)}, u32[]{:S(2)}, u32[]{:S(2)}) collective-permute-start(bf16[1024,256]{1,0:T(8,128)(2,1)S(1)} %add.8), channel_id=1, source_target_pairs={{8,16},{16,8},{9,17},{17,9},{10,18},{18,10},{11,19},{19,11},{12,20... | collective-permute-start | bytes 1572872 | tf_op jit(solution)/shard_map/ppermute | solution.py:523
  104.5 6.1 %copy-start.1 = (bf16[1200,256]{1,0:T(8,128)(2,1)S(1)}, bf16[1200,256]{1,0:T(8,128)(2,1)}, u32[]{:S(2)}) copy-start(bf16[1200,256]{1,0:T(8,128)(2,1)} %get-tuple-element.96.refs_0_) | copy-start | bytes 1843204
  104.5 22.3 %collective-permute-start.24 = (bf16[1072,256]{1,0:T(8,128)(2,1)S(1)}, bf16[1072,256]{1,0:T(8,128)(2,1)S(1)}, u32[]{:S(2)}, u32[]{:S(2)}) collective-permute-start(bf16[1072,256]{1,0:T(8,128)(2,1)S(1)} %add.9), channel_id=1, source_target_pairs={{0,8},{8,0},{16,24},{24,16},{1,9},{9,1},{17,25},{25,17},{2,10},{10... | collective-permute-start | bytes 1646600 | tf_op jit(solution)/shard_map/ppermute | solution.py:523
  105.9 20.9 %collective-permute-start.23 = (bf16[1024,256]{1,0:T(8,128)(2,1)S(1)}, bf16[1024,256]{1,0:T(8,128)(2,1)S(1)}, u32[]{:S(2)}, u32[]{:S(2)}) collective-permute-start(bf16[1024,256]{1,0:T(8,128)(2,1)S(1)} %get-tuple-element.141), channel_id=1, source_target_pairs={{0,8},{24,16},{1,9},{25,17},{2,10},{26,18},{3,11},{27,19},{4,12},{... | collective-permute-start | bytes 1572872 | tf_op jit(solution)/shard_map/ppermute | solution.py:523
  108.6 19.1 %collective-permute-start.26 = (bf16[1072,256]{1,0:T(8,128)(2,1)S(1)}, bf16[1072,256]{1,0:T(8,128)(2,1)S(1)}, u32[]{:S(2)}, u32[]{:S(2)}) collective-permute-start(bf16[1072,256]{1,0:T(8,128)(2,1)S(1)} %add.11), channel_id=1, source_target_pairs={{8,16},{16,8},{9,17},{17,9},{10,18},{18,10},{11,19},{19,11},{12,20... | collective-permute-start | bytes 1646600 | tf_op jit(solution)/shard_map/ppermute | solution.py:523
  109.3 18.4 %collective-permute-start.25 = (bf16[1024,256]{1,0:T(8,128)(2,1)S(1)}, bf16[1024,256]{1,0:T(8,128)(2,1)S(1)}, u32[]{:S(2)}, u32[]{:S(2)}) collective-permute-start(bf16[1024,256]{1,0:T(8,128)(2,1)S(1)} %add.10), channel_id=1, source_target_pairs={{8,0},{16,24},{9,1},{17,25},{10,2},{18,26},{11,3},{19,27},{12,4},{... | collective-permute-start | bytes 1572872 | tf_op jit(solution)/shard_map/ppermute | solution.py:523
  112.1 14.7 %copy-start.6 = (s32[128,4]{0,1:T(4,128)S(1)}, s32[128,4]{0,1:T(4,128)}, u32[]{:S(2)}) copy-start(s32[128,4]{0,1:T(4,128)} %param.12) | copy-start | bytes 6148
